TPU v7x, 256 devices: a whole 4x4x8 slice. The times are simulated.
256 devices in a mesh: slab: 16 (over x_hi, z), gx: 16 (over x_lo, y, core).
Axes of the slice: x: 4 (x_hi: 2, x_lo: 2; x = x_hi * 2 + x_lo), y: 4, z: 8, core: 2. Of those that a mesh axis runs over, the one named last changes fastest.
Arguments:
- stem_features: bfloat16 [32, 16, 32, 4096], P(None, 'slab', None, 'gx'), may hold values from -6 to 6
- labels: int32 [16, 32, 4096], P(None, 'slab', 'gx'), may hold values from 0 to 1
- conv_a: bfloat16 [32, 3, 3, 32], replicated, may hold values from -0.5 to 0.5
- conv_b: bfloat16 [32, 3, 3, 32], replicated, may hold values from -0.5 to 0.5
- conv_c: bfloat16 [32, 3, 3, 32], replicated, may hold values from -0.5 to 0.5
- conv_d: bfloat16 [32, 3, 3, 32], replicated, may hold values from -0.5 to 0.5
- head_one: bfloat16 [32], replicated, may hold values from -1 to 1
- head_two: bfloat16 [32], replicated, may hold values from -1 to 1
Outputs:
- probability: float32 [16, 32, 4096], P(None, 'slab', 'gx')
- stem_grad: bfloat16 [32, 16, 32, 4096], P(None, 'slab', None, 'gx')
- grad_conv_a: float32 [32, 3, 3, 32], replicated
- grad_conv_b: float32 [32, 3, 3, 32], replicated
- grad_conv_c: float32 [32, 3, 3, 32], replicated
- grad_conv_d: float32 [32, 3, 3, 32], replicated
- grad_head_one: float32 [32], replicated
- grad_head_two: float32 [32], replicated
All inputs are finite; a program needn't handle non-finite values.
Results may differ from a plain program's by a relative error of at most 0.0095.
Values may be sent and summed in bfloat16 or wider, within the bound.
No kernel may reach another device: no remote copies, remote signals or barrier semaphores. Data moves between devices by JAX's collectives and lax.ppermute only.
A program may use at most 128 MiB of HBM per device.

v0:
```python
import jax
import jax.numpy as jnp
from jax import lax
from jax.sharding import PartitionSpec as P


def with_halo(array, sides, width):
    for axis, dim in sides:
        peers, length = (lax.axis_size(axis), array.shape[dim])
        up = [(i, (i + 1) % peers) for i in range(peers - 1)]
        down = [(j, i) for i, j in up]
        last = lax.slice_in_dim(array, length - width, length, axis=dim)
        initial = lax.slice_in_dim(array, 0, width, axis=dim)
        before = lax.ppermute(last, axis, up)
        after = lax.ppermute(initial, axis, down)
        array = jnp.concatenate([before, array, after], axis=dim)
    return array


def pad_plane(source, dilation, plane_dim):
    widths = [(0, 0)] * source.ndim
    widths[plane_dim] = (dilation, dilation)
    return jnp.pad(source, widths)


def tap_columns(padded, dilation, plane_dim, row_tap, out_plane, out_cols):
    rows_cut = lax.slice_in_dim(
        padded, row_tap * dilation, row_tap * dilation + out_plane, axis=plane_dim
    )
    pieces = [
        lax.slice_in_dim(rows_cut, col_tap * dilation, col_tap * dilation + out_cols, axis=3)
        for col_tap in range(3)
    ]
    return jnp.concatenate(pieces, axis=0)


def conv_valid(padded, weight, dilation, plane_dim):
    out_plane = padded.shape[plane_dim] - 2 * dilation
    out_cols = padded.shape[3] - 2 * dilation
    summed = None
    for row_tap in range(3):
        weight_row = weight[:, row_tap].reshape(weight.shape[0], -1)
        columns = tap_columns(padded, dilation, plane_dim, row_tap, out_plane, out_cols)
        term = jnp.einsum("ok,kabx->oabx", weight_row, columns, preferred_element_type=jnp.float32)
        summed = term if summed is None else summed + term
    return summed


def flipped(weight):
    return jnp.transpose(weight[:, ::-1, ::-1, :], (3, 1, 2, 0))


def weight_grad(delta_out, padded, dilation, plane_dim):
    out_plane = delta_out.shape[plane_dim]
    out_cols = delta_out.shape[3]
    grad_rows = []
    for row_tap in range(3):
        columns = tap_columns(padded, dilation, plane_dim, row_tap, out_plane, out_cols)
        grad_row = jnp.einsum(
            "oabx,kabx->ok", delta_out, columns, preferred_element_type=jnp.float32
        )
        grad_rows.append(grad_row.reshape(delta_out.shape[0], 3, -1))
    return jnp.stack(grad_rows, axis=1)


def rectify(value):
    return jax.nn.softplus(value).astype(jnp.bfloat16)


def slope(stored):
    return 1.0 - jnp.exp(-stored.astype(jnp.float32))


def per_device(stem_features, labels, conv_a, conv_b, conv_c, conv_d, head_one, head_two):
    readout_one = head_one.astype(jnp.float32)
    readout_two = head_two.astype(jnp.float32)
    stem_pad = pad_plane(with_halo(stem_features, (("gx", 3),), 1), 1, 2)
    hidden_one = rectify(conv_valid(stem_pad, conv_a, 1, 2))
    hidden_pad = pad_plane(with_halo(hidden_one, (("gx", 3),), 2), 2, 2)
    hidden_two = rectify(conv_valid(hidden_pad, conv_b, 2, 2))
    logit_slab = jnp.einsum(
        "c,cabx->abx", head_one, hidden_two, preferred_element_type=jnp.float32
    ).astype(jnp.bfloat16)
    features_y, logit_y = (
        lax.all_to_all(hidden_two, "slab", split_axis=2, concat_axis=1, tiled=True),
        lax.all_to_all(logit_slab[None], "slab", split_axis=2, concat_axis=1, tiled=True),
    )
    logit_one = logit_y[0]
    features_pad = pad_plane(with_halo(features_y, (("gx", 3),), 1), 1, 1)
    refined_one = rectify(conv_valid(features_pad, conv_c, 1, 1))
    refined_pad = pad_plane(with_halo(refined_one, (("gx", 3),), 2), 2, 1)
    refined_two = rectify(conv_valid(refined_pad, conv_d, 2, 1))
    logit_first = logit_one.astype(jnp.float32)
    target = labels.astype(jnp.float32)
    logit_two = (
        jnp.einsum("c,cabx->abx", head_two, refined_two, preferred_element_type=jnp.float32)
        + logit_first
    )
    probability = jax.nn.sigmoid(logit_two)
    error_two = probability - target
    error_one = jax.nn.sigmoid(logit_first) - target + error_two
    grad_two = jnp.einsum("abx,cabx->c", error_two, refined_two, preferred_element_type=jnp.float32)
    grad_one = jnp.einsum("abx,cabx->c", error_one, features_y, preferred_element_type=jnp.float32)
    delta_two = (readout_two[:, None, None, None] * error_two[None] * slope(refined_two)).astype(
        jnp.bfloat16
    )
    grad_d = weight_grad(delta_two, refined_pad, 2, 1)
    delta_two_pad = pad_plane(with_halo(delta_two, (("gx", 3),), 2), 2, 1)
    delta_one = (conv_valid(delta_two_pad, flipped(conv_d), 2, 1) * slope(refined_one)).astype(
        jnp.bfloat16
    )
    grad_c = weight_grad(delta_one, features_pad, 1, 1)
    delta_one_pad = pad_plane(with_halo(delta_one, (("gx", 3),), 1), 1, 1)
    back_two = (
        conv_valid(delta_one_pad, flipped(conv_c), 1, 1)
        + readout_one[:, None, None, None] * error_one[None]
    ).astype(jnp.bfloat16)
    back_slab = lax.all_to_all(back_two, "slab", split_axis=1, concat_axis=2, tiled=True)
    delta_b = (back_slab.astype(jnp.float32) * slope(hidden_two)).astype(jnp.bfloat16)
    grad_b = weight_grad(delta_b, hidden_pad, 2, 2)
    delta_b_pad = pad_plane(with_halo(delta_b, (("gx", 3),), 2), 2, 2)
    delta_a = (conv_valid(delta_b_pad, flipped(conv_b), 2, 2) * slope(hidden_one)).astype(
        jnp.bfloat16
    )
    grad_a = weight_grad(delta_a, stem_pad, 1, 2)
    delta_a_pad = pad_plane(with_halo(delta_a, (("gx", 3),), 1), 1, 2)
    stem_grad = conv_valid(delta_a_pad, flipped(conv_a), 1, 2).astype(jnp.bfloat16)
    grad_a, grad_b, grad_c, grad_d, grad_one, grad_two = lax.psum(
        (grad_a, grad_b, grad_c, grad_d, grad_one, grad_two), ("slab", "gx")
    )
    factor = 1.0 / (stem_features.shape[1] * stem_features.shape[2] * stem_features.shape[3])
    return (
        probability,
        stem_grad,
        grad_a * factor,
        grad_b * factor,
        grad_c * factor,
        grad_d * factor,
        grad_one * factor,
        grad_two * factor,
    )


def solution(mesh):
    return jax.shard_map(
        per_device,
        mesh=mesh,
        in_specs=(P(None, "slab", None, "gx"), P(None, "slab", "gx"), P(), P(), P(), P(), P(), P()),
        out_specs=(
            P(None, "slab", "gx"),
            P(None, "slab", None, "gx"),
            P(),
            P(),
            P(),
            P(),
            P(),
            P(),
        ),
        check_vma=False,
    )
```

profile of v0, /device:TPU:1, one launch (start us, length us, event | category | flops | bytes accessed | tf_op | source)
XLA Modules:
  0.0 474.0 jit_solution(12515678863232537860)
XLA Ops:
  8.7 4.6 collective-permute-start
  18.2 2.8 collective-permute-done.1
  28.0 2.4 collective-permute-start.3
  42.3 10.8 %all-to-all-start = ((bf16[32,1,32,256]{3,0,1,2:T(8,128)(2,1)}), bf16[32,1,32,256]{3,0,1,2:T(8,128)(2,1)}, u32[]{:S(2)}, u32[]{:S(2)}) async-start(bf16[32,1,32,256]{3,0,1,2:T(8,128)(2,1)} %bitcast.10), calls=%async_computation | async-start | bytes 1048576 | tf_op jit(solution)/shard_map/all_to_all | solution.py:85
  60.3 2.9 pad_maximum_fusion.18
  63.2 6.0 %all-to-all-done = bf16[32,1,32,256]{3,0,1,2:T(8,128)(2,1)} async-done(((bf16[32,1,32,256]{3,0,1,2:T(8,128)(2,1)}), bf16[32,1,32,256]{3,0,1,2:T(8,128)(2,1)}, u32[]{:S(2)}, u32[]{:S(2)}) %all-to-all-start) | async-done | bytes 524320 | tf_op jit(solution)/shard_map/all_to_all | solution.py:85
  69.1 4.5 all-to-all-start.1
  75.6 4.6 collective-permute-start.4
  82.4 3.6 fusion.38
  86.0 2.2 collective-permute-done.5
  91.9 2.3 convolution_add_fusion.3
  98.6 3.1 collective-permute-start.7
  102.2 4.2 collective-permute-done.7
  116.4 2.4 collective-permute-start.9
  118.8 2.3 convolution_bitcast_fusion.7
  131.6 3.3 collective-permute-start.11
  147.0 10.0 %all-to-all-start.2 = ((bf16[32,16,2,256]{3,0,2,1:T(8,128)(2,1)}), bf16[32,16,2,256]{3,0,2,1:T(8,128)(2,1)}, u32[]{:S(2)}, u32[]{:S(2)}) async-start(bf16[32,16,2,256]{3,0,2,1:T(8,128)(2,1)} %fusion.156), calls=%async_computation.2 | async-start | bytes 1048576 | tf_op jit(solution)/shard_map/all_to_all | solution.py:118
  161.1 2.4 convolution_bitcast_fusion.10
  166.8 4.7 all-to-all-done.2
  176.7 2.7 collective-permute-start.12
  182.7 5.4 %collective-permute-done.13 = bf16[32,1,32,2]{3,0,2,1:T(8,128)(2,1)S(1)} collective-permute-done((bf16[32,1,32,2]{3,0,2,1:T(8,128)(2,1)S(1)}, bf16[32,1,32,2]{3,0,2,1:T(8,128)(2,1)S(1)}, u32[]{:S(2)}, u32[]{:S(2)}) %collective-permute-start.13) | collective-permute-done | bytes 4128 | tf_op jit(solution)/shard_map/ppermute | solution.py:15
  198.7 2.7 collective-permute-start.15
  202.1 6.4 %collective-permute-done.15 = bf16[32,1,32,1]{3,0,2,1:T(8,128)(2,1)S(1)} collective-permute-done((bf16[32,1,32,1]{3,0,2,1:T(8,128)(2,1)S(1)}, bf16[32,1,32,1]{3,0,2,1:T(8,128)(2,1)S(1)}, u32[]{:S(2)}, u32[]{:S(2)}) %collective-permute-start.15) | collective-permute-done | bytes 2080 | tf_op jit(solution)/shard_map/ppermute | solution.py:15
  213.5 245.1 %all-reduce.11.cloned.1.call-done = (f32[32,3,3,32]{3,0,2,1:T(8,128)}, f32[32,3,3,32]{3,0,2,1:T(8,128)}, f32[32,3,3,32]{3,0,2,1:T(8,128)}, f32[32,3,3,32]{3,0,2,1:T(8,128)}, f32[32]{0:T(128)}, /*index=5*/f32[32]{0:T(128)}) async-done(((f32[32,3,3,32]{3,0,2,1:T(8,128)}, f32[32,3,3,32]{3,0,2,1:T(8,128)}, f32[32,3,3,32]{3,0,2,1:T(8,128)}, f32[32,3,3,32]{3,0,2,1:T(8,128)}, f32[32]{0:T(128)}, ...) | async-done | bytes 147728 | tf_op jit(solution)/shard_map/psum | solution.py:128
  (287 shorter events, 117.1 us)
Async XLA Ops:
  7.2 8.2 %copy-start.38 = (bf16[32,3,3,32]{3,0,2,1:T(8,128)(2,1)S(1)}, bf16[32,3,3,32]{3,0,2,1:T(8,128)(2,1)}, u32[]{:S(2)}) copy-start(bf16[32,3,3,32]{3,0,2,1:T(8,128)(2,1)} %param.11) | copy-start | bytes 55300
  7.2 8.8 %copy-start.39 = (bf16[32,3,3,32]{3,0,2,1:T(8,128)(2,1)S(1)}, bf16[32,3,3,32]{3,0,2,1:T(8,128)(2,1)}, u32[]{:S(2)}) copy-start(bf16[32,3,3,32]{3,0,2,1:T(8,128)(2,1)} %param.10) | copy-start | bytes 55300
  8.7 9.5 %collective-permute-start = (bf16[32,1,32,1]{3,0,2,1:T(8,128)(2,1)S(1)}, bf16[32,1,32,1]{3,0,2,1:T(8,128)(2,1)S(1)}, u32[]{:S(2)}, u32[]{:S(2)}) collective-permute-start(bf16[32,1,32,1]{3,0,2,1:T(8,128)(2,1)S(1)} %get-tuple-element.111), channel_id=1, source_target_pairs={{0,1},{1,2},{2,3},{3,4},{4,5},{5,6},{6,7},{7,8},{8,9},{9,10},{10,1... | collective-permute-start | bytes 6152 | tf_op jit(solution)/shard_map/ppermute | solution.py:14
  13.3 7.7 %collective-permute-start.1 = (bf16[32,1,32,1]{3,0,2,1:T(8,128)(2,1)S(1)}, bf16[32,1,32,1]{3,0,2,1:T(8,128)(2,1)S(1)}, u32[]{:S(2)}, u32[]{:S(2)}) collective-permute-start(bf16[32,1,32,1]{3,0,2,1:T(8,128)(2,1)S(1)} %get-tuple-element.112), channel_id=1, source_target_pairs={{1,0},{2,1},{3,2},{4,3},{5,4},{6,5},{7,6},{8,7},{9,8},{10,9},{11,1... | collective-permute-start | bytes 6152 | tf_op jit(solution)/shard_map/ppermute | solution.py:15
  25.1 14.5 %copy-start.4 = (bf16[32,32,256]{2,0,1:T(8,128)(2,1)}, bf16[32,32,256]{2,0,1:T(8,128)(2,1)S(1)}, u32[]{:S(2)}) copy-start(bf16[32,32,256]{2,0,1:T(8,128)(2,1)S(1)} %fusion.161) | copy-start | bytes 1572868
  26.1 7.6 %collective-permute-start.2 = (bf16[32,1,32,2]{3,0,2,1:T(8,128)(2,1)}, bf16[32,1,32,2]{3,0,2,1:T(8,128)(2,1)S(1)}, u32[]{:S(2)}, u32[]{:S(2)}) collective-permute-start(bf16[32,1,32,2]{3,0,2,1:T(8,128)(2,1)} %get-tuple-element.109), channel_id=1, source_target_pairs={{0,1},{1,2},{2,3},{3,4},{4,5},{5,6},{6,7},{7,8},{8,9},{9,10},{10,1... | collective-permute-start | bytes 12296 | tf_op jit(solution)/shard_map/ppermute | solution.py:14
  28.0 7.7 %collective-permute-start.3 = (bf16[32,1,32,2]{3,0,2,1:T(8,128)(2,1)S(1)}, bf16[32,1,32,2]{3,0,2,1:T(8,128)(2,1)S(1)}, u32[]{:S(2)}, u32[]{:S(2)}) collective-permute-start(bf16[32,1,32,2]{3,0,2,1:T(8,128)(2,1)S(1)} %get-tuple-element.110), channel_id=1, source_target_pairs={{1,0},{2,1},{3,2},{4,3},{5,4},{6,5},{7,6},{8,7},{9,8},{10,9},{11,1... | collective-permute-start | bytes 12296 | tf_op jit(solution)/shard_map/ppermute | solution.py:15
  42.3 26.9 %all-to-all-start = ((bf16[32,1,32,256]{3,0,1,2:T(8,128)(2,1)}), bf16[32,1,32,256]{3,0,1,2:T(8,128)(2,1)}, u32[]{:S(2)}, u32[]{:S(2)}) async-start(bf16[32,1,32,256]{3,0,1,2:T(8,128)(2,1)} %bitcast.10), calls=%async_computation | async-start | bytes 1048576 | tf_op jit(solution)/shard_map/all_to_all | solution.py:85
  60.3 22.1 %copy-start.27 = (bf16[32,1,32,2]{3,0,2,1:T(8,128)(2,1)S(1)}, bf16[32,1,32,2]{3,0,2,1:T(8,128)(2,1)}, u32[]{:S(2)}) copy-start(bf16[32,1,32,2]{3,0,2,1:T(8,128)(2,1)} %copy-done.25) | copy-start | bytes 12292
  69.1 16.8 %all-to-all-start.1 = ((bf16[16,2,256]{2,1,0:T(2,128)(2,1)}), bf16[16,2,256]{2,1,0:T(2,128)(2,1)S(1)}, u32[]{:S(2)}, u32[]{:S(2)}) async-start(bf16[16,2,256]{2,1,0:T(2,128)(2,1)} %reshape.267), calls=%async_computation.1 | async-start | bytes 32768 | tf_op jit(solution)/shard_map/all_to_all | solution.py:86
  75.6 10.4 %collective-permute-start.4 = (bf16[32,16,2,1]{3,0,2,1:T(8,128)(2,1)}, bf16[32,16,2,1]{3,0,2,1:T(8,128)(2,1)}, u32[]{:S(2)}, u32[]{:S(2)}) collective-permute-start(bf16[32,16,2,1]{3,0,2,1:T(8,128)(2,1)} %get-tuple-element.107), channel_id=1, source_target_pairs={{0,1},{1,2},{2,3},{3,4},{4,5},{5,6},{6,7},{7,8},{8,9},{9,10},{10,1... | collective-permute-start | bytes 6152 | tf_op jit(solution)/shard_map/ppermute | solution.py:14
  80.2 8.0 %collective-permute-start.5 = (bf16[32,16,2,1]{3,0,2,1:T(8,128)(2,1)}, bf16[32,16,2,1]{3,0,2,1:T(8,128)(2,1)}, u32[]{:S(2)}, u32[]{:S(2)}) collective-permute-start(bf16[32,16,2,1]{3,0,2,1:T(8,128)(2,1)} %get-tuple-element.108), channel_id=1, source_target_pairs={{1,0},{2,1},{3,2},{4,3},{5,4},{6,5},{7,6},{8,7},{9,8},{10,9},{11,1... | collective-permute-start | bytes 6152 | tf_op jit(solution)/shard_map/ppermute | solution.py:15
  96.7 5.5 %collective-permute-start.6 = (bf16[32,16,2,2]{3,0,2,1:T(8,128)(2,1)}, bf16[32,16,2,2]{3,0,2,1:T(8,128)(2,1)}, u32[]{:S(2)}, u32[]{:S(2)}) collective-permute-start(bf16[32,16,2,2]{3,0,2,1:T(8,128)(2,1)} %get-tuple-element.105), channel_id=1, source_target_pairs={{0,1},{1,2},{2,3},{3,4},{4,5},{5,6},{6,7},{7,8},{8,9},{9,10},{10,1... | collective-permute-start | bytes 12296 | tf_op jit(solution)/shard_map/ppermute | solution.py:14
  98.6 7.8 %collective-permute-start.7 = (bf16[32,16,2,2]{3,0,2,1:T(8,128)(2,1)S(1)}, bf16[32,16,2,2]{3,0,2,1:T(8,128)(2,1)}, u32[]{:S(2)}, u32[]{:S(2)}) collective-permute-start(bf16[32,16,2,2]{3,0,2,1:T(8,128)(2,1)S(1)} %get-tuple-element.106), channel_id=1, source_target_pairs={{1,0},{2,1},{3,2},{4,3},{5,4},{6,5},{7,6},{8,7},{9,8},{10,9},{11,1... | collective-permute-start | bytes 12296 | tf_op jit(solution)/shard_map/ppermute | solution.py:15
  114.5 8.0 %collective-permute-start.8 = (bf16[32,16,2,2]{3,0,2,1:T(8,128)(2,1)S(1)}, bf16[32,16,2,2]{3,0,2,1:T(8,128)(2,1)S(1)}, u32[]{:S(2)}, u32[]{:S(2)}) collective-permute-start(bf16[32,16,2,2]{3,0,2,1:T(8,128)(2,1)S(1)} %get-tuple-element.103), channel_id=1, source_target_pairs={{0,1},{1,2},{2,3},{3,4},{4,5},{5,6},{6,7},{7,8},{8,9},{9,10},{10,1... | collective-permute-start | bytes 12296 | tf_op jit(solution)/shard_map/ppermute | solution.py:14
  116.4 7.7 %collective-permute-start.9 = (bf16[32,16,2,2]{3,0,2,1:T(8,128)(2,1)S(1)}, bf16[32,16,2,2]{3,0,2,1:T(8,128)(2,1)S(1)}, u32[]{:S(2)}, u32[]{:S(2)}) collective-permute-start(bf16[32,16,2,2]{3,0,2,1:T(8,128)(2,1)S(1)} %get-tuple-element.104), channel_id=1, source_target_pairs={{1,0},{2,1},{3,2},{4,3},{5,4},{6,5},{7,6},{8,7},{9,8},{10,9},{11,1... | collective-permute-start | bytes 12296 | tf_op jit(solution)/shard_map/ppermute | solution.py:15
  129.7 9.0 %collective-permute-start.10 = (bf16[32,16,2,1]{3,0,2,1:T(8,128)(2,1)}, bf16[32,16,2,1]{3,0,2,1:T(8,128)(2,1)}, u32[]{:S(2)}, u32[]{:S(2)}) collective-permute-start(bf16[32,16,2,1]{3,0,2,1:T(8,128)(2,1)} %get-tuple-element.101), channel_id=1, source_target_pairs={{0,1},{1,2},{2,3},{3,4},{4,5},{5,6},{6,7},{7,8},{8,9},{9,10},{10,1... | collective-permute-start | bytes 6152 | tf_op jit(solution)/shard_map/ppermute | solution.py:14
  131.6 9.0 %collective-permute-start.11 = (bf16[32,16,2,1]{3,0,2,1:T(8,128)(2,1)S(1)}, bf16[32,16,2,1]{3,0,2,1:T(8,128)(2,1)}, u32[]{:S(2)}, u32[]{:S(2)}) collective-permute-start(bf16[32,16,2,1]{3,0,2,1:T(8,128)(2,1)S(1)} %get-tuple-element.102), channel_id=1, source_target_pairs={{1,0},{2,1},{3,2},{4,3},{5,4},{6,5},{7,6},{8,7},{9,8},{10,9},{11,1... | collective-permute-start | bytes 6152 | tf_op jit(solution)/shard_map/ppermute | solution.py:15
  147.0 24.5 %all-to-all-start.2 = ((bf16[32,16,2,256]{3,0,2,1:T(8,128)(2,1)}), bf16[32,16,2,256]{3,0,2,1:T(8,128)(2,1)}, u32[]{:S(2)}, u32[]{:S(2)}) async-start(bf16[32,16,2,256]{3,0,2,1:T(8,128)(2,1)} %fusion.156), calls=%async_computation.2 | async-start | bytes 1048576 | tf_op jit(solution)/shard_map/all_to_all | solution.py:118
  157.0 301.5 %all-reduce.11.cloned.1.call-start = ((), (), s32[]{:S(2)}) async-start(), calls=%async_computation.3 | async-start | bytes 1181696 | tf_op jit(solution)/shard_map/psum | solution.py:128
  176.7 6.0 %collective-permute-start.12 = (bf16[32,1,32,2]{3,0,2,1:T(8,128)(2,1)S(1)}, bf16[32,1,32,2]{3,0,2,1:T(8,128)(2,1)S(1)}, u32[]{:S(2)}, u32[]{:S(2)}) collective-permute-start(bf16[32,1,32,2]{3,0,2,1:T(8,128)(2,1)S(1)} %get-tuple-element.99), channel_id=1, source_target_pairs={{0,1},{1,2},{2,3},{3,4},{4,5},{5,6},{6,7},{7,8},{8,9},{9,10},{10,1... | collective-permute-start | bytes 12296 | tf_op jit(solution)/shard_map/ppermute | solution.py:14
  179.4 8.7 %collective-permute-start.13 = (bf16[32,1,32,2]{3,0,2,1:T(8,128)(2,1)S(1)}, bf16[32,1,32,2]{3,0,2,1:T(8,128)(2,1)S(1)}, u32[]{:S(2)}, u32[]{:S(2)}) collective-permute-start(bf16[32,1,32,2]{3,0,2,1:T(8,128)(2,1)S(1)} %get-tuple-element.100), channel_id=1, source_target_pairs={{1,0},{2,1},{3,2},{4,3},{5,4},{6,5},{7,6},{8,7},{9,8},{10,9},{11,1... | collective-permute-start | bytes 12296 | tf_op jit(solution)/shard_map/ppermute | solution.py:15
  196.7 5.3 %collective-permute-start.14 = (bf16[32,1,32,1]{3,0,2,1:T(8,128)(2,1)S(1)}, bf16[32,1,32,1]{3,0,2,1:T(8,128)(2,1)S(1)}, u32[]{:S(2)}, u32[]{:S(2)}) collective-permute-start(bf16[32,1,32,1]{3,0,2,1:T(8,128)(2,1)S(1)} %get-tuple-element.97), channel_id=1, source_target_pairs={{0,1},{1,2},{2,3},{3,4},{4,5},{5,6},{6,7},{7,8},{8,9},{9,10},{10,1... | collective-permute-start | bytes 6152 | tf_op jit(solution)/shard_map/ppermute | solution.py:14
  198.7 9.8 %collective-permute-start.15 = (bf16[32,1,32,1]{3,0,2,1:T(8,128)(2,1)S(1)}, bf16[32,1,32,1]{3,0,2,1:T(8,128)(2,1)S(1)}, u32[]{:S(2)}, u32[]{:S(2)}) collective-permute-start(bf16[32,1,32,1]{3,0,2,1:T(8,128)(2,1)S(1)} %get-tuple-element.98), channel_id=1, source_target_pairs={{1,0},{2,1},{3,2},{4,3},{5,4},{6,5},{7,6},{8,7},{9,8},{10,9},{11,1... | collective-permute-start | bytes 6152 | tf_op jit(solution)/shard_map/ppermute | solution.py:15
  (61 other events, 124.4 us)
Sparse Core Ops, SparseCore 0:
  202.2 256.3 all-reduce.10
where the time goes:
time: 476 us; the launch traced here: 474 us
  waiting for transfers between devices  284 us (60%)
  starting transfers between devices  66.7 us (14%)
  matrix products  41.9 us (9%)
  local copies, waits for them, and re-layouts  34.1 us (7%)
  other arithmetic  32.4 us (7%)
  between operations  15.4 us (3%)
    psum x1, waiting for transfers between devices, per_device(): lax.psum((grad_a, grad_b, grad_c, grad_d, grad_one, grad_two), ('slab', '...  245 us
    ppermute x8, waiting for transfers between devices, with_halo(): after = lax.ppermute(initial, axis, down)  26.7 us
    ppermute x8, starting transfers between devices, with_halo(): before = lax.ppermute(last, axis, up)  21.5 us
    dot_general x24, matrix products, conv_valid(): jnp.einsum('ok,kabx->oabx', weight_row, columns, preferred_element_type=j...  20.6 us
    ppermute x8, starting transfers between devices, with_halo(): after = lax.ppermute(initial, axis, down)  19.9 us
    dot_general x12, matrix products, weight_grad(): jnp.einsum('oabx,kabx->ok', delta_out, columns, preferred_element_type=jn...  17.3 us
    unnamed x135, local copies, waits for them, and re-layouts  13.4 us
    all_to_all x1, starting transfers between devices, per_device(): lax.all_to_all(hidden_two, 'slab', split_axis=2, concat_axis=1, tiled=True)  10.8 us
  transfers between devices with their start and end apart: 20, of which 13 were waited for; matrix products, arithmetic and copies ran while one was open for 9% of the time, Pallas kernels for 0%

commit v1 on v0

v1 whole, which is shorter than its diff:
```python
import functools

import jax
import jax.numpy as jnp
from jax import lax
from jax.experimental import pallas as pl
from jax.experimental.pallas import tpu as pltpu
from jax.sharding import PartitionSpec as P

HALO = 16
C = 32
F32 = jnp.float32
BF16 = jnp.bfloat16
VMEM = pl.BlockSpec(memory_space=pltpu.VMEM)
SMEM = pl.BlockSpec(memory_space=pltpu.SMEM)
PARAMS = pltpu.CompilerParams(vmem_limit_bytes=56 * 1024 * 1024)
CONTRACT_ROWS = (((0,), (0,)), ((), ()))
CONTRACT_LANES = (((1,), (1,)), ((), ()))


def softplus(v):
    small = jnp.exp(-jnp.abs(v))
    tail = jnp.where(small < 1e-4, small, jnp.log(1.0 + small))
    return jnp.maximum(v, 0.0) + tail


def slope(stored):
    return 1.0 - jnp.exp(-stored.astype(F32))


def gated(value, gates):
    rows = value.shape[0]
    return jnp.concatenate(
        [value[:HALO] * gates[0], value[HALO : rows - HALO], value[rows - HALO :] * gates[1]], axis=0
    )


def clear_margins(shifted):
    lanes = shifted.shape[-1]
    edge = jnp.zeros(shifted.shape[:-1] + (128,), BF16)
    shifted[..., 0:128] = edge
    shifted[..., lanes - 128 : lanes] = edge


def store_shifted(shifted, plane, start, value, step):
    rows, lanes = value.shape
    where = slice(128 + start, 128 + start + lanes)
    shifted[plane, 1, :, where] = value.astype(BF16)
    shifted[plane, 0, :, where] = pltpu.roll(value, step, 0).astype(BF16)
    shifted[plane, 2, :, where] = pltpu.roll(value, rows - step, 0).astype(BF16)


def conv_window(shifted, plane, window, band):
    lanes = slice(256 * window, 256 * window + 512)
    total = None
    for tap in range(3):
        term = jnp.dot(
            shifted[plane, tap, :, lanes],
            band[512 * tap : 512 * tap + 512, :],
            preferred_element_type=F32,
        )
        total = term if total is None else total + term
    return total


def windows_of(shifted):
    planes = shifted.shape[0]
    windows = (shifted.shape[-1] - 256) // 256
    return [(plane, window) for plane in range(planes) for window in range(windows)]


def weight_grad(delta, shifted, step, grads, first_piece):
    rows = delta.shape[2]
    own = slice(HALO, rows - HALO)
    for tap in range(3):
        total = None
        for plane, window in windows_of(shifted):
            term = lax.dot_general(
                delta[plane, 1, own, 128 + 256 * window : 384 + 256 * window],
                shifted[plane, tap, own, 256 * window : 256 * window + 512],
                CONTRACT_ROWS,
                preferred_element_type=F32,
            )
            total = term if total is None else total + term
        folded = None
        for r in range(4):
            near = total[32 * r : 32 * r + 32, 0:384]
            far = total[32 * r + 128 : 32 * r + 160, 128:512]
            part = near + far
            if r:
                part = pltpu.roll(part, 384 - 32 * r, 1)
            folded = part if folded is None else folded + part
        for row_tap in range(3):
            at = 32 * (4 + step * (row_tap - 1))
            put_piece(grads, first_piece + 3 * row_tap + tap, folded[:, at : at + 32])


def put_piece(grads, index, value):
    row, lane = 32 * (index // 4), 32 * (index % 4)
    grads[row : row + value.shape[0], lane : lane + 32] = value


def band_kernel(steps, base, *bands):
    lane = lax.broadcasted_iota(jnp.int32, (32, 128), 1) // 32
    for conv, (step, band) in enumerate(zip(steps, bands)):
        for col_tap in range(3):
            blocks = []
            for row_tap in range(3):
                at = 32 * (9 * conv + 3 * row_tap + col_tap)
                blocks.append(base[at : at + 32, :].astype(F32))
            cut = [[jnp.where(lane == q, block, 0.0) for q in range(4)] for block in blocks]
            for source in range(16):
                for group in range(2):
                    panel = None
                    for q in range(4):
                        off = source - 4 - (4 * group + q)
                        if off % step == 0 and abs(off) <= step:
                            term = cut[off // step + 1][q]
                            panel = term if panel is None else panel + term
                    if panel is None:
                        panel = jnp.zeros((32, 128), F32)
                    row = 512 * col_tap + 32 * source
                    band[row : row + 32, 128 * group : 128 * group + 128] = panel.astype(BF16)


def forward_xy_kernel(gate_ref, stem, band_a, band_b, hidden_one, hidden_two, message, stem_s, one_s):
    gates = (gate_ref[0], gate_ref[1])
    clear_margins(stem_s)
    clear_margins(one_s)
    for window in range(4):
        lanes = slice(256 * window, 256 * window + 256)
        store_shifted(stem_s, 0, 256 * window, stem[:, lanes].astype(F32), 1)
    for window in range(4):
        value = gated(softplus(conv_window(stem_s, 0, window, band_a)), gates)
        hidden_one[:, 256 * window : 256 * window + 256] = value.astype(BF16)
        store_shifted(one_s, 0, 256 * window, value, 2)
    for window in range(4):
        value = gated(softplus(conv_window(one_s, 0, window, band_b)), gates).astype(BF16)
        hidden_two[:, 256 * window : 256 * window + 256] = value
        half = value.shape[0] // 2
        for peer in range(4):
            lanes = slice(64 * peer, 64 * peer + 64)
            message[4 * window + peer] = jnp.concatenate(
                [value[:half, lanes], value[half:, lanes]], axis=1
            )


def section_xz_kernel(
    gate_ref, message, labels, head_one, head_two, band_c, band_d, band_dt, band_ct,
    probability, back, grads,
    two_s, ref_one_s, ref_two, delta_two_s, delta_one_s,
):
    gates = (gate_ref[0], gate_ref[1])
    rows = labels.shape[0]
    half = rows // 2
    own = slice(HALO, rows - HALO)
    for shifted in (two_s, ref_one_s, delta_two_s, delta_one_s):
        clear_margins(shifted)
    for plane in range(2):
        for group in range(4):
            parts = []
            for side in range(2):
                at = 64 * side + 32 * plane
                parts.append(
                    jnp.concatenate(
                        [message[4 * group + q][:, at : at + 32] for q in range(4)], axis=1
                    )
                )
            value = jnp.concatenate(parts, axis=0).astype(F32)
            store_shifted(two_s, plane, 128 * group, value, 1)
    for plane, window in windows_of(two_s):
        value = gated(softplus(conv_window(two_s, plane, window, band_c)), gates)
        store_shifted(ref_one_s, plane, 256 * window, value, 2)
    for plane, window in windows_of(two_s):
        value = softplus(conv_window(ref_one_s, plane, window, band_d))
        ref_two[plane, :, 256 * window : 256 * window + 256] = value.astype(BF16)

    voxel = lax.broadcasted_iota(jnp.int32, (32, 1024), 0)
    lane = lax.broadcasted_iota(jnp.int32, (32, 1024), 1) // 32
    same = voxel == lane
    spread_one = jnp.where(same, head_one[...], 0.0).astype(BF16)
    spread_two = jnp.where(same, head_two[...], 0.0).astype(BF16)
    first, second = None, None
    for plane in range(2):
        lanes = slice(512 * plane, 512 * plane + 512)
        one = lax.dot_general(
            two_s[plane, 1, :, 128:640], spread_one[:, lanes], CONTRACT_LANES,
            preferred_element_type=F32,
        )
        two = lax.dot_general(
            ref_two[plane], spread_two[:, lanes], CONTRACT_LANES, preferred_element_type=F32
        )
        first = one if first is None else first + one
        second = two if second is None else second + two
    first = first.astype(BF16).astype(F32)
    second = second + first
    share = 1.0 / (1.0 + jnp.exp(-second))
    probability[...] = share[own]
    error_two = gated(share - labels[...], gates)
    error_one = 1.0 / (1.0 + jnp.exp(-first)) - labels[...] + error_two

    def split(error):
        high = error.astype(BF16)
        low = (error - high.astype(F32)).astype(BF16)
        return jnp.concatenate([high, low], axis=1)

    error_two = split(error_two)
    error_one = split(error_one)
    spread_one = jnp.concatenate([spread_one, spread_one], axis=0)
    spread_two = jnp.concatenate([spread_two, spread_two], axis=0)
    same = jnp.concatenate([same, same], axis=0)

    def head_grad(error, planes):
        total = None
        for plane, feature in enumerate(planes):
            full = lax.dot_general(
                error[own], feature, CONTRACT_ROWS, preferred_element_type=F32
            )
            kept = jnp.where(same[:, 512 * plane : 512 * plane + 512], full, 0.0)
            kept = jnp.sum(kept, axis=0, keepdims=True)
            kept = kept[:, 0:128] + kept[:, 128:256] + kept[:, 256:384] + kept[:, 384:512]
            total = kept if total is None else total + kept
        total = total + pltpu.roll(total, 64, 1)
        total = total + pltpu.roll(total, 32, 1)
        return total[:, 0:32]

    grads[...] = jnp.zeros(grads.shape, F32)
    put_piece(grads, 18, head_grad(error_one, [two_s[plane, 1, own, 128:640] for plane in range(2)]))
    put_piece(grads, 19, head_grad(error_two, [ref_two[plane, own, :] for plane in range(2)]))

    for plane, window in windows_of(two_s):
        at = 256 * window
        lanes = slice(512 * plane + at, 512 * plane + at + 256)
        value = jnp.dot(error_two, spread_two[:, lanes], preferred_element_type=F32)
        value = value * slope(ref_two[plane, :, at : at + 256])
        store_shifted(delta_two_s, plane, at, value, 2)
    weight_grad(delta_two_s, ref_one_s, 2, grads, 9)
    for plane, window in windows_of(two_s):
        at = 256 * window
        value = conv_window(delta_two_s, plane, window, band_dt)
        value = gated(value * slope(ref_one_s[plane, 1, :, 128 + at : 384 + at]), gates)
        store_shifted(delta_one_s, plane, at, value, 1)
    weight_grad(delta_one_s, two_s, 1, grads, 0)
    for window in range(2):
        values = []
        for plane in range(2):
            at = 256 * window
            lanes = slice(512 * plane + at, 512 * plane + at + 256)
            value = conv_window(delta_one_s, plane, window, band_ct)
            value = value + jnp.dot(error_one, spread_one[:, lanes], preferred_element_type=F32)
            values.append(value.astype(BF16))
        for z in range(8):
            lanes = slice(32 * z, 32 * z + 32)
            back[8 * window + z] = jnp.concatenate(
                [
                    values[0][:half, lanes], values[1][:half, lanes],
                    values[0][half:, lanes], values[1][half:, lanes],
                ],
                axis=1,
            )


def backward_xy_kernel(
    gate_ref, back, stem, hidden_one, hidden_two, band_bt, band_at,
    stem_grad, grads,
    stem_s, one_s, delta_b_s, delta_a_s,
):
    gates = (gate_ref[0], gate_ref[1])
    rows = stem.shape[0]
    for shifted in (stem_s, one_s, delta_b_s, delta_a_s):
        clear_margins(shifted)
    for window in range(4):
        lanes = slice(256 * window, 256 * window + 256)
        store_shifted(stem_s, 0, 256 * window, stem[:, lanes].astype(F32), 1)
        store_shifted(one_s, 0, 256 * window, hidden_one[:, lanes].astype(F32), 2)
    for group in range(8):
        parts = []
        for side in range(2):
            at = 64 * side
            parts.append(
                jnp.concatenate(
                    [back[2 * group + q][:, at : at + 64] for q in range(2)], axis=1
                )
            )
        value = jnp.concatenate(parts, axis=0).astype(F32)
        value = gated(value * slope(hidden_two[:, 128 * group : 128 * group + 128]), gates)
        store_shifted(delta_b_s, 0, 128 * group, value, 2)
    grads[...] = jnp.zeros(grads.shape, F32)
    for window in range(4):
        at = 256 * window
        value = conv_window(delta_b_s, 0, window, band_bt)
        value = gated(value * slope(hidden_one[:, at : at + 256]), gates)
        store_shifted(delta_a_s, 0, at, value, 1)
    weight_grad(delta_b_s, one_s, 2, grads, 9)
    weight_grad(delta_a_s, stem_s, 1, grads, 0)
    for window in range(4):
        at = 256 * window
        value = conv_window(delta_a_s, 0, window, band_at)
        stem_grad[:, at : at + 256] = value[HALO : rows - HALO].astype(BF16)


def call(kernel, outs, specs, scratch=(), flops=0):
    return pl.pallas_call(
        kernel,
        out_shape=outs,
        in_specs=specs,
        out_specs=jax.tree.map(lambda _: VMEM, outs),
        scratch_shapes=scratch,
        compiler_params=PARAMS,
        cost_estimate=pl.CostEstimate(flops=flops, bytes_accessed=1 << 20, transcendentals=0),
    )


def shape(dims, dtype):
    return jax.ShapeDtypeStruct(dims, dtype)


def sum_everywhere(grads, slab, gx):
    peers, rows = lax.axis_size(gx), grads.shape[0]
    mine = lax.all_to_all(grads, gx, 0, 0, tiled=True)
    mine = jnp.sum(mine.reshape(peers, rows // peers, 128), axis=0)
    copies = lax.axis_size(slab)
    spread = jnp.broadcast_to(mine[None], (copies,) + mine.shape)
    mine = jnp.sum(lax.all_to_all(spread, slab, 0, 0, tiled=True), axis=0)
    spread = jnp.broadcast_to(mine[None], (peers,) + mine.shape)
    return lax.all_to_all(spread, gx, 0, 0, tiled=True).reshape(rows, 128)


def per_device(stem_features, labels, conv_a, conv_b, conv_c, conv_d, head_one, head_two):
    _, depth, height, cols = stem_features.shape
    rows = cols + 2 * HALO
    half = rows // 2
    peers = lax.axis_size("gx")
    me = lax.axis_index("gx")
    gates = jnp.stack([me > 0, me < peers - 1]).astype(F32)

    weights = jnp.stack([conv_a, conv_b, conv_c, conv_d])
    ahead = jnp.transpose(weights, (0, 2, 3, 4, 1))
    behind = jnp.transpose(weights[:, :, ::-1, ::-1, :], (0, 2, 3, 1, 4))
    base = jnp.concatenate([ahead, behind], axis=0).reshape(8 * 9 * C, C)
    base = jnp.tile(base, (1, 4))
    bands = call(
        functools.partial(band_kernel, (1, 2, 1, 2, 1, 2, 1, 2)),
        [shape((1536, 256), BF16)] * 8,
        [VMEM],
        flops=1 << 28,
    )(base)
    band_a, band_b, band_c, band_d, band_at, band_bt, band_ct, band_dt = bands

    stem = jnp.transpose(stem_features[:, 0], (2, 1, 0)).reshape(cols, height * C)
    marks = jnp.transpose(labels, (2, 1, 0)).reshape(cols, 32).astype(BF16)
    marks = jnp.pad(marks, ((0, 0), (0, 96)))
    both = jnp.concatenate([stem, marks], axis=1)
    up = [(i, i + 1) for i in range(peers - 1)]
    down = [(j, i) for i, j in up]
    before = lax.ppermute(both[cols - HALO :], "gx", up)
    after = lax.ppermute(both[:HALO], "gx", down)
    both = jnp.concatenate([before, both, after], axis=0)
    stem = both[:, : height * C]
    marks = both[:, height * C : height * C + 32].astype(F32)

    wide = pltpu.VMEM((1, 3, rows, 1280), BF16)
    tall = pltpu.VMEM((2, 3, rows, 768), BF16)
    hidden_one, hidden_two, message = call(
        forward_xy_kernel,
        [shape((rows, 1024), BF16), shape((rows, 1024), BF16), shape((16, half, 128), BF16)],
        [SMEM] + [VMEM] * 3,
        [wide, wide],
        flops=1 << 30,
    )(gates, stem, band_a, band_b)
    message = lax.all_to_all(message, "slab", 0, 0, tiled=True)
    tile_one = jnp.tile(head_one.astype(F32), 32)[None]
    tile_two = jnp.tile(head_two.astype(F32), 32)[None]
    probability, back, grads_cd = call(
        section_xz_kernel,
        [shape((cols, 32), F32), shape((16, half, 128), BF16), shape((160, 128), F32)],
        [SMEM] + [VMEM] * 8,
        [tall, tall, pltpu.VMEM((2, rows, 512), BF16), tall, tall],
        flops=1 << 31,
    )(gates, message, marks, tile_one, tile_two, band_c, band_d, band_dt, band_ct)
    back = lax.all_to_all(back, "slab", 0, 0, tiled=True)
    stem_grad, grads_ab = call(
        backward_xy_kernel,
        [shape((cols, 1024), BF16), shape((160, 128), F32)],
        [SMEM] + [VMEM] * 6,
        [wide, wide, wide, wide],
        flops=1 << 31,
    )(gates, back, stem, hidden_one, hidden_two, band_bt, band_at)

    stem_grad = jnp.transpose(stem_grad.reshape(cols, height, C), (2, 1, 0))[:, None]
    probability = jnp.transpose(probability.reshape(cols, 2, 16), (2, 1, 0))

    factor = 1.0 / (depth * height * cols)
    total = sum_everywhere(jnp.concatenate([grads_ab, grads_cd], axis=0), "slab", "gx") * factor
    pieces = total.reshape(2, 5, 32, 4, 32).transpose(0, 1, 3, 2, 4).reshape(2, 20, 32, 32)

    def kernel_grad(pair, first):
        taken = pieces[pair, first : first + 9].reshape(3, 3, 32, 32)
        return jnp.transpose(taken, (2, 0, 1, 3))

    return (
        probability,
        stem_grad,
        kernel_grad(0, 0),
        kernel_grad(0, 9),
        kernel_grad(1, 0),
        kernel_grad(1, 9),
        pieces[1, 18, 0],
        pieces[1, 19, 0],
    )


def solution(mesh):
    return jax.shard_map(
        per_device,
        mesh=mesh,
        in_specs=(P(None, "slab", None, "gx"), P(None, "slab", "gx"), P(), P(), P(), P(), P(), P()),
        out_specs=(
            P(None, "slab", "gx"),
            P(None, "slab", None, "gx"),
            P(),
            P(),
            P(),
            P(),
            P(),
            P(),
        ),
        check_vma=False,
    )
```

time: 476 us -> 137 us (0.29)
  waiting for transfers between devices: 284 us -> 20 us
  blocking collectives: 0 us -> 49.3 us
  starting transfers between devices: 66.7 us -> 23.2 us
  matrix products: 41.9 us -> 0 us
  other arithmetic: 32.4 us -> 3.26 us
  Pallas kernels: 0 us -> 28.5 us
  local copies, waits for them, and re-layouts: 34.1 us -> 10.7 us
  between operations: 15.4 us -> 0.89 us
    psum x1 -> x0, waiting for transfers between devices: 245 us -> none  [per_device(): lax.psum((grad_a, grad_b, grad_c, grad_d, grad_one, grad_two), ('slab', '...]
    all_to_all x0 -> x3, blocking collectives: none -> 49.3 us  [the longest x1 23.4 us: per_device(): back = lax.all_to_all(back, 'slab', 0, 0, tiled=True)]
    dot_general x40 -> x0, matrix products: 41.9 us -> none  [the longest x24 20.6 us: conv_valid(): jnp.einsum('ok,kabx->oabx', weight_row, columns, preferred_element_type=j...]
    ppermute x16 -> x2, starting transfers between devices: 41.4 us -> 6.52 us  [the longest x1 4.59 us: per_device(): before = lax.ppermute(both[cols - HALO:], 'gx', up)]
    pallas_call x0 -> x4, Pallas kernels: none -> 28.5 us  [the longest x1 11.3 us: per_device(): call(section_xz_kernel, [shape((cols, 32), F32), shape((16, half, 128), B...]
    ppermute x16 -> x2, waiting for transfers between devices: 27.8 us -> 0.01 us  [the longest x1 0.01 us: per_device(): before = lax.ppermute(both[cols - HALO:], 'gx', up)]
    concatenate x12 -> x3, other arithmetic: 17.3 us -> 1.07 us  [the longest x1 0.9 us: per_device(): jnp.concatenate([grads_ab, grads_cd], axis=0)]
    slice x36 -> x2, local copies, waits for them, and re-layouts: 15 us -> 1.71 us  [the longest x1 0.89 us: per_device(): stem = both[:, :height * C]]
  transfers between devices with their start and end apart: 20 -> 4, of which waited for: 13 -> 2; matrix products, arithmetic and copies ran while one was open for 9% -> 5% of each run, Pallas kernels for 0% -> 3%
where the time goes in v1:
time: 137 us; the launch traced here: 136 us
  blocking collectives  49.3 us (36%)
  Pallas kernels  28.5 us (21%)
  starting transfers between devices  23.2 us (17%)
  waiting for transfers between devices  20 us (15%)
  local copies, waits for them, and re-layouts  10.7 us (8%)
  other arithmetic  3.26 us (2%)
    all_to_all x1, blocking collectives, per_device(): back = lax.all_to_all(back, 'slab', 0, 0, tiled=True)  23.4 us
    all_to_all x1, waiting for transfers between devices, per_device(): message = lax.all_to_all(message, 'slab', 0, 0, tiled=True)  15.3 us
    all_to_all x1, blocking collectives, sum_everywhere(): mine = lax.all_to_all(grads, gx, 0, 0, tiled=True)  13.9 us
    all_to_all x1, blocking collectives, sum_everywhere(): mine = jnp.sum(lax.all_to_all(spread, slab, 0, 0, tiled=True), axis=0)  11.9 us
    pallas_call x1, Pallas kernels, per_device(): call(section_xz_kernel, [shape((cols, 32), F32), shape((16, half, 128), B...  11.3 us
    all_to_all x1, starting transfers between devices, per_device(): message = lax.all_to_all(message, 'slab', 0, 0, tiled=True)  10.9 us
    pallas_call x1, Pallas kernels, per_device(): call(backward_xy_kernel, [shape((cols, 1024), BF16), shape((160, 128), F3...  7.48 us
    all_to_all x1, starting transfers between devices, sum_everywhere(): return lax.all_to_all(spread, gx, 0, 0, tiled=True).reshape(rows, 128)  5.75 us
  transfers between devices with their start and end apart: 4, of which 2 were waited for; matrix products, arithmetic and copies ran while one was open for 5% of the time, Pallas kernels for 3%

profile of v1, /device:TPU:1, one launch (start us, length us, event | category | flops | bytes accessed | tf_op | source)
XLA Modules:
  0.0 135.8 jit_solution(10668232345501695919)
XLA Ops:
  0.6 0.8 copy_convert_fusion
  1.5 1.3 copy.56
  3.2 4.6 %collective-permute-start = (bf16[16,1152]{1,0:T(8,128)(2,1)S(1)}, bf16[16,1152]{1,0:T(8,128)(2,1)S(1)}, u32[]{:S(2)}, u32[]{:S(2)}) collective-permute-start(bf16[16,1152]{1,0:T(8,128)(2,1)S(1)} %get-tuple-element.78), channel_id=1, source_target_pairs={{0,1},{1,2},{2,3},{3,4},{4,5},{5,6},{6,7},{7,8},{8,9},{9,10},{10,1... | collective-permute-start | bytes 110600 | tf_op jit(solution)/shard_map/ppermute | solution.py:356
  7.8 1.9 %collective-permute-start.1 = (bf16[16,1152]{1,0:T(8,128)(2,1)S(1)}, bf16[16,1152]{1,0:T(8,128)(2,1)S(1)}, u32[]{:S(2)}, u32[]{:S(2)}) collective-permute-start(bf16[16,1152]{1,0:T(8,128)(2,1)S(1)} %get-tuple-element.79), channel_id=1, source_target_pairs={{1,0},{2,1},{3,2},{4,3},{5,4},{6,5},{7,6},{8,7},{9,8},{10,9},{11,1... | collective-permute-start | bytes 110600 | tf_op jit(solution)/shard_map/ppermute | solution.py:357
  11.0 1.1 copy.62.base
  12.1 4.2 %shard_map.143 = (bf16[1536,256]{1,0:T(8,128)(2,1)}, bf16[1536,256]{1,0:T(8,128)(2,1)}, bf16[1536,256]{1,0:T(8,128)(2,1)}, bf16[1536,256]{1,0:T(8,128)(2,1)}, bf...) custom-call(bf16[2304,128]{1,0:T(8,128)(2,1)} %copy.62.base), custom_call_target="tpu_custom_call" | custom-call | flops 268435456 | bytes 1048576 | tf_op jit(solution)/shard_map/pallas_call | solution.py:342
  16.4 0.9 slice.40.stem
  17.3 5.5 %shard_map.144 = (bf16[288,1024]{1,0:T(8,128)(2,1)}, bf16[288,1024]{1,0:T(8,128)(2,1)}, bf16[16,144,128]{2,1,0:T(8,128)(2,1)}) custom-call(f32[2]{0:T(128)} %add_convert_fusion.gate_ref, bf16[288,1024]{1,0:T(8,128)(2,1)} %slice.40.stem, bf16[1536,256]{1,0:T(8,128)(2,1)} %get-tuple-element.24.band_a, bf16[1536,256]{1,0:T(8,128)(2,1)} %get-tuple-element.25.band_b), custom_call_target="tpu_custom_call" | custom-call | flops 1073741824 | bytes 1048576 | tf_op jit(solution)/shard_map/pallas_call | solution.py:364
  22.8 10.9 %all-to-all-start = ((bf16[16,144,128]{2,1,0:T(8,128)(2,1)}), bf16[16,144,128]{2,1,0:T(8,128)(2,1)S(1)}, u32[]{:S(2)}, u32[]{:S(2)}) async-start(bf16[16,144,128]{2,1,0:T(8,128)(2,1)} %get-tuple-element.26), calls=%async_computation | async-start | bytes 1179648 | tf_op jit(solution)/shard_map/all_to_all | solution.py:371
  33.7 0.7 broadcast_in_dim_tile.6.head_one
  34.4 0.7 broadcast_in_dim_tile.7.head_two
  35.8 15.3 %all-to-all-done.message = bf16[16,144,128]{2,1,0:T(8,128)(2,1)S(1)} async-done(((bf16[16,144,128]{2,1,0:T(8,128)(2,1)}), bf16[16,144,128]{2,1,0:T(8,128)(2,1)S(1)}, u32[]{:S(2)}, u32[]{:S(2)}) %all-to-all-start) | async-done | bytes 589856 | tf_op jit(solution)/shard_map/all_to_all | solution.py:371
  51.1 0.8 copy-done
  51.9 11.3 %shard_map.145 = (f32[256,32]{1,0:T(8,128)}, bf16[16,144,128]{2,1,0:T(8,128)(2,1)}, f32[160,128]{1,0:T(8,128)}) custom-call(f32[2]{0:T(128)} %add_convert_fusion.gate_ref, bf16[16,144,128]{2,1,0:T(8,128)(2,1)} %copy-done, f32[288,32]{1,0:T(8,128)} %maximum_convert_fusion.labels, f32[1,1024]{1,0:T(1,128)} %broadcast_in_dim_tile.6.head_one, ...), custom_call_target="tpu_custom_call" | custom-call | flops 2147483648 | bytes 1048576 | tf_op jit(solution)/shard_map/pallas_call | solution.py:374
  63.1 23.4 %all_to_all.29.back = bf16[16,144,128]{2,1,0:T(8,128)(2,1)} all-to-all(bf16[16,144,128]{2,1,0:T(8,128)(2,1)} %get-tuple-element.32), channel_id=1, replica_groups=mesh['slab'=16,'gx'=16] {'slab'}, dimensions={0} | all-to-all | bytes 1179648 | tf_op jit(solution)/shard_map/all_to_all | solution.py:381
  86.6 7.5 %shard_map.146 = (bf16[256,1024]{1,0:T(8,128)(2,1)}, f32[160,128]{1,0:T(8,128)}) custom-call(f32[2]{0:T(128)} %add_convert_fusion.gate_ref, bf16[16,144,128]{2,1,0:T(8,128)(2,1)} %all_to_all.29.back, bf16[288,1024]{1,0:T(8,128)(2,1)} %slice.40.stem, bf16[288,1024]{1,0:T(8,128)(2,1)} %get-tuple-element.33.hidden_one, ...), custom_call_target="tpu_custom_call" | custom-call | flops 2147483648 | bytes 1048576 | tf_op jit(solution)/shard_map/pallas_call | solution.py:382
  94.1 0.9 pad_maximum_fusion.3
  95.0 13.9 %all_to_all.30 = f32[16,20,128]{2,1,0:T(8,128)S(1)} all-to-all(f32[16,20,128]{2,1,0:T(8,128)S(1)} %all_to_all.20), channel_id=1, replica_groups=mesh['slab'=16,'gx'=16] {'gx'}, dimensions={0} | all-to-all | bytes 327680 | tf_op jit(solution)/shard_map/all_to_all | solution.py:320
  109.0 11.9 %all_to_all.31 = f32[16,20,128]{2,1,0:T(8,128)S(1)} all-to-all(f32[16,20,128]{2,1,0:T(8,128)S(1)} %broadcast_in_dim.7), channel_id=1, replica_groups=mesh['slab'=16,'gx'=16] {'slab'}, dimensions={0} | all-to-all | bytes 327680 | tf_op jit(solution)/shard_map/all_to_all | solution.py:324
  120.9 0.7 broadcast_in_dim.8
  121.6 5.8 %all-to-all-start.4 = ((f32[16,20,128]{2,1,0:T(8,128)}), f32[16,20,128]{2,1,0:T(8,128)S(1)}, u32[]{:S(2)}, u32[]{:S(2)}) async-start(f32[16,20,128]{2,1,0:T(8,128)} %broadcast_in_dim.8), calls=%async_computation.4 | async-start | bytes 393216 | tf_op jit(solution)/shard_map/all_to_all | solution.py:326
  128.3 1.1 copy.68
  129.3 4.7 %all-to-all-done.4 = f32[16,20,128]{2,1,0:T(8,128)S(1)} async-done(((f32[16,20,128]{2,1,0:T(8,128)}), f32[16,20,128]{2,1,0:T(8,128)S(1)}, u32[]{:S(2)}, u32[]{:S(2)}) %all-to-all-start.4) | async-done | bytes 163872 | tf_op jit(solution)/shard_map/all_to_all | solution.py:326
  135.0 0.8 fusion
  (47 shorter events, 4.3 us)
Async XLA Ops:
  2.9 6.8 %copy-start.4 = (bf16[32,3,3,32]{3,0,2,1:T(8,128)(2,1)S(1)}, bf16[32,3,3,32]{3,0,2,1:T(8,128)(2,1)}, u32[]{:S(2)}) copy-start(bf16[32,3,3,32]{3,0,2,1:T(8,128)(2,1)} %param.13) | copy-start | bytes 55300
  2.9 6.8 %copy-start.5 = (bf16[32,3,3,32]{3,0,2,1:T(8,128)(2,1)S(1)}, bf16[32,3,3,32]{3,0,2,1:T(8,128)(2,1)}, u32[]{:S(2)}) copy-start(bf16[32,3,3,32]{3,0,2,1:T(8,128)(2,1)} %param.12) | copy-start | bytes 55300
  2.9 6.8 %copy-start.6 = (bf16[32,3,3,32]{3,0,2,1:T(8,128)(2,1)S(1)}, bf16[32,3,3,32]{3,0,2,1:T(8,128)(2,1)}, u32[]{:S(2)}) copy-start(bf16[32,3,3,32]{3,0,2,1:T(8,128)(2,1)} %param.11) | copy-start | bytes 55300
  2.9 6.8 %copy-start.7 = (bf16[32,3,3,32]{3,0,2,1:T(8,128)(2,1)S(1)}, bf16[32,3,3,32]{3,0,2,1:T(8,128)(2,1)}, u32[]{:S(2)}) copy-start(bf16[32,3,3,32]{3,0,2,1:T(8,128)(2,1)} %param.10) | copy-start | bytes 55300
  3.2 13.2 %collective-permute-start = (bf16[16,1152]{1,0:T(8,128)(2,1)S(1)}, bf16[16,1152]{1,0:T(8,128)(2,1)S(1)}, u32[]{:S(2)}, u32[]{:S(2)}) collective-permute-start(bf16[16,1152]{1,0:T(8,128)(2,1)S(1)} %get-tuple-element.78), channel_id=1, source_target_pairs={{0,1},{1,2},{2,3},{3,4},{4,5},{5,6},{6,7},{7,8},{8,9},{9,10},{10,1... | collective-permute-start | bytes 110600 | tf_op jit(solution)/shard_map/ppermute | solution.py:356
  7.8 8.6 %collective-permute-start.1 = (bf16[16,1152]{1,0:T(8,128)(2,1)S(1)}, bf16[16,1152]{1,0:T(8,128)(2,1)S(1)}, u32[]{:S(2)}, u32[]{:S(2)}) collective-permute-start(bf16[16,1152]{1,0:T(8,128)(2,1)S(1)} %get-tuple-element.79), channel_id=1, source_target_pairs={{1,0},{2,1},{3,2},{4,3},{5,4},{6,5},{7,6},{8,7},{9,8},{10,9},{11,1... | collective-permute-start | bytes 110600 | tf_op jit(solution)/shard_map/ppermute | solution.py:357
  22.8 10.9 %copy-start.8 = (bf16[32]{0:T(256)(128)(2,1)S(1)}, bf16[32]{0:T(256)(128)(2,1)}, u32[]{:S(2)}) copy-start(bf16[32]{0:T(256)(128)(2,1)} %param.14) | copy-start | bytes 196
  22.8 11.6 %copy-start.9 = (bf16[32]{0:T(256)(128)(2,1)S(1)}, bf16[32]{0:T(256)(128)(2,1)}, u32[]{:S(2)}) copy-start(bf16[32]{0:T(256)(128)(2,1)} %param.15) | copy-start | bytes 196
  22.8 28.2 %all-to-all-start = ((bf16[16,144,128]{2,1,0:T(8,128)(2,1)}), bf16[16,144,128]{2,1,0:T(8,128)(2,1)S(1)}, u32[]{:S(2)}, u32[]{:S(2)}) async-start(bf16[16,144,128]{2,1,0:T(8,128)(2,1)} %get-tuple-element.26), calls=%async_computation | async-start | bytes 1179648 | tf_op jit(solution)/shard_map/all_to_all | solution.py:371
  51.1 0.8 copy-start
  86.6 7.5 %copy-start.3 = (f32[160,128]{1,0:T(8,128)S(1)}, f32[160,128]{1,0:T(8,128)}, u32[]{:S(2)}) copy-start(f32[160,128]{1,0:T(8,128)} %get-tuple-element.39) | copy-start | bytes 245764
  108.9 18.4 %copy-start.2 = (f32[256,32]{1,0:T(8,128)S(1)}, f32[256,32]{1,0:T(8,128)}, u32[]{:S(2)}) copy-start(f32[256,32]{1,0:T(8,128)} %get-tuple-element.31) | copy-start | bytes 98308
  109.0 19.1 %copy-start.1 = (bf16[256,1024]{1,0:T(8,128)(2,1)S(1)}, bf16[256,1024]{1,0:T(8,128)(2,1)}, u32[]{:S(2)}) copy-start(bf16[256,1024]{1,0:T(8,128)(2,1)} %get-tuple-element.37) | copy-start | bytes 1572868
  121.6 12.5 %all-to-all-start.4 = ((f32[16,20,128]{2,1,0:T(8,128)}), f32[16,20,128]{2,1,0:T(8,128)S(1)}, u32[]{:S(2)}, u32[]{:S(2)}) async-start(f32[16,20,128]{2,1,0:T(8,128)} %broadcast_in_dim.8), calls=%async_computation.4 | async-start | bytes 393216 | tf_op jit(solution)/shard_map/all_to_all | solution.py:326

commit v2 on v1

v2 whole, which is shorter than its diff:
```python
import functools

import jax
import jax.numpy as jnp
from jax import lax
from jax.experimental import pallas as pl
from jax.experimental.pallas import tpu as pltpu
from jax.sharding import PartitionSpec as P

HALO = 16
C = 32
F32 = jnp.float32
BF16 = jnp.bfloat16
VMEM = pl.BlockSpec(memory_space=pltpu.VMEM)
CONTRACT_ROWS = (((0,), (0,)), ((), ()))
CONTRACT_LANES = (((1,), (1,)), ((), ()))


def softplus(v):
    small = jnp.exp(-jnp.abs(v))
    tail = jnp.where(small < 1e-4, small, jnp.log(1.0 + small))
    return jnp.maximum(v, 0.0) + tail


def slope(stored):
    return 1.0 - jnp.exp(-stored.astype(F32))


def edge_gates():
    me, peers = lax.axis_index("gx"), lax.axis_size("gx")
    return jnp.where(me > 0, 1.0, 0.0), jnp.where(me < peers - 1, 1.0, 0.0)


def gated(value, gates):
    rows = value.shape[0]
    return jnp.concatenate(
        [value[:HALO] * gates[0], value[HALO : rows - HALO], value[rows - HALO :] * gates[1]], axis=0
    )


def clear_margins(shifted):
    lanes = shifted.shape[-1]
    edge = jnp.zeros(shifted.shape[:-1] + (128,), BF16)
    shifted[..., 0:128] = edge
    shifted[..., lanes - 128 : lanes] = edge


def store_shifted(shifted, plane, start, value, step):
    rows, lanes = value.shape
    where = slice(128 + start, 128 + start + lanes)
    shifted[plane, 1, :, where] = value.astype(BF16)
    shifted[plane, 0, :, where] = pltpu.roll(value, step, 0).astype(BF16)
    shifted[plane, 2, :, where] = pltpu.roll(value, rows - step, 0).astype(BF16)


def conv_window(shifted, plane, window, band):
    lanes = slice(256 * window, 256 * window + 512)
    total = None
    for tap in range(3):
        term = jnp.dot(
            shifted[plane, tap, :, lanes],
            band[512 * tap : 512 * tap + 512, :],
            preferred_element_type=F32,
        )
        total = term if total is None else total + term
    return total


def windows_of(shifted):
    planes = shifted.shape[0]
    windows = (shifted.shape[-1] - 256) // 256
    return [(plane, window) for plane in range(planes) for window in range(windows)]


def weight_grad(delta, shifted, step, grads, first_piece):
    rows = delta.shape[1]
    own = slice(HALO, rows - HALO)
    for tap in range(3):
        total = None
        for plane, window in windows_of(shifted):
            term = lax.dot_general(
                delta[plane, own, 256 * window : 256 * window + 256],
                shifted[plane, tap, own, 256 * window : 256 * window + 512],
                CONTRACT_ROWS,
                preferred_element_type=F32,
            )
            total = term if total is None else total + term
        folded = None
        for r in range(4):
            near = total[32 * r : 32 * r + 32, 0:384]
            far = total[32 * r + 128 : 32 * r + 160, 128:512]
            part = near + far
            if r:
                part = pltpu.roll(part, 384 - 32 * r, 1)
            folded = part if folded is None else folded + part
        for row_tap in range(3):
            at = 32 * (4 + step * (row_tap - 1))
            put_piece(grads, first_piece + 3 * row_tap + tap, folded[:, at : at + 32])


def put_piece(grads, index, value):
    row, lane = 32 * (index // 4), 32 * (index % 4)
    grads[row : row + value.shape[0], lane : lane + 32] = value


def band_kernel(plans, *refs):
    weights, bands = refs[: len(plans)], refs[len(plans) :]
    lane = lax.broadcasted_iota(jnp.int32, (32, 128), 1) // 32
    for (step, backward), weight, band in zip(plans, weights, bands):
        for col_tap in range(3):
            cut = []
            for row_tap in range(3):
                if backward:
                    block = weight[2 - row_tap, 2 - col_tap].astype(F32)
                else:
                    block = weight[row_tap, col_tap].astype(F32).T
                block = jnp.concatenate([block] * 4, axis=1)
                cut.append([jnp.where(lane == q, block, 0.0) for q in range(4)])
            for source in range(16):
                for group in range(2):
                    panel = None
                    for q in range(4):
                        off = source - 4 - (4 * group + q)
                        if off % step == 0 and abs(off) <= step:
                            term = cut[off // step + 1][q]
                            panel = term if panel is None else panel + term
                    if panel is None:
                        panel = jnp.zeros((32, 128), F32)
                    row = 512 * col_tap + 32 * source
                    band[row : row + 32, 128 * group : 128 * group + 128] = panel.astype(BF16)


def load_stem(before, stem, after, stem_s):
    for window in range(4):
        lanes = slice(256 * window, 256 * window + 256)
        value = jnp.concatenate([before[:, lanes], stem[:, lanes], after[:, lanes]], axis=0)
        store_shifted(stem_s, 0, 256 * window, value.astype(F32), 1)


def forward_xy_kernel(
    before, stem, after, band_a, band_b, hidden_one, hidden_two, message, stem_s, one_s
):
    gates = edge_gates()
    clear_margins(stem_s)
    clear_margins(one_s)
    load_stem(before, stem, after, stem_s)
    for window in range(4):
        value = gated(softplus(conv_window(stem_s, 0, window, band_a)), gates)
        hidden_one[:, 256 * window : 256 * window + 256] = value.astype(BF16)
        store_shifted(one_s, 0, 256 * window, value, 2)
    for window in range(4):
        value = gated(softplus(conv_window(one_s, 0, window, band_b)), gates).astype(BF16)
        hidden_two[:, 256 * window : 256 * window + 256] = value
        half = value.shape[0] // 2
        for peer in range(4):
            lanes = slice(64 * peer, 64 * peer + 64)
            message[4 * window + peer] = jnp.concatenate(
                [value[:half, lanes], value[half:, lanes]], axis=1
            )


def load_features(message, two_s):
    for plane in range(2):
        for group in range(4):
            parts = []
            for side in range(2):
                at = 64 * side + 32 * plane
                parts.append(
                    jnp.concatenate(
                        [message[4 * group + q][:, at : at + 32] for q in range(4)], axis=1
                    )
                )
            value = jnp.concatenate(parts, axis=0).astype(F32)
            store_shifted(two_s, plane, 128 * group, value, 1)


def own_voxel():
    voxel = lax.broadcasted_iota(jnp.int32, (32, 1024), 0)
    return voxel == lax.broadcasted_iota(jnp.int32, (32, 1024), 1) // 32


def split(error):
    high = error.astype(BF16)
    low = (error - high.astype(F32)).astype(BF16)
    return jnp.concatenate([high, low], axis=1)


def section_xz_kernel(
    message, labels, head_one, head_two, band_c, band_d, band_dt, band_ct,
    probability, back, ref_one, ref_two, delta_two, delta_one, errors_one, errors_two,
    two_s, ref_one_s, delta_two_s, delta_one_s,
):
    gates = edge_gates()
    rows = labels.shape[0]
    half = rows // 2
    own = slice(HALO, rows - HALO)
    for shifted in (two_s, ref_one_s, delta_two_s, delta_one_s):
        clear_margins(shifted)
    load_features(message, two_s)
    for plane, window in windows_of(two_s):
        at = 256 * window
        value = gated(softplus(conv_window(two_s, plane, window, band_c)), gates)
        ref_one[plane, :, at : at + 256] = value.astype(BF16)
        store_shifted(ref_one_s, plane, at, value, 2)
    for plane, window in windows_of(two_s):
        value = softplus(conv_window(ref_one_s, plane, window, band_d))
        ref_two[plane, :, 256 * window : 256 * window + 256] = value.astype(BF16)

    same = own_voxel()
    spread_one = jnp.where(same, head_one[...], 0.0).astype(BF16)
    spread_two = jnp.where(same, head_two[...], 0.0).astype(BF16)
    first, second = None, None
    for plane in range(2):
        lanes = slice(512 * plane, 512 * plane + 512)
        one = lax.dot_general(
            two_s[plane, 1, :, 128:640], spread_one[:, lanes], CONTRACT_LANES,
            preferred_element_type=F32,
        )
        two = lax.dot_general(
            ref_two[plane], spread_two[:, lanes], CONTRACT_LANES, preferred_element_type=F32
        )
        first = one if first is None else first + one
        second = two if second is None else second + two
    first = first.astype(BF16).astype(F32)
    second = second + first
    share = 1.0 / (1.0 + jnp.exp(-second))
    probability[...] = share[own]
    error_two = gated(share - labels[...], gates)
    error_one = 1.0 / (1.0 + jnp.exp(-first)) - labels[...] + error_two
    error_two = split(error_two)
    error_one = split(error_one)
    errors_one[...] = error_one
    errors_two[...] = error_two
    spread_one = jnp.concatenate([spread_one, spread_one], axis=0)
    spread_two = jnp.concatenate([spread_two, spread_two], axis=0)

    for plane, window in windows_of(two_s):
        at = 256 * window
        lanes = slice(512 * plane + at, 512 * plane + at + 256)
        value = jnp.dot(error_two, spread_two[:, lanes], preferred_element_type=F32)
        value = value * slope(ref_two[plane, :, at : at + 256])
        delta_two[plane, :, at : at + 256] = value.astype(BF16)
        store_shifted(delta_two_s, plane, at, value, 2)
    for plane, window in windows_of(two_s):
        at = 256 * window
        value = conv_window(delta_two_s, plane, window, band_dt)
        value = gated(value * slope(ref_one[plane, :, at : at + 256]), gates)
        delta_one[plane, :, at : at + 256] = value.astype(BF16)
        store_shifted(delta_one_s, plane, at, value, 1)
    for window in range(2):
        values = []
        for plane in range(2):
            at = 256 * window
            lanes = slice(512 * plane + at, 512 * plane + at + 256)
            value = conv_window(delta_one_s, plane, window, band_ct)
            value = value + jnp.dot(error_one, spread_one[:, lanes], preferred_element_type=F32)
            values.append(value.astype(BF16))
        for z in range(8):
            lanes = slice(32 * z, 32 * z + 32)
            back[8 * window + z] = jnp.concatenate(
                [
                    values[0][:half, lanes], values[1][:half, lanes],
                    values[0][half:, lanes], values[1][half:, lanes],
                ],
                axis=1,
            )


def section_grads_kernel(
    message, ref_one, ref_two, delta_two, delta_one, errors_one, errors_two,
    grads_out, two_s, ref_one_s, grads,
):
    rows = errors_one.shape[0]
    own = slice(HALO, rows - HALO)
    same = own_voxel()
    same = jnp.concatenate([same, same], axis=0)
    clear_margins(two_s)
    clear_margins(ref_one_s)
    load_features(message, two_s)
    for plane, window in windows_of(two_s):
        at = 256 * window
        value = ref_one[plane, :, at : at + 256].astype(F32)
        store_shifted(ref_one_s, plane, at, value, 2)

    def head_grad(error, planes):
        total = None
        for plane, feature in enumerate(planes):
            full = lax.dot_general(
                error[own, :], feature, CONTRACT_ROWS, preferred_element_type=F32
            )
            kept = jnp.where(same[:, 512 * plane : 512 * plane + 512], full, 0.0)
            kept = jnp.sum(kept, axis=0, keepdims=True)
            kept = kept[:, 0:128] + kept[:, 128:256] + kept[:, 256:384] + kept[:, 384:512]
            total = kept if total is None else total + kept
        total = total + pltpu.roll(total, 64, 1)
        total = total + pltpu.roll(total, 32, 1)
        return total[:, 0:32]

    grads[...] = jnp.zeros(grads.shape, F32)
    features = [two_s[plane, 1, own, 128:640] for plane in range(2)]
    put_piece(grads, 18, head_grad(errors_one, features))
    put_piece(grads, 19, head_grad(errors_two, [ref_two[plane, own, :] for plane in range(2)]))
    weight_grad(delta_two, ref_one_s, 2, grads, 9)
    weight_grad(delta_one, two_s, 1, grads, 0)
    grads_out[...] = grads[...].astype(BF16)


def backward_xy_kernel(
    back, before, stem, after, hidden_one, hidden_two, band_bt, grads_cd,
    delta_a, grads_out,
    stem_s, one_s, delta_b_s, delta_b, grads,
):
    gates = edge_gates()
    for shifted in (stem_s, one_s, delta_b_s):
        clear_margins(shifted)
    load_stem(before, stem, after, stem_s)
    for window in range(4):
        lanes = slice(256 * window, 256 * window + 256)
        store_shifted(one_s, 0, 256 * window, hidden_one[:, lanes].astype(F32), 2)
    for group in range(8):
        parts = []
        for side in range(2):
            at = 64 * side
            parts.append(
                jnp.concatenate(
                    [back[2 * group + q][:, at : at + 64] for q in range(2)], axis=1
                )
            )
        lanes = slice(128 * group, 128 * group + 128)
        value = jnp.concatenate(parts, axis=0).astype(F32)
        value = gated(value * slope(hidden_two[:, lanes]), gates)
        delta_b[0, :, lanes] = value.astype(BF16)
        store_shifted(delta_b_s, 0, 128 * group, value, 2)
    grads[...] = jnp.zeros(grads.shape, F32)
    for window in range(4):
        at = 256 * window
        value = conv_window(delta_b_s, 0, window, band_bt)
        value = gated(value * slope(hidden_one[:, at : at + 256]), gates)
        delta_a[0, :, at : at + 256] = value.astype(BF16)
    weight_grad(delta_b, one_s, 2, grads, 9)
    weight_grad(delta_a, stem_s, 1, grads, 0)
    for peer in range(8):
        grads_out[peer] = grads[20 * peer : 20 * peer + 20, :].astype(BF16)
        grads_out[8 + peer] = grads_cd[20 * peer : 20 * peer + 20, :]


def stem_grad_kernel(delta_a, band_at, stem_grad, delta_a_s):
    rows = delta_a.shape[1]
    clear_margins(delta_a_s)
    for window in range(4):
        lanes = slice(256 * window, 256 * window + 256)
        store_shifted(delta_a_s, 0, 256 * window, delta_a[0, :, lanes].astype(F32), 1)
    for window in range(4):
        at = 256 * window
        value = conv_window(delta_a_s, 0, window, band_at)
        stem_grad[:, at : at + 256] = value[HALO : rows - HALO].astype(BF16)


def finish_kernel(factor, total, grad_a, grad_b, grad_c, grad_d, head_one, head_two):
    flat = total[...].reshape(320, 128) * factor

    def piece(pair, index):
        row, lane = 160 * pair + 32 * (index // 4), 32 * (index % 4)
        return flat[row : row + 32, lane : lane + 32]

    for pair, (near, far) in enumerate(((grad_a, grad_b), (grad_c, grad_d))):
        for tap in range(9):
            near[tap // 3, tap % 3] = piece(pair, tap)
            far[tap // 3, tap % 3] = piece(pair, 9 + tap)
    head_one[...] = piece(1, 18)[0:1]
    head_two[...] = piece(1, 19)[0:1]


def call(kernel, outs, count, scratch=(), flops=0, megabytes=16):
    return pl.pallas_call(
        kernel,
        out_shape=outs,
        in_specs=[VMEM] * count,
        out_specs=jax.tree.map(lambda _: VMEM, outs),
        scratch_shapes=scratch,
        compiler_params=pltpu.CompilerParams(vmem_limit_bytes=megabytes * 1024 * 1024),
        cost_estimate=pl.CostEstimate(flops=flops, bytes_accessed=1 << 20, transcendentals=0),
    )


def shape(dims, dtype):
    return jax.ShapeDtypeStruct(dims, dtype)


def sum_everywhere(grads, slab, gx):
    peers, copies = lax.axis_size(gx), lax.axis_size(slab)
    mine = lax.all_to_all(grads, gx, 0, 0, tiled=True)
    mine = jnp.sum(mine.astype(F32), axis=0)
    spread = jnp.broadcast_to(mine[None], (copies,) + mine.shape)
    mine = jnp.sum(lax.all_to_all(spread, slab, 0, 0, tiled=True), axis=0)
    spread = jnp.broadcast_to(mine[None], (peers,) + mine.shape)
    return lax.all_to_all(spread, gx, 0, 0, tiled=True)


def per_device(stem_features, labels, conv_a, conv_b, conv_c, conv_d, head_one, head_two):
    _, depth, height, cols = stem_features.shape
    rows = cols + 2 * HALO
    half = rows // 2
    peers = lax.axis_size("gx")
    up = [(i, i + 1) for i in range(peers - 1)]
    down = [(j, i) for i, j in up]

    def columns_first(part):
        return jnp.transpose(part, (2, 1, 0)).reshape(part.shape[2], -1)

    slab = stem_features[:, 0]
    last = columns_first(slab[:, :, cols - HALO :])
    initial = columns_first(slab[:, :, :HALO])
    before = lax.ppermute(last, "gx", up)
    after = lax.ppermute(initial, "gx", down)
    stem = columns_first(slab)

    weights = [jnp.transpose(w, (1, 2, 0, 3)) for w in (conv_a, conv_b, conv_c, conv_d)]
    band = shape((1536, 256), BF16)
    band_a, band_b = call(
        functools.partial(band_kernel, ((1, False), (2, False))),
        [band] * 2, 2, flops=1 << 29, megabytes=8,
    )(*weights[:2])

    wide = pltpu.VMEM((1, 3, rows, 1280), BF16)
    tall = pltpu.VMEM((2, 3, rows, 768), BF16)
    whole = shape((rows, 1024), BF16)
    sections = shape((2, rows, 512), BF16)
    hidden_one, hidden_two, message = call(
        forward_xy_kernel,
        [whole, whole, shape((16, half, 128), BF16)],
        5, [wide, wide], flops=1 << 30, megabytes=16,
    )(before, stem, after, band_a, band_b)

    message, labels, weights, head_one, head_two = lax.optimization_barrier(
        (message, labels, weights, head_one, head_two)
    )
    message = lax.all_to_all(message, "slab", 0, 0, tiled=True)
    marks = columns_first(labels).astype(F32)
    marks_before = lax.ppermute(marks[cols - HALO :], "gx", up)
    marks_after = lax.ppermute(marks[:HALO], "gx", down)
    marks = jnp.concatenate([marks_before, marks, marks_after], axis=0)
    band_c, band_d, band_ct, band_dt, band_bt, band_at = call(
        functools.partial(
            band_kernel,
            ((1, False), (2, False), (1, True), (2, True), (2, True), (1, True)),
        ),
        [band] * 6, 6, flops=1 << 31, megabytes=8,
    )(weights[2], weights[3], weights[2], weights[3], weights[1], weights[0])
    tile_one = jnp.tile(head_one.astype(F32), 32)[None]
    tile_two = jnp.tile(head_two.astype(F32), 32)[None]

    pairs = shape((rows, 64), BF16)
    probability, back, ref_one, ref_two, delta_two, delta_one, errors_one, errors_two = call(
        section_xz_kernel,
        [shape((cols, 32), F32), shape((16, half, 128), BF16)] + [sections] * 4 + [pairs] * 2,
        8, [tall, tall, tall, tall], flops=1 << 31, megabytes=24,
    )(message, marks, tile_one, tile_two, band_c, band_d, band_dt, band_ct)
    back = lax.all_to_all(back, "slab", 0, 0, tiled=True)
    grads_cd = call(
        section_grads_kernel,
        shape((160, 128), BF16),
        7, [tall, tall, pltpu.VMEM((160, 128), F32)], flops=1 << 31, megabytes=16,
    )(message, ref_one, ref_two, delta_two, delta_one, errors_one, errors_two)

    delta_a, grads = call(
        backward_xy_kernel,
        [shape((1, rows, 1024), BF16), shape((16, 20, 128), BF16)],
        8,
        [wide, wide, wide, pltpu.VMEM((1, rows, 1024), BF16), pltpu.VMEM((160, 128), F32)],
        flops=1 << 31, megabytes=24,
    )(back, before, stem, after, hidden_one, hidden_two, band_bt, grads_cd)
    stem_grad = call(
        stem_grad_kernel,
        shape((cols, 1024), BF16),
        2, [wide], flops=1 << 30, megabytes=12,
    )(delta_a, band_at)
    stem_grad = jnp.transpose(stem_grad.reshape(cols, height, C), (2, 1, 0))[:, None]
    probability = jnp.transpose(probability.reshape(cols, 2, 16), (2, 1, 0))

    total = sum_everywhere(grads, "slab", "gx")
    taps = shape((3, 3, C, C), F32)
    finals = call(
        functools.partial(finish_kernel, 1.0 / (depth * height * cols)),
        [taps] * 4 + [shape((1, C), F32)] * 2,
        1, flops=1 << 20, megabytes=8,
    )(total)
    kernels = [jnp.transpose(grad, (2, 0, 1, 3)) for grad in finals[:4]]
    return (probability, stem_grad, *kernels, finals[4][0], finals[5][0])


def solution(mesh):
    return jax.shard_map(
        per_device,
        mesh=mesh,
        in_specs=(P(None, "slab", None, "gx"), P(None, "slab", "gx"), P(), P(), P(), P(), P(), P()),
        out_specs=(
            P(None, "slab", "gx"),
            P(None, "slab", None, "gx"),
            P(),
            P(),
            P(),
            P(),
            P(),
            P(),
        ),
        check_vma=False,
    )
```

time: 137 us -> 131 us (0.956)
  blocking collectives: 49.3 us -> 27.3 us
  local copies, waits for them, and re-layouts: 10.7 us -> 26.6 us
  starting transfers between devices: 23.2 us -> 32.9 us
  Pallas kernels: 28.5 us -> 20.7 us
  other arithmetic: 3.26 us -> 0.13 us
    all_to_all x1 -> x0, blocking collectives: 23.4 us -> none  [per_device(): back = lax.all_to_all(back, 'slab', 0, 0, tiled=True)]
    unnamed x23 -> x61, local copies, waits for them, and re-layouts: 3.94 us -> 24.7 us
    all_to_all x1, waiting for transfers between devices: 15.3 us -> 5.15 us  [per_device(): message = lax.all_to_all(message, 'slab', 0, 0, tiled=True)]
    all_to_all x1 -> x2, waiting for transfers between devices: 4.72 us -> 13.8 us  [the longest x1 10.2 us: per_device(): back = lax.all_to_all(back, 'slab', 0, 0, tiled=True)]
    ppermute x2 -> x4, starting transfers between devices: 6.52 us -> 12.1 us  [the longest x1 4.59 us: per_device(): before = lax.ppermute(last, 'gx', up)]
    all_to_all x1 -> x2, starting transfers between devices: 5.75 us -> 10.1 us  [the longest x1 5.6 us: sum_everywhere(): return lax.all_to_all(spread, gx, 0, 0, tiled=True)]
    pallas_call x1, Pallas kernels: 11.3 us -> 7.09 us  [per_device(): call(section_xz_kernel, [shape((cols, 32), F32), shape((16, half, 128), B...]
    pallas_call x3 -> x7, Pallas kernels: 17.3 us -> 13.6 us  [the longest x1 3.79 us: per_device(): call(forward_xy_kernel, [whole, whole, shape((16, half, 128), BF16)], 5,...]
  transfers between devices with their start and end apart: 4 -> 7, of which waited for: 2 -> 4; matrix products, arithmetic and copies ran while one was open for 5% -> 2% of each run, Pallas kernels for 3% -> 4%
where the time goes in v2:
time: 131 us; the launch traced here: 129 us
  starting transfers between devices  32.9 us (25%)
  blocking collectives  27.3 us (21%)
  local copies, waits for them, and re-layouts  26.6 us (20%)
  waiting for transfers between devices  20.9 us (16%)
  Pallas kernels  20.7 us (16%)
    unnamed x61, local copies, waits for them, and re-layouts  24.7 us
    all_to_all x1, blocking collectives, sum_everywhere(): mine = jnp.sum(lax.all_to_all(spread, slab, 0, 0, tiled=True), axis=0)  14 us
    all_to_all x1, blocking collectives, sum_everywhere(): mine = lax.all_to_all(grads, gx, 0, 0, tiled=True)  13.3 us
    all_to_all x1, starting transfers between devices, per_device(): message = lax.all_to_all(message, 'slab', 0, 0, tiled=True)  10.7 us
    all_to_all x1, waiting for transfers between devices, per_device(): back = lax.all_to_all(back, 'slab', 0, 0, tiled=True)  10.2 us
    pallas_call x1, Pallas kernels, per_device(): call(section_xz_kernel, [shape((cols, 32), F32), shape((16, half, 128), B...  7.09 us
    all_to_all x1, starting transfers between devices, sum_everywhere(): return lax.all_to_all(spread, gx, 0, 0, tiled=True)  5.6 us
    all_to_all x1, waiting for transfers between devices, per_device(): message = lax.all_to_all(message, 'slab', 0, 0, tiled=True)  5.15 us
  transfers between devices with their start and end apart: 7, of which 4 were waited for; matrix products, arithmetic and copies ran while one was open for 2% of the time, Pallas kernels for 4%

profile of v2, /device:TPU:1, one launch (start us, length us, event | category | flops | bytes accessed | tf_op | source)
XLA Modules:
  0.0 129.5 jit_solution(7388168982615521419)
XLA Ops:
  0.6 1.3 %copy.79 = bf16[32,1,32,256]{3,0,2,1:T(8,128)(2,1)S(1)} copy(bf16[32,1,32,256]{3,2,1,0:T(8,128)(2,1)} %param.8) | data formatting | bytes 1048576 | tf_op args[0]
  2.2 4.6 %collective-permute-start = (bf16[16,1024]{1,0:T(8,128)(2,1)S(1)}, bf16[16,1024]{1,0:T(8,128)(2,1)S(1)}, u32[]{:S(2)}, u32[]{:S(2)}) collective-permute-start(bf16[16,1024]{1,0:T(8,128)(2,1)S(1)} %copy.71), channel_id=1, source_target_pairs={{0,1},{1,2},{2,3},{3,4},{4,5},{5,6},{6,7},{7,8},{8,9},{9,10},{10,1... | collective-permute-start | bytes 98312 | tf_op jit(solution)/shard_map/ppermute | solution.py:414
  6.9 1.9 %collective-permute-start.1 = (bf16[16,1024]{1,0:T(8,128)(2,1)S(1)}, bf16[16,1024]{1,0:T(8,128)(2,1)S(1)}, u32[]{:S(2)}, u32[]{:S(2)}) collective-permute-start(bf16[16,1024]{1,0:T(8,128)(2,1)S(1)} %copy.72), channel_id=1, source_target_pairs={{1,0},{2,1},{3,2},{4,3},{5,4},{6,5},{7,6},{8,7},{9,8},{10,9},{11,1... | collective-permute-start | bytes 98312 | tf_op jit(solution)/shard_map/ppermute | solution.py:415
  10.2 1.9 %collective-permute-done.1.after = bf16[16,1024]{1,0:T(8,128)(2,1)S(1)} collective-permute-done((bf16[16,1024]{1,0:T(8,128)(2,1)S(1)}, bf16[16,1024]{1,0:T(8,128)(2,1)S(1)}, u32[]{:S(2)}, u32[]{:S(2)}) %collective-permute-start.1) | collective-permute-done | bytes 32800 | tf_op jit(solution)/shard_map/ppermute | solution.py:415
  12.2 3.8 %shard_map.144 = (bf16[288,1024]{1,0:T(8,128)(2,1)S(1)}, bf16[288,1024]{1,0:T(8,128)(2,1)S(1)}, bf16[16,144,128]{2,1,0:T(8,128)(2,1)}) custom-call(bf16[16,1024]{1,0:T(8,128)(2,1)S(1)} %collective-permute-done.before, bf16[256,1024]{1,0:T(8,128)(2,1)S(1)} %copy.62.stem, bf16[16,1024]{1,0:T(8,128)(2,1)S(1)} %collective-permute-done.1.after, ...), custom_call_target="tpu_custom_call" | custom-call | flops 1073741824 | bytes 1048576 | tf_op jit(solution)/shard_map/pallas_call | solution.py:429
  16.8 10.7 %all-to-all-start = ((bf16[16,144,128]{2,1,0:T(8,128)(2,1)}), bf16[16,144,128]{2,1,0:T(8,128)(2,1)S(1)}, u32[]{:S(2)}, u32[]{:S(2)}) async-start(bf16[16,144,128]{2,1,0:T(8,128)(2,1)} %get-tuple-element.46), calls=%async_computation | async-start | bytes 1179648 | tf_op jit(solution)/shard_map/all_to_all | solution.py:438
  27.7 1.9 %collective-permute-start.3 = (f32[16,32]{0,1:T(8,128)S(1)}, f32[16,32]{0,1:T(8,128)S(1)}, u32[]{:S(2)}, u32[]{:S(2)}) collective-permute-start(f32[16,32]{0,1:T(8,128)S(1)} %bitcast.52), channel_id=1, source_target_pairs={{1,0},{2,1},{3,2},{4,3},{5,4},{6,5},{7,6},{8,7},{9,8},{10,9},{11,1... | collective-permute-start | bytes 6152 | tf_op jit(solution)/shard_map/ppermute | solution.py:441
  29.6 3.6 %collective-permute-start.2 = (f32[16,32]{0,1:T(8,128)S(1)}, f32[16,32]{0,1:T(8,128)S(1)}, u32[]{:S(2)}, u32[]{:S(2)}) collective-permute-start(f32[16,32]{0,1:T(8,128)S(1)} %bitcast.51), channel_id=1, source_target_pairs={{0,1},{1,2},{2,3},{3,4},{4,5},{5,6},{6,7},{7,8},{8,9},{9,10},{10,1... | collective-permute-start | bytes 6152 | tf_op jit(solution)/shard_map/ppermute | solution.py:440
  39.7 5.1 %all-to-all-done.message = bf16[16,144,128]{2,1,0:T(8,128)(2,1)S(1)} async-done(((bf16[16,144,128]{2,1,0:T(8,128)(2,1)}), bf16[16,144,128]{2,1,0:T(8,128)(2,1)S(1)}, u32[]{:S(2)}, u32[]{:S(2)}) %all-to-all-start) | async-done | bytes 589856 | tf_op jit(solution)/shard_map/all_to_all | solution.py:438
  44.8 1.1 copy-done.9
  45.9 1.1 copy-done.11
  47.1 1.1 copy-done.13
  48.2 1.1 copy-done.15
  49.3 7.1 %shard_map.146 = (f32[256,32]{1,0:T(8,128)S(1)}, bf16[16,144,128]{2,1,0:T(8,128)(2,1)}, bf16[2,288,512]{2,1,0:T(8,128)(2,1)S(1)}, bf16[2,288,512]{2,1,0:T(8,128)...) custom-call(bf16[16,144,128]{2,1,0:T(8,128)(2,1)S(1)} %all-to-all-do, ...), custom_call_target="tpu_custom_call" | custom-call | flops 2147483648 | bytes 1048576 | tf_op jit(solution)/shard_map/pallas_call | solution.py:454
  59.7 4.5 %all-to-all-start.1 = ((bf16[16,144,128]{2,1,0:T(8,128)(2,1)}), bf16[16,144,128]{2,1,0:T(8,128)(2,1)S(1)}, u32[]{:S(2)}, u32[]{:S(2)}) async-start(bf16[16,144,128]{2,1,0:T(8,128)(2,1)} %get-tuple-element.59), calls=%async_computation.1 | async-start | bytes 1179648 | tf_op jit(solution)/shard_map/all_to_all | solution.py:459
  68.5 2.8 %shard_map.147.grads_cd = bf16[160,128]{1,0:T(8,128)(2,1)S(1)} custom-call(bf16[16,144,128]{2,1,0:T(8,128)(2,1)S(1)} %all-to-all-done.message, bf16[2,288,512]{2,1,0:T(8,128)(2,1)S(1)} %copy-done.17, bf16[2,288,512]{2,1,0:T(8,128)(2,1)S(1)} %copy-done.19, bf16[2,288,512]{2,1,0:T(8,128)(2,1)S(1)} %copy-done.21, bf16[2,288,512]{2,1,0:T(8,128)(2,1)S(1)} %copy-done.23, ...), custom_call_target="tpu_custom_call" | custom-call | flops 2147483648 | bytes 1048576 | tf_op jit(solution)/shard_map/pallas_call | solution.py:460
  71.3 10.2 %all-to-all-done.1.back = bf16[16,144,128]{2,1,0:T(8,128)(2,1)S(1)} async-done(((bf16[16,144,128]{2,1,0:T(8,128)(2,1)}), bf16[16,144,128]{2,1,0:T(8,128)(2,1)S(1)}, u32[]{:S(2)}, u32[]{:S(2)}) %all-to-all-start.1) | async-done | bytes 589856 | tf_op jit(solution)/shard_map/all_to_all | solution.py:459
  82.6 1.1 copy-done.25
  83.7 3.6 %shard_map.148 = (bf16[1,288,1024]{2,1,0:T(8,128)(2,1)S(1)}, bf16[16,20,128]{2,1,0:T(8,128)(2,1)S(1)}) custom-call(bf16[16,144,128]{2,1,0:T(8,128)(2,1)S(1)} %all-to-all-done.1.back, bf16[16,1024]{1,0:T(8,128)(2,1)S(1)} %collective-permute-done.before, bf16[256,1024]{1,0:T(8,128)(2,1)S(1)} %copy.62.stem, bf16[16,1024]{1,0:T(8,128)(2,1)S(1)} %collective-permute-done.1.after, ...), custom_call_target="tpu_custom_call" | custom-call | flops 2147483648 | bytes 1048576 | tf_op jit(solution)/shard_map/pallas_call | solution.py:466
  88.1 13.3 %all_to_all.25 = bf16[16,20,128]{2,1,0:T(8,128)(2,1)S(1)} all-to-all(bf16[16,20,128]{2,1,0:T(8,128)(2,1)S(1)} %get-tuple-element.71), channel_id=1, replica_groups=mesh['slab'=16,'gx'=16] {'gx'}, dimensions={0} | all-to-all | bytes 163840 | tf_op jit(solution)/shard_map/all_to_all | solution.py:392
  101.5 14.0 %all_to_all.26 = f32[16,20,128]{2,1,0:T(8,128)S(1)} all-to-all(f32[16,20,128]{2,1,0:T(8,128)S(1)} %broadcast_in_dim.7), channel_id=1, replica_groups=mesh['slab'=16,'gx'=16] {'slab'}, dimensions={0} | all-to-all | bytes 327680 | tf_op jit(solution)/shard_map/all_to_all | solution.py:395
  116.2 5.6 %all-to-all-start.4 = ((f32[16,20,128]{2,1,0:T(8,128)}), f32[16,20,128]{2,1,0:T(8,128)S(1)}, u32[]{:S(2)}, u32[]{:S(2)}) async-start(f32[16,20,128]{2,1,0:T(8,128)} %broadcast_in_dim.8), calls=%async_computation.4 | async-start | bytes 393216 | tf_op jit(solution)/shard_map/all_to_all | solution.py:397
  122.5 1.1 shard_map.149
  124.9 3.6 %all-to-all-done.4.total = f32[16,20,128]{2,1,0:T(8,128)S(1)} async-done(((f32[16,20,128]{2,1,0:T(8,128)}), f32[16,20,128]{2,1,0:T(8,128)S(1)}, u32[]{:S(2)}, u32[]{:S(2)}) %all-to-all-start.4) | async-done | bytes 163872 | tf_op jit(solution)/shard_map/all_to_all | solution.py:397
  (79 shorter events, 22.1 us)
Async XLA Ops:
  2.2 8.0 %collective-permute-start = (bf16[16,1024]{1,0:T(8,128)(2,1)S(1)}, bf16[16,1024]{1,0:T(8,128)(2,1)S(1)}, u32[]{:S(2)}, u32[]{:S(2)}) collective-permute-start(bf16[16,1024]{1,0:T(8,128)(2,1)S(1)} %copy.71), channel_id=1, source_target_pairs={{0,1},{1,2},{2,3},{3,4},{4,5},{5,6},{6,7},{7,8},{8,9},{9,10},{10,1... | collective-permute-start | bytes 98312 | tf_op jit(solution)/shard_map/ppermute | solution.py:414
  6.9 5.2 %collective-permute-start.1 = (bf16[16,1024]{1,0:T(8,128)(2,1)S(1)}, bf16[16,1024]{1,0:T(8,128)(2,1)S(1)}, u32[]{:S(2)}, u32[]{:S(2)}) collective-permute-start(bf16[16,1024]{1,0:T(8,128)(2,1)S(1)} %copy.72), channel_id=1, source_target_pairs={{1,0},{2,1},{3,2},{4,3},{5,4},{6,5},{7,6},{8,7},{9,8},{10,9},{11,1... | collective-permute-start | bytes 98312 | tf_op jit(solution)/shard_map/ppermute | solution.py:415
  8.9 0.9 copy-start.1
  16.0 11.6 %copy-start.26 = (s32[16,2,256]{2,1,0:T(2,128)S(1)}, s32[16,2,256]{2,1,0:T(2,128)}, u32[]{:S(2)}) copy-start(s32[16,2,256]{2,1,0:T(2,128)} %param.9) | copy-start | bytes 98308
  16.8 28.0 %all-to-all-start = ((bf16[16,144,128]{2,1,0:T(8,128)(2,1)}), bf16[16,144,128]{2,1,0:T(8,128)(2,1)S(1)}, u32[]{:S(2)}, u32[]{:S(2)}) async-start(bf16[16,144,128]{2,1,0:T(8,128)(2,1)} %get-tuple-element.46), calls=%async_computation | async-start | bytes 1179648 | tf_op jit(solution)/shard_map/all_to_all | solution.py:438
  27.6 5.7 %copy-start.2 = (bf16[32,3,3,32]{3,0,2,1:T(8,128)(2,1)S(1)}, bf16[32,3,3,32]{3,0,2,1:T(8,128)(2,1)}, u32[]{:S(2)}) copy-start(bf16[32,3,3,32]{3,0,2,1:T(8,128)(2,1)} %param.12) | copy-start | bytes 55300
  27.6 5.7 %copy-start.3 = (bf16[32,3,3,32]{3,0,2,1:T(8,128)(2,1)S(1)}, bf16[32,3,3,32]{3,0,2,1:T(8,128)(2,1)}, u32[]{:S(2)}) copy-start(bf16[32,3,3,32]{3,0,2,1:T(8,128)(2,1)} %param.13) | copy-start | bytes 55300
  27.7 11.8 %collective-permute-start.3 = (f32[16,32]{0,1:T(8,128)S(1)}, f32[16,32]{0,1:T(8,128)S(1)}, u32[]{:S(2)}, u32[]{:S(2)}) collective-permute-start(f32[16,32]{0,1:T(8,128)S(1)} %bitcast.52), channel_id=1, source_target_pairs={{1,0},{2,1},{3,2},{4,3},{5,4},{6,5},{7,6},{8,7},{9,8},{10,9},{11,1... | collective-permute-start | bytes 6152 | tf_op jit(solution)/shard_map/ppermute | solution.py:441
  29.6 9.1 %copy-start.27 = (bf16[32]{0:T(256)(128)(2,1)S(1)}, bf16[32]{0:T(256)(128)(2,1)}, u32[]{:S(2)}) copy-start(bf16[32]{0:T(256)(128)(2,1)} %param.14) | copy-start | bytes 196
  29.6 9.9 %collective-permute-start.2 = (f32[16,32]{0,1:T(8,128)S(1)}, f32[16,32]{0,1:T(8,128)S(1)}, u32[]{:S(2)}, u32[]{:S(2)}) collective-permute-start(f32[16,32]{0,1:T(8,128)S(1)} %bitcast.51), channel_id=1, source_target_pairs={{0,1},{1,2},{2,3},{3,4},{4,5},{5,6},{6,7},{7,8},{8,9},{9,10},{10,1... | collective-permute-start | bytes 6152 | tf_op jit(solution)/shard_map/ppermute | solution.py:440
  37.8 0.9 copy-start.24
  44.8 1.1 copy-start.9
  45.9 1.1 copy-start.11
  47.1 1.1 copy-start.13
  48.2 1.1 copy-start.15
  59.7 21.8 %all-to-all-start.1 = ((bf16[16,144,128]{2,1,0:T(8,128)(2,1)}), bf16[16,144,128]{2,1,0:T(8,128)(2,1)S(1)}, u32[]{:S(2)}, u32[]{:S(2)}) async-start(bf16[16,144,128]{2,1,0:T(8,128)(2,1)} %get-tuple-element.59), calls=%async_computation.1 | async-start | bytes 1179648 | tf_op jit(solution)/shard_map/all_to_all | solution.py:459
  64.2 1.1 copy-start.17
  65.3 1.1 copy-start.19
  66.4 1.1 copy-start.21
  67.4 1.1 copy-start.23
  81.5 1.1 copy-start.5
  82.6 1.1 copy-start.25
  115.5 7.0 %copy-start.7 = (bf16[1,288,1024]{2,1,0:T(8,128)(2,1)S(1)}, bf16[1,288,1024]{2,1,0:T(8,128)(2,1)}, u32[]{:S(2)}) copy-start(bf16[1,288,1024]{2,1,0:T(8,128)(2,1)} %copy-done.6) | copy-start | bytes 1769476
  116.2 12.3 %all-to-all-start.4 = ((f32[16,20,128]{2,1,0:T(8,128)}), f32[16,20,128]{2,1,0:T(8,128)S(1)}, u32[]{:S(2)}, u32[]{:S(2)}) async-start(f32[16,20,128]{2,1,0:T(8,128)} %broadcast_in_dim.8), calls=%async_computation.4 | async-start | bytes 393216 | tf_op jit(solution)/shard_map/all_to_all | solution.py:397
  (12 other events, 10.0 us)

commit v3 on v2

v3 whole, which is shorter than its diff:
```python
import functools

import jax
import jax.numpy as jnp
from jax import lax
from jax.experimental import pallas as pl
from jax.experimental.pallas import tpu as pltpu
from jax.sharding import PartitionSpec as P

HALO = 32
LEFT = 16
C = 32
F32 = jnp.float32
BF16 = jnp.bfloat16
VMEM = pl.BlockSpec(memory_space=pltpu.VMEM)
HBM = pl.BlockSpec(memory_space=pltpu.HBM)
CONTRACT_ROWS = (((0,), (0,)), ((), ()))
CONTRACT_LANES = (((1,), (1,)), ((), ()))


def softplus(v):
    small = jnp.exp(-jnp.abs(v))
    tail = jnp.where(small < 1e-4, small, jnp.log(1.0 + small))
    return jnp.maximum(v, 0.0) + tail


def slope(stored):
    return 1.0 - jnp.exp(-stored.astype(F32))


def edge_gates():
    me, peers = lax.axis_index("gx"), lax.axis_size("gx")
    return jnp.where(me > 0, 0.0, 1.0), jnp.where(me < peers - 1, 1.0, 0.0)


def gated(value, inside):
    cols = value.shape[0] - HALO
    return jnp.concatenate([value[:cols], value[cols:] * inside], axis=0)


def clear_margins(shifted):
    lanes = shifted.shape[-1]
    edge = jnp.zeros(shifted.shape[:-1] + (128,), BF16)
    shifted[..., 0:128] = edge
    shifted[..., lanes - 128 : lanes] = edge


def store_shifted(shifted, plane, start, value, step):
    rows, lanes = value.shape
    where = slice(128 + start, 128 + start + lanes)
    shifted[plane, 1, :, where] = value.astype(BF16)
    lower = pltpu.roll(value, step, 0)
    row = lax.broadcasted_iota(jnp.int32, (8, lanes), 0)
    lower = jnp.concatenate([jnp.where(row < step, 0.0, lower[:8]), lower[8:]], axis=0)
    shifted[plane, 0, :, where] = lower.astype(BF16)
    shifted[plane, 2, :, where] = pltpu.roll(value, rows - step, 0).astype(BF16)


def conv_window(shifted, plane, window, band):
    lanes = slice(256 * window, 256 * window + 512)
    total = None
    for tap in range(3):
        term = jnp.dot(
            shifted[plane, tap, :, lanes],
            band[512 * tap : 512 * tap + 512, :],
            preferred_element_type=F32,
        )
        total = term if total is None else total + term
    return total


def windows_of(shifted):
    planes = shifted.shape[0]
    windows = (shifted.shape[-1] - 256) // 256
    return [(plane, window) for plane in range(planes) for window in range(windows)]


def weight_grad(delta, shifted, step, grads, first_piece, first):
    own = slice(LEFT, delta.shape[1] - LEFT)
    places = windows_of(shifted)
    head = jnp.concatenate(
        [delta[plane, :LEFT, 256 * window : 256 * window + 256] for plane, window in places], axis=0
    )
    head = (head.astype(F32) * first).astype(BF16)
    for tap in range(3):
        total = lax.dot_general(
            head,
            jnp.concatenate(
                [
                    shifted[plane, tap, :LEFT, 256 * window : 256 * window + 512]
                    for plane, window in places
                ],
                axis=0,
            ),
            CONTRACT_ROWS,
            preferred_element_type=F32,
        )
        for plane, window in places:
            total = total + lax.dot_general(
                delta[plane, own, 256 * window : 256 * window + 256],
                shifted[plane, tap, own, 256 * window : 256 * window + 512],
                CONTRACT_ROWS,
                preferred_element_type=F32,
            )
        folded = None
        for r in range(4):
            near = total[32 * r : 32 * r + 32, 0:384]
            far = total[32 * r + 128 : 32 * r + 160, 128:512]
            part = near + far
            if r:
                part = pltpu.roll(part, 384 - 32 * r, 1)
            folded = part if folded is None else folded + part
        for row_tap in range(3):
            at = 32 * (4 + step * (row_tap - 1))
            put_piece(grads, first_piece + 3 * row_tap + tap, folded[:, at : at + 32])


def put_piece(grads, index, value):
    row, lane = 32 * (index // 4), 32 * (index % 4)
    grads[row : row + value.shape[0], lane : lane + 32] = value


def fill_tap(weight, band, step, backward, col_tap):
    lane = lax.broadcasted_iota(jnp.int32, (32, 128), 1) // 32
    cut = []
    for row_tap in range(3):
        if backward:
            block = weight[2 - row_tap, 2 - col_tap].astype(F32)
        else:
            block = weight[row_tap, col_tap].astype(F32).T
        block = jnp.concatenate([block] * 4, axis=1)
        cut.append([jnp.where(lane == q, block, 0.0) for q in range(4)])
    for source in range(16):
        for group in range(2):
            panel = None
            for q in range(4):
                off = source - 4 - (4 * group + q)
                if off % step == 0 and abs(off) <= step:
                    term = cut[off // step + 1][q]
                    panel = term if panel is None else panel + term
            if panel is None:
                panel = jnp.zeros((32, 128), F32)
            row = 512 * col_tap + 32 * source
            band[row : row + 32, 128 * group : 128 * group + 128] = panel.astype(BF16)


def fill_band(weight, band, step, backward):
    for col_tap in range(3):
        fill_tap(weight, band, step, backward, col_tap)


class Copies:
    def __init__(self, sems):
        self.sems, self.started = sems, []

    def start(self, source, target):
        copy = pltpu.make_async_copy(source, target, self.sems.at[len(self.started)])
        copy.start()
        self.started.append(copy)
        return copy

    def start_lanes(self, source, target, parts):
        size = source.shape[-1] // parts
        return [
            self.start(
                source.at[..., pl.ds(size * k, size)], target.at[..., pl.ds(size * k, size)]
            )
            for k in range(parts)
        ]


def wait_all(copies):
    for copy in copies:
        copy.wait()


def centre(shifted):
    return shifted.at[:, 1, :, pl.ds(128, shifted.shape[-1] - 256)]


def arrange_kernel(stem_in, labels_in, stem_out, marks_out, initial, flat, stem, labels, sems):
    cols = stem.shape[2]
    copies = Copies(sems)
    for k in range(4):
        rows = pl.ds(8 * k, 8)
        copies.start(stem_in.at[rows], stem.at[rows])
    labels_here = copies.start(labels_in, labels)
    wait_all(copies.started[:4])
    for side in range(cols // 128):
        part = stem[:, :, 128 * side : 128 * side + 128].reshape(1024, 128)
        flat[1024 * side : 1024 * side + 1024, :] = part.astype(F32)
    for group in range(8):
        sides = []
        for side in range(cols // 128):
            first = 1024 * side + 4 * group
            rows = [flat[pl.ds(first + k, 32, stride=32), :] for k in range(4)]
            sides.append(jnp.concatenate(rows, axis=0).T)
        lanes = slice(128 * group, 128 * group + 128)
        value = jnp.concatenate(sides, axis=0).astype(BF16)
        stem_out[:, lanes] = value
        initial[:, lanes] = value[:HALO]
    labels_here.wait()
    marks = labels[...].astype(F32)
    marks = jnp.concatenate([marks[:, 0, :], marks[:, 1, :], jnp.zeros((96, cols), F32)], axis=0)
    marks = marks.T.astype(BF16)
    marks_out[...] = marks
    initial[:, 1024:1152] = marks[:HALO]


def own_voxel():
    voxel = lax.broadcasted_iota(jnp.int32, (32, 1024), 0)
    return voxel == lax.broadcasted_iota(jnp.int32, (32, 1024), 1) // 32


def first_bands_kernel(conv_a, conv_b, head_one, head_two, band_a, band_b, spread_out, spread, sems):
    same = own_voxel()
    for k, head in enumerate((head_one, head_two)):
        four = jnp.concatenate([head[...].astype(F32)] * 4, axis=1)
        along = jnp.concatenate([four] * 8, axis=1)
        spread[32 * k : 32 * k + 32, :] = jnp.where(same, along, 0.0).astype(BF16)
    copies = Copies(sems)
    copies.start(spread, spread_out)
    fill_band(conv_a, band_a, 1, False)
    fill_band(conv_b, band_b, 2, False)
    wait_all(copies.started)


def forward_xy_kernel(
    stem, marks, after, band_a, band_b,
    stem_frame, hidden_one, hidden_two, marks_out, message,
    stem_s, one_s, two, packed, sems,
):
    _, inside = edge_gates()
    copies = Copies(sems)
    clear_margins(stem_s)
    clear_margins(one_s)
    for window in range(4):
        lanes = slice(256 * window, 256 * window + 256)
        value = jnp.concatenate([stem[:, lanes], after[:, lanes]], axis=0)
        store_shifted(stem_s, 0, 256 * window, value.astype(F32), 1)
    copies.start(centre(stem_s), stem_frame)
    marks_out[...] = jnp.concatenate([marks[...], after[:, 1024:1152]], axis=0)
    for window in range(4):
        value = gated(softplus(conv_window(stem_s, 0, window, band_a)), inside)
        store_shifted(one_s, 0, 256 * window, value, 2)
    copies.start(centre(one_s), hidden_one)
    for window in range(4):
        value = gated(softplus(conv_window(one_s, 0, window, band_b)), inside).astype(BF16)
        lanes = pl.ds(256 * window, 256)
        two[0, :, lanes] = value
        copies.start(two.at[:, :, lanes], hidden_two.at[:, :, lanes])
        half = value.shape[0] // 2
        for peer in range(4):
            lanes = slice(64 * peer, 64 * peer + 64)
            packed[4 * window + peer] = jnp.concatenate(
                [value[:half, lanes], value[half:, lanes]], axis=1
            )
        peers = pl.ds(4 * window, 4)
        copies.start(packed.at[peers], message.at[peers])
    wait_all(copies.started)


def load_features(message, two_s):
    for plane in range(2):
        for group in range(4):
            parts = []
            for side in range(2):
                at = 64 * side + 32 * plane
                parts.append(
                    jnp.concatenate(
                        [message[4 * group + q][:, at : at + 32] for q in range(4)], axis=1
                    )
                )
            value = jnp.concatenate(parts, axis=0).astype(F32)
            store_shifted(two_s, plane, 128 * group, value, 1)


def split(error):
    high = error.astype(BF16)
    low = (error - high.astype(F32)).astype(BF16)
    return jnp.concatenate([high, low], axis=1)


def section_xz_kernel(
    message, marks, conv_c, conv_d, spread_in,
    probability, errors_one, errors_two, back, ref_one_out, ref_two_out, delta_two_out, delta_one_out,
    two_s, ref_one_s, delta_two_s, delta_one_s, ref_two, packed, bands, spread, sems,
):
    _, inside = edge_gates()
    copies = Copies(sems)
    spread_here = copies.start(spread_in, spread)
    band_c, band_d, band_dt, band_ct = [bands.at[k] for k in range(4)]
    rows = marks.shape[0]
    half = rows // 2
    for shifted in (two_s, ref_one_s, delta_two_s, delta_one_s):
        clear_margins(shifted)
    places = windows_of(two_s)
    fill_band(conv_c, band_c, 1, False)
    load_features(message, two_s)
    for plane, window in places:
        value = gated(softplus(conv_window(two_s, plane, window, band_c)), inside)
        store_shifted(ref_one_s, plane, 256 * window, value, 2)
    copies.start(centre(ref_one_s), ref_one_out)
    fill_band(conv_d, band_d, 2, False)
    for plane, window in places:
        value = softplus(conv_window(ref_one_s, plane, window, band_d))
        ref_two[plane, :, 256 * window : 256 * window + 256] = value.astype(BF16)
    copies.start(ref_two, ref_two_out)
    fill_band(conv_d, band_dt, 2, True)

    labels = marks[:, 0:32].astype(F32)
    spread_here.wait()
    spread_one, spread_two = spread[0:32, :], spread[32:64, :]
    first, second = None, None
    for plane in range(2):
        lanes = slice(512 * plane, 512 * plane + 512)
        one = lax.dot_general(
            two_s[plane, 1, :, 128:640], spread_one[:, lanes], CONTRACT_LANES,
            preferred_element_type=F32,
        )
        two = lax.dot_general(
            ref_two[plane], spread_two[:, lanes], CONTRACT_LANES, preferred_element_type=F32
        )
        first = one if first is None else first + one
        second = two if second is None else second + two
    first = first.astype(BF16).astype(F32)
    second = second + first
    share = 1.0 / (1.0 + jnp.exp(-second))
    probability[...] = share[: rows - LEFT]
    error_two = gated(share - labels, inside)
    error_one = 1.0 / (1.0 + jnp.exp(-first)) - labels + error_two
    error_two = split(error_two)
    error_one = split(error_one)
    errors_one[...] = error_one
    errors_two[...] = error_two
    spread_one = jnp.concatenate([spread_one, spread_one], axis=0)
    spread_two = jnp.concatenate([spread_two, spread_two], axis=0)

    for plane, window in places:
        at = 256 * window
        lanes = slice(512 * plane + at, 512 * plane + at + 256)
        value = jnp.dot(error_two, spread_two[:, lanes], preferred_element_type=F32)
        value = value * slope(ref_two[plane, :, at : at + 256])
        store_shifted(delta_two_s, plane, at, value, 2)
    copies.start(centre(delta_two_s), delta_two_out)
    fill_band(conv_c, band_ct, 1, True)
    for plane, window in places:
        at = 256 * window
        value = conv_window(delta_two_s, plane, window, band_dt)
        stored = ref_one_s[plane, 1, :, 128 + at : 384 + at]
        value = gated(value * slope(stored), inside)
        store_shifted(delta_one_s, plane, at, value, 1)
    copies.start(centre(delta_one_s), delta_one_out)
    for window in range(2):
        values = []
        for plane in range(2):
            at = 256 * window
            lanes = slice(512 * plane + at, 512 * plane + at + 256)
            value = conv_window(delta_one_s, plane, window, band_ct)
            value = value + jnp.dot(error_one, spread_one[:, lanes], preferred_element_type=F32)
            values.append(value.astype(BF16))
        for z in range(8):
            lanes = slice(32 * z, 32 * z + 32)
            packed[8 * window + z] = jnp.concatenate(
                [
                    values[0][:half, lanes], values[1][:half, lanes],
                    values[0][half:, lanes], values[1][half:, lanes],
                ],
                axis=1,
            )
        for part in range(2):
            peers = pl.ds(8 * window + 4 * part, 4)
            copies.start(packed.at[peers], back.at[peers])
    wait_all(copies.started[1:])


def section_grads_kernel(message, errors_one, errors_two, *refs):
    sources, grads_out = refs[:4], refs[4]
    two_s, ref_one_s, grads, ref_one, ref_two, delta_two, delta_one, sems = refs[5:]
    first, _ = edge_gates()
    copies = Copies(sems)
    for source, target in zip(sources, (ref_one, ref_two, delta_two, delta_one)):
        copies.start(source, target)
    rows = errors_one.shape[0]
    own = slice(0, rows - LEFT)
    same = own_voxel()
    same = jnp.concatenate([same, same], axis=0)
    clear_margins(two_s)
    clear_margins(ref_one_s)
    load_features(message, two_s)
    wait_all(copies.started)
    for plane, window in windows_of(two_s):
        at = 256 * window
        value = ref_one[plane, :, at : at + 256].astype(F32)
        store_shifted(ref_one_s, plane, at, value, 2)

    def head_grad(errors, planes):
        error = errors[own, :].astype(F32)
        error = jnp.concatenate([error[:LEFT] * first, error[LEFT:]], axis=0).astype(BF16)
        total = None
        for plane, feature in enumerate(planes):
            full = lax.dot_general(error, feature, CONTRACT_ROWS, preferred_element_type=F32)
            kept = jnp.where(same[:, 512 * plane : 512 * plane + 512], full, 0.0)
            kept = jnp.sum(kept, axis=0, keepdims=True)
            kept = kept[:, 0:128] + kept[:, 128:256] + kept[:, 256:384] + kept[:, 384:512]
            total = kept if total is None else total + kept
        total = total + pltpu.roll(total, 64, 1)
        total = total + pltpu.roll(total, 32, 1)
        return total[:, 0:32]

    grads[...] = jnp.zeros(grads.shape, F32)
    features = [two_s[plane, 1, own, 128:640] for plane in range(2)]
    put_piece(grads, 18, head_grad(errors_one, features))
    put_piece(grads, 19, head_grad(errors_two, [ref_two[plane, own, :] for plane in range(2)]))
    weight_grad(delta_two, ref_one_s, 2, grads, 9, first)
    weight_grad(delta_one, two_s, 1, grads, 0, first)
    grads_out[...] = grads[...].astype(BF16)


def backward_xy_kernel(
    back, grads_cd, conv_b, hidden_two_in, hidden_one_in, stem_in,
    grads_out, delta_a_out,
    stem_s, one_s, delta_b_s, delta_b, delta_a, grads, hidden_two, band_bt, hidden_one, stem, sems,
):
    first, inside = edge_gates()
    copies = Copies(sems)
    two_here = copies.start_lanes(hidden_two_in, hidden_two, 4)
    one_here = copies.start_lanes(hidden_one_in, hidden_one, 4)
    stem_here = copies.start_lanes(stem_in, stem, 4)
    for shifted in (stem_s, one_s, delta_b_s):
        clear_margins(shifted)
    fill_band(conv_b, band_bt, 2, True)
    for group in range(8):
        parts = []
        for side in range(2):
            at = 64 * side
            parts.append(
                jnp.concatenate(
                    [back[2 * group + q][:, at : at + 64] for q in range(2)], axis=1
                )
            )
        lanes = slice(128 * group, 128 * group + 128)
        value = jnp.concatenate(parts, axis=0).astype(F32)
        if group % 2 == 0:
            two_here[group // 2].wait()
        value = gated(value * slope(hidden_two[0, :, lanes]), inside)
        delta_b[0, :, lanes] = value.astype(BF16)
        store_shifted(delta_b_s, 0, 128 * group, value, 2)
    wait_all(one_here)
    for window in range(4):
        at = 256 * window
        value = conv_window(delta_b_s, 0, window, band_bt)
        stored = hidden_one[0, :, at : at + 256]
        value = gated(value * slope(stored), inside)
        delta_a[0, :, at : at + 256] = value.astype(BF16)
        store_shifted(one_s, 0, at, stored.astype(F32), 2)
    leaving = copies.start(delta_a, delta_a_out)
    wait_all(stem_here)
    for window in range(4):
        lanes = slice(256 * window, 256 * window + 256)
        store_shifted(stem_s, 0, 256 * window, stem[0, :, lanes].astype(F32), 1)
    grads[...] = jnp.zeros(grads.shape, F32)
    weight_grad(delta_b, one_s, 2, grads, 9, first)
    weight_grad(delta_a, stem_s, 1, grads, 0, first)
    for peer in range(8):
        grads_out[peer] = grads[20 * peer : 20 * peer + 20, :].astype(BF16)
        grads_out[8 + peer] = grads_cd[20 * peer : 20 * peer + 20, :]
    leaving.wait()


def stem_grad_kernel(delta_a_in, conv_a, stem_grad, delta_a_s, delta_a, band_at, sems):
    copies = Copies(sems)
    copies.start(delta_a_in, delta_a)
    rows = delta_a.shape[1]
    clear_margins(delta_a_s)
    fill_band(conv_a, band_at, 1, True)
    wait_all(copies.started)
    for window in range(4):
        lanes = slice(256 * window, 256 * window + 256)
        store_shifted(delta_a_s, 0, 256 * window, delta_a[0, :, lanes].astype(F32), 1)
    for window in range(4):
        at = 256 * window
        value = conv_window(delta_a_s, 0, window, band_at)
        stem_grad[:, at : at + 256] = value[: rows - LEFT].astype(BF16)


def finish_kernel(factor, total, grad_a, grad_b, grad_c, grad_d, head_one, head_two):
    flat = total[...].reshape(320, 128) * factor

    def piece(pair, index):
        row, lane = 160 * pair + 32 * (index // 4), 32 * (index % 4)
        return flat[row : row + 32, lane : lane + 32]

    for pair, (near, far) in enumerate(((grad_a, grad_b), (grad_c, grad_d))):
        for tap in range(9):
            near[tap // 3, tap % 3] = piece(pair, tap)
            far[tap // 3, tap % 3] = piece(pair, 9 + tap)
    head_one[...] = piece(1, 18)[0:1]
    head_two[...] = piece(1, 19)[0:1]


def call(kernel, outs, ins, scratch=(), flops=0, megabytes=16):
    places = [place for _, place in outs]
    shapes = [pltpu.HBM(out.shape, out.dtype) if place is HBM else out for out, place in outs]

    def run(*operands):
        operands = [
            pltpu.with_memory_space_constraint(operand, pltpu.HBM) if place is HBM else operand
            for operand, place in zip(operands, ins)
        ]
        return bound(*operands)

    bound = pl.pallas_call(
        kernel,
        out_shape=shapes,
        in_specs=ins,
        out_specs=list(places),
        scratch_shapes=scratch,
        compiler_params=pltpu.CompilerParams(vmem_limit_bytes=megabytes * 1024 * 1024),
        cost_estimate=pl.CostEstimate(flops=flops, bytes_accessed=1 << 20, transcendentals=0),
    )
    return run


def shape(dims, dtype):
    return jax.ShapeDtypeStruct(dims, dtype)


def sum_everywhere(grads, beside, slab, gx):
    peers, copies = lax.axis_size(gx), lax.axis_size(slab)
    mine = lax.all_to_all(grads, gx, 0, 0, tiled=True)
    mine, beside = lax.optimization_barrier((mine, beside))
    mine = jnp.sum(mine.astype(F32), axis=0)
    spread = jnp.broadcast_to(mine[None], (copies,) + mine.shape)
    mine = jnp.sum(lax.all_to_all(spread, slab, 0, 0, tiled=True), axis=0)
    spread = jnp.broadcast_to(mine[None], (peers,) + mine.shape)
    return lax.all_to_all(spread, gx, 0, 0, tiled=True), beside


def per_device(stem_features, labels, conv_a, conv_b, conv_c, conv_d, head_one, head_two):
    _, depth, height, cols = stem_features.shape
    rows = cols + HALO
    half = rows // 2
    peers = lax.axis_size("gx")
    up = [(i, i + 1) for i in range(peers - 1)]
    down = [(j, i) for i, j in up]
    sems = lambda count: pltpu.SemaphoreType.DMA((count,))
    vmem = lambda kind: pltpu.VMEM(kind.shape, kind.dtype)

    stem_features = stem_features[:, 0]
    stem, marks, initial = call(
        arrange_kernel,
        [
            (shape((cols, 1024), BF16), VMEM),
            (shape((cols, 128), BF16), VMEM),
            (shape((HALO, 1152), BF16), VMEM),
        ],
        [HBM, HBM],
        [pltpu.VMEM((1024 * cols // 128, 128), F32), vmem(stem_features), vmem(labels), sems(5)],
        flops=1 << 28, megabytes=6,
    )(stem_features, labels)
    after = lax.ppermute(initial, "gx", down)

    taps_a, taps_b, taps_c, taps_d = [
        jnp.transpose(w, (1, 2, 0, 3)) for w in (conv_a, conv_b, conv_c, conv_d)
    ]
    band = shape((1536, 256), BF16)
    spreads = shape((64, 1024), BF16)
    band_a, band_b, spread = call(
        first_bands_kernel, [(band, VMEM)] * 2 + [(spreads, HBM)], [VMEM] * 4,
        [vmem(spreads), sems(1)], flops=1 << 29, megabytes=3,
    )(taps_a, taps_b, head_one[None], head_two[None])

    wide = pltpu.VMEM((1, 3, rows, 1280), BF16)
    tall = pltpu.VMEM((2, 3, rows, 768), BF16)
    whole = shape((1, rows, 1024), BF16)
    planes = shape((2, rows, 512), BF16)
    messages = shape((16, half, 128), BF16)
    stem, hidden_one, hidden_two, marks, message = call(
        forward_xy_kernel,
        [(whole, HBM)] * 3 + [(shape((rows, 128), BF16), VMEM), (messages, HBM)],
        [VMEM] * 5,
        [wide, wide, vmem(whole), vmem(messages), sems(10)], flops=1 << 30, megabytes=8,
    )(stem, marks, after, band_a, band_b)
    message = lax.all_to_all(message, "slab", 0, 0, tiled=True)

    pairs = shape((rows, 64), BF16)
    probability, errors_one, errors_two, back, *held = call(
        section_xz_kernel,
        [(shape((rows - LEFT, 32), F32), VMEM), (pairs, VMEM), (pairs, VMEM), (messages, HBM)]
        + [(planes, HBM)] * 4,
        [VMEM] * 4 + [HBM],
        [tall, tall, tall, tall, vmem(planes), vmem(messages), pltpu.VMEM((4, 1536, 256), BF16)]
        + [vmem(spreads), sems(9)],
        flops=1 << 31, megabytes=18,
    )(message, marks, taps_c, taps_d, spread)
    back = lax.all_to_all(back, "slab", 0, 0, tiled=True)
    (grads_cd,) = call(
        section_grads_kernel,
        [(shape((160, 128), BF16), VMEM)],
        [VMEM] * 3 + [HBM] * 4,
        [tall, tall, pltpu.VMEM((160, 128), F32)] + [vmem(planes)] * 4 + [sems(4)],
        flops=1 << 31, megabytes=12,
    )(message, errors_one, errors_two, *held)

    grads, delta_a = call(
        backward_xy_kernel,
        [(shape((16, 20, 128), BF16), VMEM), (whole, HBM)],
        [VMEM] * 3 + [HBM] * 3,
        [wide, wide, wide, vmem(whole), vmem(whole), pltpu.VMEM((160, 128), F32)]
        + [vmem(whole), vmem(band), vmem(whole), vmem(whole), sems(13)],
        flops=1 << 31, megabytes=15,
    )(back, grads_cd, taps_b, hidden_two, hidden_one, stem)
    (stem_grad,) = call(
        stem_grad_kernel,
        [(shape((rows - LEFT, 1024), BF16), VMEM)],
        [HBM, VMEM], [wide, vmem(whole), vmem(band), sems(1)], flops=1 << 30, megabytes=6,
    )(delta_a, taps_a)

    total, stem_grad = sum_everywhere(grads, stem_grad, "slab", "gx")

    def in_place(found):
        moved = lax.ppermute(found[cols:], "gx", up)
        moved = jnp.where(lax.axis_index("gx") > 0, moved, found[:LEFT])
        return jnp.concatenate([moved, found[LEFT:cols]], axis=0)

    stem_grad = in_place(stem_grad).reshape(cols, height, C)
    stem_grad = jnp.transpose(stem_grad, (2, 1, 0))[:, None]
    probability = in_place(probability).reshape(cols, 2, 16)
    probability = jnp.transpose(probability, (2, 1, 0))

    taps = shape((3, 3, C, C), F32)
    finals = call(
        functools.partial(finish_kernel, 1.0 / (depth * height * cols)),
        [(taps, VMEM)] * 4 + [(shape((1, C), F32), VMEM)] * 2,
        [VMEM], flops=1 << 20, megabytes=2,
    )(total)
    kernels = [jnp.transpose(grad, (2, 0, 1, 3)) for grad in finals[:4]]
    return (probability, stem_grad, *kernels, finals[4][0], finals[5][0])


def solution(mesh):
    return jax.shard_map(
        per_device,
        mesh=mesh,
        in_specs=(P(None, "slab", None, "gx"), P(None, "slab", "gx"), P(), P(), P(), P(), P(), P()),
        out_specs=(
            P(None, "slab", "gx"),
            P(None, "slab", None, "gx"),
            P(),
            P(),
            P(),
            P(),
            P(),
            P(),
        ),
        check_vma=False,
    )
```

time: 131 us -> 122 us (0.931)
  local copies, waits for them, and re-layouts: 26.6 us -> 4.16 us
  Pallas kernels: 20.7 us -> 29 us
  waiting for transfers between devices: 20.9 us -> 24.2 us
  blocking collectives: 27.3 us -> 30.5 us
    unnamed x61 -> x14, local copies, waits for them, and re-layouts: 24.7 us -> 2.39 us
    pallas_call x8, Pallas kernels: 20.7 us -> 29 us  [run(): return bound(*operands)]
    all_to_all x2 -> x3, waiting for transfers between devices: 8.76 us -> 14.4 us  [the longest x1 5.38 us: sum_everywhere(): return (lax.all_to_all(spread, gx, 0, 0, tiled=True), beside)]
    ppermute x3 -> x2, starting transfers between devices: 10.1 us -> 6.28 us  [in_place(): moved = lax.ppermute(found[cols:], 'gx', up)]
    ppermute x1, starting transfers between devices: 1.92 us -> 5.15 us  [per_device(): after = lax.ppermute(initial, 'gx', down)]
    all_to_all x2 -> x1, blocking collectives: 27.3 us -> 30.5 us  [per_device(): message = lax.all_to_all(message, 'slab', 0, 0, tiled=True)]
    ppermute x1, waiting for transfers between devices: 1.95 us -> 0.01 us  [per_device(): after = lax.ppermute(initial, 'gx', down)]
    all_to_all x2 -> x3, starting transfers between devices: 16.3 us -> 17.2 us  [the longest x1 6.2 us: sum_everywhere(): mine = lax.all_to_all(grads, gx, 0, 0, tiled=True)]
  transfers between devices with their start and end apart: 7 -> 7, of which waited for: 4 -> 4; matrix products, arithmetic and copies ran while one was open for 2% -> 3% of each run, Pallas kernels for 4% -> 11%
where the time goes in v3:
time: 122 us; the launch traced here: 121 us
  starting transfers between devices  32.3 us (26%)
  blocking collectives  30.5 us (25%)
  Pallas kernels  29 us (24%)
  waiting for transfers between devices  24.2 us (20%)
  local copies, waits for them, and re-layouts  4.16 us (3%)
    all_to_all x1, blocking collectives, per_device(): message = lax.all_to_all(message, 'slab', 0, 0, tiled=True)  30.5 us
    pallas_call x8, Pallas kernels, run(): return bound(*operands)  29 us
    all_to_all x1, waiting for transfers between devices, per_device(): back = lax.all_to_all(back, 'slab', 0, 0, tiled=True)  9.79 us
    ppermute x2, starting transfers between devices, in_place(): moved = lax.ppermute(found[cols:], 'gx', up)  6.28 us
    all_to_all x1, starting transfers between devices, sum_everywhere(): mine = lax.all_to_all(grads, gx, 0, 0, tiled=True)  6.2 us
    all_to_all x1, starting transfers between devices, sum_everywhere(): return (lax.all_to_all(spread, gx, 0, 0, tiled=True), beside)  5.6 us
    all_to_all x1, starting transfers between devices, sum_everywhere(): mine = jnp.sum(lax.all_to_all(spread, slab, 0, 0, tiled=True), axis=0)  5.44 us
    all_to_all x1, waiting for transfers between devices, sum_everywhere(): return (lax.all_to_all(spread, gx, 0, 0, tiled=True), beside)  5.38 us
  transfers between devices with their start and end apart: 7, of which 4 were waited for; matrix products, arithmetic and copies ran while one was open for 3% of the time, Pallas kernels for 11%

profile of v3, /device:TPU:1, one launch (start us, length us, event | category | flops | bytes accessed | tf_op | source)
XLA Modules:
  0.0 121.1 jit_solution(6728748535252723518)
XLA Ops:
  0.7 2.1 %shard_map.143 = (bf16[256,1024]{1,0:T(8,128)(2,1)S(1)}, bf16[256,128]{1,0:T(8,128)(2,1)S(1)}, bf16[32,1152]{1,0:T(8,128)(2,1)S(1)}) custom-call(bf16[32,32,256]{2,1,0:T(8,128)(2,1)} %bitcast.31, s32[16,2,256]{2,1,0:T(2,128)} %labels_in.1), custom_call_target="tpu_custom_call" | custom-call | flops 268435456 | bytes 1048576 | tf_op jit(solution)/shard_map/pallas_call | solution.py:511
  2.8 5.1 %collective-permute-start = (bf16[32,1152]{1,0:T(8,128)(2,1)S(1)}, bf16[32,1152]{1,0:T(8,128)(2,1)S(1)}, u32[]{:S(2)}, u32[]{:S(2)}) collective-permute-start(bf16[32,1152]{1,0:T(8,128)(2,1)S(1)} %get-tuple-element.39), channel_id=1, source_target_pairs={{1,0},{2,1},{3,2},{4,3},{5,4},{6,5},{7,6},{8,7},{9,8},{10,9},{11,1... | collective-permute-start | bytes 221192 | tf_op jit(solution)/shard_map/ppermute | solution.py:562
  8.6 0.9 shard_map.144
  9.5 3.9 %shard_map.145 = (bf16[1,288,1024]{2,1,0:T(8,128)(2,1)}, bf16[1,288,1024]{2,1,0:T(8,128)(2,1)}, bf16[1,288,1024]{2,1,0:T(8,128)(2,1)}, bf16[288,128]{1,0:T(8,128)(2,1)S(1)}, bf16[16,144,128]{2,1,0:T(8,128)(2,1)}) custom-call(bf16[256,1024]{1,0:T(8,128)(2,1)S(1)} %get-tuple-element.37.stem, bf16[256,128]{1,0:T(8,128)(2,1)S(1)} %get-tuple-element.38.marks, ...), custom_call_target="tpu_custom_call" | custom-call | flops 1073741824 | bytes 1048576 | tf_op jit(solution)/shard_map/pallas_call | solution.py:511
  13.4 30.5 %all_to_all.25.message = bf16[16,144,128]{2,1,0:T(8,128)(2,1)S(1)} all-to-all(bf16[16,144,128]{2,1,0:T(8,128)(2,1)} %get-tuple-element.42), channel_id=1, replica_groups=mesh['slab'=16,'gx'=16] {'slab'}, dimensions={0} | all-to-all | bytes 1179648 | tf_op jit(solution)/shard_map/all_to_all | solution.py:585
  43.9 8.5 %shard_map.146 = (f32[272,32]{1,0:T(8,128)S(1)}, bf16[288,64]{1,0:T(8,128)(2,1)S(1)}, bf16[288,64]{1,0:T(8,128)(2,1)S(1)}, bf16[16,144,128]{2,1,0:T(8,128)(2,1)}...) custom-call(bf16[16,144,128]{2,1,0:T(8,128)(2,1)S(1)} %all_to_all.25, ...), custom_call_target="tpu_custom_call" | custom-call | flops 2147483648 | bytes 1048576 | tf_op jit(solution)/shard_map/pallas_call | solution.py:511
  52.4 3.6 %all-to-all-start.1 = ((bf16[16,144,128]{2,1,0:T(8,128)(2,1)}), bf16[16,144,128]{2,1,0:T(8,128)(2,1)S(1)}, u32[]{:S(2)}, u32[]{:S(2)}) async-start(bf16[16,144,128]{2,1,0:T(8,128)(2,1)} %get-tuple-element.46), calls=%async_computation.1 | async-start | bytes 1179648 | tf_op jit(solution)/shard_map/all_to_all | solution.py:597
  56.0 3.5 %collective-permute-start.1 = (f32[16,32]{1,0:T(8,128)S(1)}, f32[16,32]{1,0:T(8,128)S(1)}, u32[]{:S(2)}, u32[]{:S(2)}) collective-permute-start(f32[16,32]{1,0:T(8,128)S(1)} %slice.18), channel_id=1, source_target_pairs={{0,1},{1,2},{2,3},{3,4},{4,5},{5,6},{6,7},{7,8},{8,9},{9,10},{10,1... | collective-permute-start | bytes 6152 | tf_op jit(solution)/shard_map/ppermute | solution.py:623
  59.6 4.4 %shard_map.147.grads_cd = bf16[160,128]{1,0:T(8,128)(2,1)S(1)} custom-call(bf16[16,144,128]{2,1,0:T(8,128)(2,1)S(1)} %all_to_all.25.message, bf16[288,64]{1,0:T(8,128)(2,1)S(1)} %get-tuple-element.47.errors_one, bf16[288,64]{1,0:T(8,128)(2,1)S(1)} %get-tuple-element.48.errors_two, bf16[2,288,512]{2,1,0:T(8,128)(2,1)} %get-tuple-element.49.refs_0_, ...), custom_call_target="tpu_custom_call" | custom-call | flops 2147483648 | bytes 1048576 | tf_op jit(solution)/shard_map/pallas_call | solution.py:511
  64.0 9.8 %all-to-all-done.1.back = bf16[16,144,128]{2,1,0:T(8,128)(2,1)S(1)} async-done(((bf16[16,144,128]{2,1,0:T(8,128)(2,1)}), bf16[16,144,128]{2,1,0:T(8,128)(2,1)S(1)}, u32[]{:S(2)}, u32[]{:S(2)}) %all-to-all-start.1) | async-done | bytes 589856 | tf_op jit(solution)/shard_map/all_to_all | solution.py:597
  73.8 6.1 %shard_map.148 = (bf16[16,20,128]{2,1,0:T(8,128)(2,1)}, bf16[1,288,1024]{2,1,0:T(8,128)(2,1)}) custom-call(bf16[16,144,128]{2,1,0:T(8,128)(2,1)S(1)} %all-to-all-done.1.back, bf16[160,128]{1,0:T(8,128)(2,1)S(1)} %shard_map.147.grads_cd, bf16[3,3,32,32]{3,2,1,0:T(8,128)(2,1)S(1)} %bitcast.24, bf16[1,288,1024]{2,1,0:T(8,128)(2,1)} %get-tuple-element.53.hidden_two_in, ...), custom_call_target="tpu_custom_call" | custom-call | flops 2147483648 | bytes 1048576 | tf_op jit(solution)/shard_map/pallas_call | solution.py:511
  79.9 6.2 %all-to-all-start.2 = ((bf16[16,20,128]{2,1,0:T(8,128)(2,1)}), bf16[16,20,128]{2,1,0:T(8,128)(2,1)S(1)}, u32[]{:S(2)}, u32[]{:S(2)}) async-start(bf16[16,20,128]{2,1,0:T(8,128)(2,1)} %get-tuple-element.56), calls=%async_computation.2 | async-start | bytes 196608 | tf_op jit(solution)/shard_map/all_to_all | solution.py:531
  86.1 2.2 %shard_map.149 = bf16[272,1024]{1,0:T(8,128)(2,1)S(1)} custom-call(bf16[1,288,1024]{2,1,0:T(8,128)(2,1)} %get-tuple-element.57.delta_a_in, bf16[3,3,32,32]{3,2,1,0:T(8,128)(2,1)S(1)} %bitcast.26), custom_call_target="tpu_custom_call" | custom-call | flops 1073741824 | bytes 1048576 | tf_op jit(solution)/shard_map/pallas_call | solution.py:511
  88.3 3.6 %all-to-all-done.2 = bf16[16,20,128]{2,1,0:T(8,128)(2,1)S(1)} async-done(((bf16[16,20,128]{2,1,0:T(8,128)(2,1)}), bf16[16,20,128]{2,1,0:T(8,128)(2,1)S(1)}, u32[]{:S(2)}, u32[]{:S(2)}) %all-to-all-start.2) | async-done | bytes 81952 | tf_op jit(solution)/shard_map/all_to_all | solution.py:531
  92.0 0.7 broadcast_in_dim.24
  92.7 5.4 %all-to-all-start.3 = ((f32[16,20,128]{2,1,0:T(8,128)}), f32[16,20,128]{2,1,0:T(8,128)S(1)}, u32[]{:S(2)}, u32[]{:S(2)}) async-start(f32[16,20,128]{2,1,0:T(8,128)} %broadcast_in_dim.24), calls=%async_computation.3 | async-start | bytes 393216 | tf_op jit(solution)/shard_map/all_to_all | solution.py:535
  98.2 2.7 %collective-permute-start.2 = (bf16[16,1024]{1,0:T(8,128)(2,1)S(1)}, bf16[16,1024]{1,0:T(8,128)(2,1)S(1)}, u32[]{:S(2)}, u32[]{:S(2)}) collective-permute-start(bf16[16,1024]{1,0:T(8,128)(2,1)S(1)} %slice.21), channel_id=1, source_target_pairs={{0,1},{1,2},{2,3},{3,4},{4,5},{5,6},{6,7},{7,8},{8,9},{9,10},{10,1... | collective-permute-start | bytes 98312 | tf_op jit(solution)/shard_map/ppermute | solution.py:623
  101.0 0.6 copy.36
  101.7 5.4 %all-to-all-done.3 = f32[16,20,128]{2,1,0:T(8,128)S(1)} async-done(((f32[16,20,128]{2,1,0:T(8,128)}), f32[16,20,128]{2,1,0:T(8,128)S(1)}, u32[]{:S(2)}, u32[]{:S(2)}) %all-to-all-start.3) | async-done | bytes 163872 | tf_op jit(solution)/shard_map/all_to_all | solution.py:535
  107.1 0.7 broadcast_in_dim.25
  107.8 5.6 %all-to-all-start.4 = ((f32[16,20,128]{2,1,0:T(8,128)}), f32[16,20,128]{2,1,0:T(8,128)S(1)}, u32[]{:S(2)}, u32[]{:S(2)}) async-start(f32[16,20,128]{2,1,0:T(8,128)} %broadcast_in_dim.25), calls=%async_computation.4 | async-start | bytes 393216 | tf_op jit(solution)/shard_map/all_to_all | solution.py:537
  113.7 1.1 copy.37
  114.8 5.4 %all-to-all-done.4.total = f32[16,20,128]{2,1,0:T(8,128)S(1)} async-done(((f32[16,20,128]{2,1,0:T(8,128)}), f32[16,20,128]{2,1,0:T(8,128)S(1)}, u32[]{:S(2)}, u32[]{:S(2)}) %all-to-all-start.4) | async-done | bytes 163872 | tf_op jit(solution)/shard_map/all_to_all | solution.py:537
  120.2 0.9 shard_map.150
  (28 shorter events, 1.2 us)
Async XLA Ops:
  0.6 7.3 %copy-start.2 = (bf16[32,3,3,32]{3,0,2,1:T(8,128)(2,1)S(1)}, bf16[32,3,3,32]{3,0,2,1:T(8,128)(2,1)}, u32[]{:S(2)}) copy-start(bf16[32,3,3,32]{3,0,2,1:T(8,128)(2,1)} %param.11) | copy-start | bytes 55300
  0.6 7.3 %copy-start.3 = (bf16[32,3,3,32]{3,0,2,1:T(8,128)(2,1)S(1)}, bf16[32,3,3,32]{3,0,2,1:T(8,128)(2,1)}, u32[]{:S(2)}) copy-start(bf16[32,3,3,32]{3,0,2,1:T(8,128)(2,1)} %param.10) | copy-start | bytes 55300
  2.8 6.7 %collective-permute-start = (bf16[32,1152]{1,0:T(8,128)(2,1)S(1)}, bf16[32,1152]{1,0:T(8,128)(2,1)S(1)}, u32[]{:S(2)}, u32[]{:S(2)}) collective-permute-start(bf16[32,1152]{1,0:T(8,128)(2,1)S(1)} %get-tuple-element.39), channel_id=1, source_target_pairs={{1,0},{2,1},{3,2},{4,3},{5,4},{6,5},{7,6},{8,7},{9,8},{10,9},{11,1... | collective-permute-start | bytes 221192 | tf_op jit(solution)/shard_map/ppermute | solution.py:562
  7.9 0.7 copy-start.4
  7.9 0.7 copy-start.5
  13.4 30.5 %copy-start = (bf16[32,3,3,32]{3,0,2,1:T(8,128)(2,1)S(1)}, bf16[32,3,3,32]{3,0,2,1:T(8,128)(2,1)}, u32[]{:S(2)}) copy-start(bf16[32,3,3,32]{3,0,2,1:T(8,128)(2,1)} %param.12) | copy-start | bytes 55300
  13.4 30.5 %copy-start.1 = (bf16[32,3,3,32]{3,0,2,1:T(8,128)(2,1)S(1)}, bf16[32,3,3,32]{3,0,2,1:T(8,128)(2,1)}, u32[]{:S(2)}) copy-start(bf16[32,3,3,32]{3,0,2,1:T(8,128)(2,1)} %param.13) | copy-start | bytes 55300
  52.4 21.4 %all-to-all-start.1 = ((bf16[16,144,128]{2,1,0:T(8,128)(2,1)}), bf16[16,144,128]{2,1,0:T(8,128)(2,1)S(1)}, u32[]{:S(2)}, u32[]{:S(2)}) async-start(bf16[16,144,128]{2,1,0:T(8,128)(2,1)} %get-tuple-element.46), calls=%async_computation.1 | async-start | bytes 1179648 | tf_op jit(solution)/shard_map/all_to_all | solution.py:597
  56.0 42.1 %collective-permute-start.1 = (f32[16,32]{1,0:T(8,128)S(1)}, f32[16,32]{1,0:T(8,128)S(1)}, u32[]{:S(2)}, u32[]{:S(2)}) collective-permute-start(f32[16,32]{1,0:T(8,128)S(1)} %slice.18), channel_id=1, source_target_pairs={{0,1},{1,2},{2,3},{3,4},{4,5},{5,6},{6,7},{7,8},{8,9},{9,10},{10,1... | collective-permute-start | bytes 6152 | tf_op jit(solution)/shard_map/ppermute | solution.py:623
  79.9 12.0 %all-to-all-start.2 = ((bf16[16,20,128]{2,1,0:T(8,128)(2,1)}), bf16[16,20,128]{2,1,0:T(8,128)(2,1)S(1)}, u32[]{:S(2)}, u32[]{:S(2)}) async-start(bf16[16,20,128]{2,1,0:T(8,128)(2,1)} %get-tuple-element.56), calls=%async_computation.2 | async-start | bytes 196608 | tf_op jit(solution)/shard_map/all_to_all | solution.py:531
  92.7 14.4 %all-to-all-start.3 = ((f32[16,20,128]{2,1,0:T(8,128)}), f32[16,20,128]{2,1,0:T(8,128)S(1)}, u32[]{:S(2)}, u32[]{:S(2)}) async-start(f32[16,20,128]{2,1,0:T(8,128)} %broadcast_in_dim.24), calls=%async_computation.3 | async-start | bytes 393216 | tf_op jit(solution)/shard_map/all_to_all | solution.py:535
  98.2 15.2 %collective-permute-start.2 = (bf16[16,1024]{1,0:T(8,128)(2,1)S(1)}, bf16[16,1024]{1,0:T(8,128)(2,1)S(1)}, u32[]{:S(2)}, u32[]{:S(2)}) collective-permute-start(bf16[16,1024]{1,0:T(8,128)(2,1)S(1)} %slice.21), channel_id=1, source_target_pairs={{0,1},{1,2},{2,3},{3,4},{4,5},{5,6},{6,7},{7,8},{8,9},{9,10},{10,1... | collective-permute-start | bytes 98312 | tf_op jit(solution)/shard_map/ppermute | solution.py:623
  107.8 12.3 %all-to-all-start.4 = ((f32[16,20,128]{2,1,0:T(8,128)}), f32[16,20,128]{2,1,0:T(8,128)S(1)}, u32[]{:S(2)}, u32[]{:S(2)}) async-start(f32[16,20,128]{2,1,0:T(8,128)} %broadcast_in_dim.25), calls=%async_computation.4 | async-start | bytes 393216 | tf_op jit(solution)/shard_map/all_to_all | solution.py:537

commit v4 on v3

--- a/solution.py
+++ b/solution.py
@@ -58,15 +58,8 @@
 
 def conv_window(shifted, plane, window, band):
     lanes = slice(256 * window, 256 * window + 512)
-    total = None
-    for tap in range(3):
-        term = jnp.dot(
-            shifted[plane, tap, :, lanes],
-            band[512 * tap : 512 * tap + 512, :],
-            preferred_element_type=F32,
-        )
-        total = term if total is None else total + term
-    return total
+    columns = jnp.concatenate([shifted[plane, tap, :, lanes] for tap in range(3)], axis=1)
+    return jnp.dot(columns, band[...], preferred_element_type=F32)
 
 
 def windows_of(shifted):
@@ -178,33 +171,72 @@
     return shifted.at[:, 1, :, pl.ds(128, shifted.shape[-1] - 256)]
 
 
-def arrange_kernel(stem_in, labels_in, stem_out, marks_out, initial, flat, stem, labels, sems):
+def columns_first(stem, flat, side, group):
+    first = 1024 * side + 4 * group
+    rows = [flat[pl.ds(first + k, 32, stride=32), :] for k in range(4)]
+    return jnp.concatenate(rows, axis=0).T
+
+
+def fill_flat(stem, flat, side):
+    part = stem[:, :, 128 * side : 128 * side + 128].reshape(1024, 128)
+    flat[1024 * side : 1024 * side + 1024, :] = part.astype(F32)
+
+
+def marks_first(labels):
+    marks = labels.astype(F32)
+    blank = jnp.zeros((96, labels.shape[2]), F32)
+    marks = jnp.concatenate([marks[:, 0, :], marks[:, 1, :], blank], axis=0)
+    return marks.T.astype(BF16)
+
+
+def edge_kernel(stem_in, labels_in, initial, flat, stem, labels, sems):
+    copies = Copies(sems)
+    near = pl.ds(0, 128)
+    for k in range(4):
+        rows = pl.ds(8 * k, 8)
+        copies.start(stem_in.at[rows, :, near], stem.at[rows])
+    copies.start(labels_in.at[:, :, near], labels)
+    wait_all(copies.started)
+    fill_flat(stem, flat, 0)
+    for group in range(8):
+        value = columns_first(stem, flat, 0, group)
+        initial[:, 128 * group : 128 * group + 128] = value[:HALO].astype(BF16)
+    initial[:, 1024:1152] = marks_first(labels[...])[:HALO]
+
+
+def arrange_kernel(
+    stem_in, labels_in, conv_a_in, conv_b_in, head_one_in, head_two_in,
+    stem_out, marks_out, band_a, band_b, spread_out,
+    flat, stem, labels, conv_a, conv_b, heads, spread, sems,
+):
     cols = stem.shape[2]
     copies = Copies(sems)
+    copies.start(conv_a_in, conv_a)
+    copies.start(conv_b_in, conv_b)
+    copies.start(head_one_in, heads.at[0])
+    copies.start(head_two_in, heads.at[1])
+    copies.start(labels_in, labels)
     for k in range(4):
         rows = pl.ds(8 * k, 8)
         copies.start(stem_in.at[rows], stem.at[rows])
-    labels_here = copies.start(labels_in, labels)
-    wait_all(copies.started[:4])
+    wait_all(copies.started[:5])
+    same = own_voxel()
+    for k in range(2):
+        four = jnp.concatenate([heads[k].astype(F32)] * 4, axis=1)
+        along = jnp.concatenate([four] * 8, axis=1)
+        spread[32 * k : 32 * k + 32, :] = jnp.where(same, along, 0.0).astype(BF16)
+    leaving = copies.start(spread, spread_out)
+    marks_out[...] = marks_first(labels[...])
+    fill_band(conv_a, band_a, 1, False)
+    fill_band(conv_b, band_b, 2, False)
+    wait_all(copies.started[5:9])
     for side in range(cols // 128):
-        part = stem[:, :, 128 * side : 128 * side + 128].reshape(1024, 128)
-        flat[1024 * side : 1024 * side + 1024, :] = part.astype(F32)
+        fill_flat(stem, flat, side)
     for group in range(8):
-        sides = []
-        for side in range(cols // 128):
-            first = 1024 * side + 4 * group
-            rows = [flat[pl.ds(first + k, 32, stride=32), :] for k in range(4)]
-            sides.append(jnp.concatenate(rows, axis=0).T)
-        lanes = slice(128 * group, 128 * group + 128)
+        sides = [columns_first(stem, flat, side, group) for side in range(cols // 128)]
         value = jnp.concatenate(sides, axis=0).astype(BF16)
-        stem_out[:, lanes] = value
-        initial[:, lanes] = value[:HALO]
-    labels_here.wait()
-    marks = labels[...].astype(F32)
-    marks = jnp.concatenate([marks[:, 0, :], marks[:, 1, :], jnp.zeros((96, cols), F32)], axis=0)
-    marks = marks.T.astype(BF16)
-    marks_out[...] = marks
-    initial[:, 1024:1152] = marks[:HALO]
+        stem_out[:, 128 * group : 128 * group + 128] = value
+    leaving.wait()
 
 
 def own_voxel():
@@ -212,23 +244,10 @@
     return voxel == lax.broadcasted_iota(jnp.int32, (32, 1024), 1) // 32
 
 
-def first_bands_kernel(conv_a, conv_b, head_one, head_two, band_a, band_b, spread_out, spread, sems):
-    same = own_voxel()
-    for k, head in enumerate((head_one, head_two)):
-        four = jnp.concatenate([head[...].astype(F32)] * 4, axis=1)
-        along = jnp.concatenate([four] * 8, axis=1)
-        spread[32 * k : 32 * k + 32, :] = jnp.where(same, along, 0.0).astype(BF16)
-    copies = Copies(sems)
-    copies.start(spread, spread_out)
-    fill_band(conv_a, band_a, 1, False)
-    fill_band(conv_b, band_b, 2, False)
-    wait_all(copies.started)
-
-
 def forward_xy_kernel(
     stem, marks, after, band_a, band_b,
     stem_frame, hidden_one, hidden_two, marks_out, message,
-    stem_s, one_s, two, packed, sems,
+    stem_s, one_s, two, sems,
 ):
     _, inside = edge_gates()
     copies = Copies(sems)
@@ -252,11 +271,9 @@
         half = value.shape[0] // 2
         for peer in range(4):
             lanes = slice(64 * peer, 64 * peer + 64)
-            packed[4 * window + peer] = jnp.concatenate(
+            message[4 * window + peer] = jnp.concatenate(
                 [value[:half, lanes], value[half:, lanes]], axis=1
             )
-        peers = pl.ds(4 * window, 4)
-        copies.start(packed.at[peers], message.at[peers])
     wait_all(copies.started)
 
 
@@ -283,10 +300,10 @@
 
 def section_xz_kernel(
     message, marks, conv_c, conv_d, spread_in,
-    probability, errors_one, errors_two, back, ref_one_out, ref_two_out, delta_two_out, delta_one_out,
-    two_s, ref_one_s, delta_two_s, delta_one_s, ref_two, packed, bands, spread, sems,
+    probability, back,
+    two_s, ref_one_s, delta_two_s, delta_one_s, ref_two, packed, bands, spread, grads, sems,
 ):
-    _, inside = edge_gates()
+    left, inside = edge_gates()
     copies = Copies(sems)
     spread_here = copies.start(spread_in, spread)
     band_c, band_d, band_dt, band_ct = [bands.at[k] for k in range(4)]
@@ -300,12 +317,10 @@
     for plane, window in places:
         value = gated(softplus(conv_window(two_s, plane, window, band_c)), inside)
         store_shifted(ref_one_s, plane, 256 * window, value, 2)
-    copies.start(centre(ref_one_s), ref_one_out)
     fill_band(conv_d, band_d, 2, False)
     for plane, window in places:
         value = softplus(conv_window(ref_one_s, plane, window, band_d))
         ref_two[plane, :, 256 * window : 256 * window + 256] = value.astype(BF16)
-    copies.start(ref_two, ref_two_out)
     fill_band(conv_d, band_dt, 2, True)
 
     labels = marks[:, 0:32].astype(F32)
@@ -331,8 +346,6 @@
     error_one = 1.0 / (1.0 + jnp.exp(-first)) - labels + error_two
     error_two = split(error_two)
     error_one = split(error_one)
-    errors_one[...] = error_one
-    errors_two[...] = error_two
     spread_one = jnp.concatenate([spread_one, spread_one], axis=0)
     spread_two = jnp.concatenate([spread_two, spread_two], axis=0)
 
@@ -342,7 +355,6 @@
         value = jnp.dot(error_two, spread_two[:, lanes], preferred_element_type=F32)
         value = value * slope(ref_two[plane, :, at : at + 256])
         store_shifted(delta_two_s, plane, at, value, 2)
-    copies.start(centre(delta_two_s), delta_two_out)
     fill_band(conv_c, band_ct, 1, True)
     for plane, window in places:
         at = 256 * window
@@ -350,7 +362,6 @@
         stored = ref_one_s[plane, 1, :, 128 + at : 384 + at]
         value = gated(value * slope(stored), inside)
         store_shifted(delta_one_s, plane, at, value, 1)
-    copies.start(centre(delta_one_s), delta_one_out)
     for window in range(2):
         values = []
         for plane in range(2):
@@ -361,7 +372,7 @@
             values.append(value.astype(BF16))
         for z in range(8):
             lanes = slice(32 * z, 32 * z + 32)
-            packed[8 * window + z] = jnp.concatenate(
+            packed[8 * window + z, :half] = jnp.concatenate(
                 [
                     values[0][:half, lanes], values[1][:half, lanes],
                     values[0][half:, lanes], values[1][half:, lanes],
@@ -370,33 +381,16 @@
             )
         for part in range(2):
             peers = pl.ds(8 * window + 4 * part, 4)
-            copies.start(packed.at[peers], back.at[peers])
-    wait_all(copies.started[1:])
-
-
-def section_grads_kernel(message, errors_one, errors_two, *refs):
-    sources, grads_out = refs[:4], refs[4]
-    two_s, ref_one_s, grads, ref_one, ref_two, delta_two, delta_one, sems = refs[5:]
-    first, _ = edge_gates()
-    copies = Copies(sems)
-    for source, target in zip(sources, (ref_one, ref_two, delta_two, delta_one)):
-        copies.start(source, target)
-    rows = errors_one.shape[0]
-    own = slice(0, rows - LEFT)
+            rows_sent = pl.ds(0, half)
+            copies.start(packed.at[peers, rows_sent], back.at[peers, rows_sent])
+
     same = own_voxel()
     same = jnp.concatenate([same, same], axis=0)
-    clear_margins(two_s)
-    clear_margins(ref_one_s)
-    load_features(message, two_s)
-    wait_all(copies.started)
-    for plane, window in windows_of(two_s):
-        at = 256 * window
-        value = ref_one[plane, :, at : at + 256].astype(F32)
-        store_shifted(ref_one_s, plane, at, value, 2)
+    kept_rows = slice(0, rows - LEFT)
 
     def head_grad(errors, planes):
-        error = errors[own, :].astype(F32)
-        error = jnp.concatenate([error[:LEFT] * first, error[LEFT:]], axis=0).astype(BF16)
+        error = errors[kept_rows].astype(F32)
+        error = jnp.concatenate([error[:LEFT] * left, error[LEFT:]], axis=0).astype(BF16)
         total = None
         for plane, feature in enumerate(planes):
             full = lax.dot_general(error, feature, CONTRACT_ROWS, preferred_element_type=F32)
@@ -409,40 +403,51 @@
         return total[:, 0:32]
 
     grads[...] = jnp.zeros(grads.shape, F32)
-    features = [two_s[plane, 1, own, 128:640] for plane in range(2)]
-    put_piece(grads, 18, head_grad(errors_one, features))
-    put_piece(grads, 19, head_grad(errors_two, [ref_two[plane, own, :] for plane in range(2)]))
-    weight_grad(delta_two, ref_one_s, 2, grads, 9, first)
-    weight_grad(delta_one, two_s, 1, grads, 0, first)
-    grads_out[...] = grads[...].astype(BF16)
+    features = [two_s[plane, 1, kept_rows, 128:640] for plane in range(2)]
+    put_piece(grads, 18, head_grad(error_one, features))
+    features = [ref_two[plane, kept_rows, :] for plane in range(2)]
+    put_piece(grads, 19, head_grad(error_two, features))
+    weight_grad(centre(delta_two_s), ref_one_s, 2, grads, 9, left)
+    weight_grad(centre(delta_one_s), two_s, 1, grads, 0, left)
+    blank = jnp.zeros((6, 128), F32)
+    for peer in range(16):
+        chunk = jnp.concatenate([grads[10 * peer : 10 * peer + 10, :], blank], axis=0)
+        packed[peer, half : half + 16, :] = chunk.astype(BF16)
+    rows_sent = pl.ds(half, 16)
+    copies.start(packed.at[:, rows_sent], back.at[:, rows_sent])
+    wait_all(copies.started[1:])
+
+
+def ready_kernel(conv_b, hidden_two_in, hidden_two, band_bt, sems):
+    copies = Copies(sems)
+    copies.start(hidden_two_in, hidden_two)
+    fill_band(conv_b, band_bt, 2, True)
+    wait_all(copies.started)
 
 
 def backward_xy_kernel(
-    back, grads_cd, conv_b, hidden_two_in, hidden_one_in, stem_in,
-    grads_out, delta_a_out,
-    stem_s, one_s, delta_b_s, delta_b, delta_a, grads, hidden_two, band_bt, hidden_one, stem, sems,
+    back, hidden_two, band_bt, hidden_one_in, stem_in,
+    mine_out, theirs_out, delta_a_out,
+    one_s, stem_s, delta_b_s, delta_b, delta_a, grads, hidden_one, stem, sems,
 ):
     first, inside = edge_gates()
     copies = Copies(sems)
-    two_here = copies.start_lanes(hidden_two_in, hidden_two, 4)
-    one_here = copies.start_lanes(hidden_one_in, hidden_one, 4)
-    stem_here = copies.start_lanes(stem_in, stem, 4)
-    for shifted in (stem_s, one_s, delta_b_s):
+    one_here = copies.start_lanes(hidden_one_in, hidden_one, 2)
+    stem_here = copies.start_lanes(stem_in, stem, 2)
+    for shifted in (one_s, stem_s, delta_b_s):
         clear_margins(shifted)
-    fill_band(conv_b, band_bt, 2, True)
+    half = back.shape[1] - 16
     for group in range(8):
         parts = []
         for side in range(2):
             at = 64 * side
             parts.append(
                 jnp.concatenate(
-                    [back[2 * group + q][:, at : at + 64] for q in range(2)], axis=1
+                    [back[2 * group + q, :half, at : at + 64] for q in range(2)], axis=1
                 )
             )
         lanes = slice(128 * group, 128 * group + 128)
         value = jnp.concatenate(parts, axis=0).astype(F32)
-        if group % 2 == 0:
-            two_here[group // 2].wait()
         value = gated(value * slope(hidden_two[0, :, lanes]), inside)
         delta_b[0, :, lanes] = value.astype(BF16)
         store_shifted(delta_b_s, 0, 128 * group, value, 2)
@@ -462,9 +467,16 @@
     grads[...] = jnp.zeros(grads.shape, F32)
     weight_grad(delta_b, one_s, 2, grads, 9, first)
     weight_grad(delta_a, stem_s, 1, grads, 0, first)
-    for peer in range(8):
-        grads_out[peer] = grads[20 * peer : 20 * peer + 20, :].astype(BF16)
-        grads_out[8 + peer] = grads_cd[20 * peer : 20 * peer + 20, :]
+    chunk = back[0, half:, :].astype(F32)
+    for peer in range(1, 16):
+        chunk = chunk + back[peer, half:, :].astype(F32)
+    last = [grads[128 + 16 * (k % 2) : 144 + 16 * (k % 2), 32 * (k // 2) : 32 * (k // 2) + 32] for k in range(4)]
+    grads[128:144, :] = jnp.concatenate(last, axis=1)
+    core = lax.rem(lax.axis_index("gx"), 2)
+    mine_out[0:72, :] = grads[pl.ds(pl.multiple_of(72 * core, 8), 72), :]
+    theirs_out[0:72, :] = grads[pl.ds(pl.multiple_of(72 * (1 - core), 8), 72), :]
+    mine_out[72:88, :] = chunk
+    theirs_out[72:88, :] = chunk
     leaving.wait()
 
 
@@ -484,11 +496,37 @@
         stem_grad[:, at : at + 256] = value[: rows - LEFT].astype(BF16)
 
 
-def finish_kernel(factor, total, grad_a, grad_b, grad_c, grad_d, head_one, head_two):
-    flat = total[...].reshape(320, 128) * factor
+def place_kernel(found, moved, stem_grad, flat):
+    cols = stem_grad.shape[2]
+    first, _ = edge_gates()
+    for group in range(8):
+        lanes = slice(128 * group, 128 * group + 128)
+        mine = found[:cols, lanes].astype(F32)
+        head = mine[:LEFT] * first + moved[:, lanes].astype(F32) * (1.0 - first)
+        value = jnp.concatenate([head, mine[LEFT:]], axis=0)
+        for side in range(cols // 128):
+            turned = value[128 * side : 128 * side + 128].T
+            for k in range(4):
+                start = 1024 * side + 4 * group + k
+                flat[pl.ds(start, 32, stride=32), :] = turned[32 * k : 32 * k + 32]
+    for side in range(cols // 128):
+        part = flat[1024 * side : 1024 * side + 1024, :].reshape(32, 32, 128)
+        stem_grad[:, :, 128 * side : 128 * side + 128] = part.astype(BF16)
+
+
+def finish_kernel(factor, mine, theirs, chunks, grad_a, grad_b, grad_c, grad_d, head_one, head_two, flat):
+    core = lax.rem(lax.axis_index("gx"), 2)
+    flat[pl.ds(pl.multiple_of(72 * core, 8), 72), :] = mine[...] * factor
+    flat[pl.ds(pl.multiple_of(72 * (1 - core), 8), 72), :] = theirs[...] * factor
+    for peer in range(16):
+        flat[160 + 10 * peer : 170 + 10 * peer, :] = chunks[peer, 0:10, :].astype(F32) * factor
 
     def piece(pair, index):
         row, lane = 160 * pair + 32 * (index // 4), 32 * (index % 4)
+        if pair == 0 and index >= 16:
+            lane = 64 * (index % 4)
+            halves = [flat[row : row + 16, lane + at : lane + at + 32] for at in (0, 32)]
+            return jnp.concatenate(halves, axis=0)
         return flat[row : row + 32, lane : lane + 32]
 
     for pair, (near, far) in enumerate(((grad_a, grad_b), (grad_c, grad_d))):
@@ -526,15 +564,20 @@
     return jax.ShapeDtypeStruct(dims, dtype)
 
 
-def sum_everywhere(grads, beside, slab, gx):
+def sum_everywhere(mine, theirs, beside, later, slab, gx):
     peers, copies = lax.axis_size(gx), lax.axis_size(slab)
-    mine = lax.all_to_all(grads, gx, 0, 0, tiled=True)
+    swap = [(i, i ^ 1) for i in range(peers)]
+    mine = mine + lax.ppermute(theirs, gx, swap)
+    spread = jnp.broadcast_to(mine.astype(BF16)[None], (peers // 2,) + mine.shape)
+    same_core = [[i for i in range(peers) if i % 2 == core] for core in range(2)]
+    mine = lax.all_to_all(spread, gx, 0, 0, tiled=True, axis_index_groups=same_core)
     mine, beside = lax.optimization_barrier((mine, beside))
     mine = jnp.sum(mine.astype(F32), axis=0)
-    spread = jnp.broadcast_to(mine[None], (copies,) + mine.shape)
-    mine = jnp.sum(lax.all_to_all(spread, slab, 0, 0, tiled=True), axis=0)
-    spread = jnp.broadcast_to(mine[None], (peers,) + mine.shape)
-    return lax.all_to_all(spread, gx, 0, 0, tiled=True), beside
+    spread = jnp.broadcast_to(mine.astype(BF16)[None], (copies,) + mine.shape)
+    found = lax.all_to_all(spread, slab, 0, 0, tiled=True)
+    found, beside = lax.optimization_barrier((found, later(beside)))
+    mine = jnp.sum(found[:, :72].astype(F32), axis=0)
+    return (mine, lax.ppermute(mine, gx, swap), found[:, 72:]), beside
 
 
 def per_device(stem_features, labels, conv_a, conv_b, conv_c, conv_d, head_one, head_two):
@@ -548,16 +591,11 @@
     vmem = lambda kind: pltpu.VMEM(kind.shape, kind.dtype)
 
     stem_features = stem_features[:, 0]
-    stem, marks, initial = call(
-        arrange_kernel,
-        [
-            (shape((cols, 1024), BF16), VMEM),
-            (shape((cols, 128), BF16), VMEM),
-            (shape((HALO, 1152), BF16), VMEM),
-        ],
-        [HBM, HBM],
-        [pltpu.VMEM((1024 * cols // 128, 128), F32), vmem(stem_features), vmem(labels), sems(5)],
-        flops=1 << 28, megabytes=6,
+    near = pltpu.VMEM((C, height, 128), BF16)
+    near_labels = pltpu.VMEM((16, 2, 128), labels.dtype)
+    (initial,) = call(
+        edge_kernel, [(shape((HALO, 1152), BF16), VMEM)], [HBM, HBM],
+        [pltpu.VMEM((1024, 128), F32), near, near_labels, sems(5)], flops=1 << 28, megabytes=3,
     )(stem_features, labels)
     after = lax.ppermute(initial, "gx", down)
 
@@ -566,10 +604,20 @@
     ]
     band = shape((1536, 256), BF16)
     spreads = shape((64, 1024), BF16)
-    band_a, band_b, spread = call(
-        first_bands_kernel, [(band, VMEM)] * 2 + [(spreads, HBM)], [VMEM] * 4,
-        [vmem(spreads), sems(1)], flops=1 << 29, megabytes=3,
-    )(taps_a, taps_b, head_one[None], head_two[None])
+    stem, marks, band_a, band_b, spread = call(
+        arrange_kernel,
+        [
+            (shape((cols, 1024), BF16), VMEM),
+            (shape((cols, 128), BF16), VMEM),
+            (band, VMEM),
+            (band, VMEM),
+            (spreads, HBM),
+        ],
+        [HBM] * 6,
+        [pltpu.VMEM((1024 * cols // 128, 128), F32), vmem(stem_features), vmem(labels)]
+        + [vmem(taps_a), vmem(taps_b), pltpu.VMEM((2, 1, C), BF16), vmem(spreads), sems(10)],
+        flops=1 << 29, megabytes=6,
+    )(stem_features, labels, taps_a, taps_b, head_one[None], head_two[None])
 
     wide = pltpu.VMEM((1, 3, rows, 1280), BF16)
     tall = pltpu.VMEM((2, 3, rows, 768), BF16)
@@ -578,65 +626,69 @@
     messages = shape((16, half, 128), BF16)
     stem, hidden_one, hidden_two, marks, message = call(
         forward_xy_kernel,
-        [(whole, HBM)] * 3 + [(shape((rows, 128), BF16), VMEM), (messages, HBM)],
+        [(whole, HBM)] * 3 + [(shape((rows, 128), BF16), VMEM), (messages, VMEM)],
         [VMEM] * 5,
-        [wide, wide, vmem(whole), vmem(messages), sems(10)], flops=1 << 30, megabytes=8,
+        [wide, wide, vmem(whole), sems(6)], flops=1 << 30, megabytes=8,
     )(stem, marks, after, band_a, band_b)
     message = lax.all_to_all(message, "slab", 0, 0, tiled=True)
 
-    pairs = shape((rows, 64), BF16)
-    probability, errors_one, errors_two, back, *held = call(
+    larger = shape((16, half + 16, 128), BF16)
+    probability, back = call(
         section_xz_kernel,
-        [(shape((rows - LEFT, 32), F32), VMEM), (pairs, VMEM), (pairs, VMEM), (messages, HBM)]
-        + [(planes, HBM)] * 4,
+        [(shape((rows - LEFT, 32), F32), VMEM), (larger, HBM)],
         [VMEM] * 4 + [HBM],
-        [tall, tall, tall, tall, vmem(planes), vmem(messages), pltpu.VMEM((4, 1536, 256), BF16)]
-        + [vmem(spreads), sems(9)],
-        flops=1 << 31, megabytes=18,
+        [tall, tall, tall, tall, vmem(planes), vmem(larger), pltpu.VMEM((4, 1536, 256), BF16)]
+        + [vmem(spreads), pltpu.VMEM((160, 128), F32), sems(6)],
+        flops=1 << 31, megabytes=28,
     )(message, marks, taps_c, taps_d, spread)
     back = lax.all_to_all(back, "slab", 0, 0, tiled=True)
-    (grads_cd,) = call(
-        section_grads_kernel,
-        [(shape((160, 128), BF16), VMEM)],
-        [VMEM] * 3 + [HBM] * 4,
-        [tall, tall, pltpu.VMEM((160, 128), F32)] + [vmem(planes)] * 4 + [sems(4)],
-        flops=1 << 31, megabytes=12,
-    )(message, errors_one, errors_two, *held)
-
-    grads, delta_a = call(
+
+    def in_place(found):
+        moved = lax.ppermute(found[cols:], "gx", up)
+        moved = jnp.where(lax.axis_index("gx") > 0, moved, found[:LEFT])
+        return jnp.concatenate([moved, found[LEFT:cols]], axis=0)
+
+    probability = in_place(probability).reshape(cols, 2, 16)
+    probability = jnp.transpose(probability, (2, 1, 0))
+    back, probability = lax.optimization_barrier((back, probability))
+    hidden_two, band_bt = call(
+        ready_kernel, [(whole, VMEM), (band, VMEM)], [VMEM, HBM], [sems(1)],
+        flops=1 << 31, megabytes=3,
+    )(taps_b, hidden_two)
+
+    half_sums = shape((88, 128), F32)
+    mine, theirs, delta_a = call(
         backward_xy_kernel,
-        [(shape((16, 20, 128), BF16), VMEM), (whole, HBM)],
-        [VMEM] * 3 + [HBM] * 3,
+        [(half_sums, VMEM), (half_sums, VMEM), (whole, HBM)],
+        [VMEM] * 3 + [HBM] * 2,
         [wide, wide, wide, vmem(whole), vmem(whole), pltpu.VMEM((160, 128), F32)]
-        + [vmem(whole), vmem(band), vmem(whole), vmem(whole), sems(13)],
-        flops=1 << 31, megabytes=15,
-    )(back, grads_cd, taps_b, hidden_two, hidden_one, stem)
+        + [vmem(whole), vmem(whole), sems(5)],
+        flops=1 << 31, megabytes=16,
+    )(back, hidden_two, band_bt, hidden_one, stem)
     (stem_grad,) = call(
         stem_grad_kernel,
         [(shape((rows - LEFT, 1024), BF16), VMEM)],
         [HBM, VMEM], [wide, vmem(whole), vmem(band), sems(1)], flops=1 << 30, megabytes=6,
     )(delta_a, taps_a)
 
-    total, stem_grad = sum_everywhere(grads, stem_grad, "slab", "gx")
-
-    def in_place(found):
+    def outermost_last(found):
         moved = lax.ppermute(found[cols:], "gx", up)
-        moved = jnp.where(lax.axis_index("gx") > 0, moved, found[:LEFT])
-        return jnp.concatenate([moved, found[LEFT:cols]], axis=0)
-
-    stem_grad = in_place(stem_grad).reshape(cols, height, C)
-    stem_grad = jnp.transpose(stem_grad, (2, 1, 0))[:, None]
-    probability = in_place(probability).reshape(cols, 2, 16)
-    probability = jnp.transpose(probability, (2, 1, 0))
+        (placed,) = call(
+            place_kernel, [(shape((C, height, cols), BF16), VMEM)], [VMEM, VMEM],
+            [pltpu.VMEM((1024 * cols // 128, 128), F32)], flops=1 << 28, megabytes=4,
+        )(found, moved)
+        return placed
+
+    sums, stem_grad = sum_everywhere(mine, theirs, stem_grad, outermost_last, "slab", "gx")
 
     taps = shape((3, 3, C, C), F32)
     finals = call(
         functools.partial(finish_kernel, 1.0 / (depth * height * cols)),
         [(taps, VMEM)] * 4 + [(shape((1, C), F32), VMEM)] * 2,
-        [VMEM], flops=1 << 20, megabytes=2,
-    )(total)
+        [VMEM] * 3, [pltpu.VMEM((320, 128), F32)], flops=1 << 20, megabytes=2,
+    )(*sums)
     kernels = [jnp.transpose(grad, (2, 0, 1, 3)) for grad in finals[:4]]
-    return (probability, stem_grad, *kernels, finals[4][0], finals[5][0])
+    return (probability, stem_grad[:, None], *kernels, finals[4][0], finals[5][0])
 
 
 def solution(mesh):

time: 122 us -> 118 us (0.967)
  starting transfers between devices: 32.3 us -> 30.4 us
  local copies, waits for them, and re-layouts: 4.16 us -> 2.29 us
    ppermute x0 -> x3, starting transfers between devices: none -> 8.12 us  [the longest x1 3.8 us: outermost_last(): moved = lax.ppermute(found[cols:], 'gx', up)]
    all_to_all x3 -> x2, starting transfers between devices: 17.2 us -> 9.76 us  [the longest x1 5.08 us: sum_everywhere(): lax.all_to_all(spread, gx, 0, 0, tiled=True, axis_index_groups=same_core)]
    all_to_all x3 -> x2, waiting for transfers between devices: 14.4 us -> 7.87 us  [the longest x1 4.27 us: sum_everywhere(): found = lax.all_to_all(spread, slab, 0, 0, tiled=True)]
    all_to_all x1, waiting for transfers between devices: 9.79 us -> 14.6 us  [per_device(): back = lax.all_to_all(back, 'slab', 0, 0, tiled=True)]
    ppermute x2 -> x1, starting transfers between devices: 6.28 us -> 3.67 us  [in_place(): moved = lax.ppermute(found[cols:], 'gx', up)]
    ppermute x0 -> x3, waiting for transfers between devices: none -> 2.1 us  [the longest x1 1 us: outermost_last(): moved = lax.ppermute(found[cols:], 'gx', up)]
    unnamed x14 -> x9, local copies, waits for them, and re-layouts: 2.39 us -> 0.66 us
    pallas_call x8 -> x9, Pallas kernels: 29 us -> 28.7 us  [run(): return bound(*operands)]
  transfers between devices with their start and end apart: 7 -> 8, of which waited for: 4 -> 6; matrix products, arithmetic and copies ran while one was open for 3% -> 1% of each run, Pallas kernels for 11% -> 6%
where the time goes in v4:
time: 118 us; the launch traced here: 117 us
  starting transfers between devices  30.4 us (26%)
  blocking collectives  29.9 us (25%)
  Pallas kernels  28.7 us (24%)
  waiting for transfers between devices  24.6 us (21%)
  local copies, waits for them, and re-layouts  2.29 us (2%)
    all_to_all x1, blocking collectives, per_device(): message = lax.all_to_all(message, 'slab', 0, 0, tiled=True)  29.9 us
    pallas_call x9, Pallas kernels, run(): return bound(*operands)  28.7 us
    all_to_all x1, waiting for transfers between devices, per_device(): back = lax.all_to_all(back, 'slab', 0, 0, tiled=True)  14.6 us
    ppermute x1, starting transfers between devices, per_device(): after = lax.ppermute(initial, 'gx', down)  5.15 us
    all_to_all x1, starting transfers between devices, sum_everywhere(): lax.all_to_all(spread, gx, 0, 0, tiled=True, axis_index_groups=same_core)  5.08 us
    all_to_all x1, starting transfers between devices, sum_everywhere(): found = lax.all_to_all(spread, slab, 0, 0, tiled=True)  4.68 us
    all_to_all x1, waiting for transfers between devices, sum_everywhere(): found = lax.all_to_all(spread, slab, 0, 0, tiled=True)  4.27 us
    ppermute x1, starting transfers between devices, outermost_last(): moved = lax.ppermute(found[cols:], 'gx', up)  3.8 us
  transfers between devices with their start and end apart: 8, of which 6 were waited for; matrix products, arithmetic and copies ran while one was open for 1% of the time, Pallas kernels for 6%

profile of v4, /device:TPU:1, one launch (start us, length us, event | category | flops | bytes accessed | tf_op | source)
XLA Modules:
  0.0 116.9 jit_solution(2128486961531106008)
XLA Ops:
  0.6 1.4 %shard_map.144 = bf16[32,1152]{1,0:T(8,128)(2,1)S(1)} custom-call(bf16[32,32,256]{2,1,0:T(8,128)(2,1)} %bitcast.27, s32[16,2,256]{2,1,0:T(2,128)} %labels_in.3), custom_call_target="tpu_custom_call" | custom-call | flops 268435456 | bytes 1048576 | tf_op jit(solution)/shard_map/pallas_call | solution.py:549
  2.0 5.1 %collective-permute-start = (bf16[32,1152]{1,0:T(8,128)(2,1)S(1)}, bf16[32,1152]{1,0:T(8,128)(2,1)S(1)}, u32[]{:S(2)}, u32[]{:S(2)}) collective-permute-start(bf16[32,1152]{1,0:T(8,128)(2,1)S(1)} %shard_map.144), channel_id=1, source_target_pairs={{1,0},{2,1},{3,2},{4,3},{5,4},{6,5},{7,6},{8,7},{9,8},{10,9},{11,1... | collective-permute-start | bytes 221192 | tf_op jit(solution)/shard_map/ppermute | solution.py:600
  7.2 2.3 %shard_map.143 = (bf16[256,1024]{1,0:T(8,128)(2,1)S(1)}, bf16[256,128]{1,0:T(8,128)(2,1)S(1)}, bf16[1536,256]{1,0:T(8,128)(2,1)S(1)}, bf16[1536,256]{1,0:T(8,128)(2,1)S(1)}, bf16[64,1024]{1,0:T(8,128)(2,1)}) custom-call(bf16[32,32,256]{2,1,0:T(8,128)(2,1)} %bitcast.28, s32[16,2,256]{2,1,0:T(2,128)} %labels_in.3, bf16[3,3,32,32]{3,2,1,0:T(8,128)(2,1)} %bitcast.23, ...), custom_call_target="tpu_custom_call" | custom-call | flops 536870912 | bytes 1048576 | tf_op jit(solution)/shard_map/pallas_call | solution.py:549
  9.5 3.6 %shard_map.145 = (bf16[1,288,1024]{2,1,0:T(8,128)(2,1)}, bf16[1,288,1024]{2,1,0:T(8,128)(2,1)}, bf16[1,288,1024]{2,1,0:T(8,128)(2,1)}, bf16[288,128]{1,0:T(8,128)(2,1)S(1)}, bf16[16,144,128]{2,1,0:T(8,128)(2,1)S(1)}) custom-call(bf16[256,1024]{1,0:T(8,128)(2,1)S(1)} %get-tuple-element.37.stem, bf16[256,128]{1,0:T(8,128)(2,1)S(1)} %get-tuple-element.38.marks, ...), custom_call_target="tpu_custom_call" | custom-call | flops 1073741824 | bytes 1048576 | tf_op jit(solution)/shard_map/pallas_call | solution.py:549
  13.1 29.9 %all_to_all.20.message = bf16[16,144,128]{2,1,0:T(8,128)(2,1)S(1)} all-to-all(bf16[16,144,128]{2,1,0:T(8,128)(2,1)S(1)} %get-tuple-element.41), channel_id=1, replica_groups=mesh['slab'=16,'gx'=16] {'slab'}, dimensions={0} | all-to-all | bytes 1179648 | tf_op jit(solution)/shard_map/all_to_all | solution.py:633
  43.0 10.7 %shard_map.146 = (f32[272,32]{1,0:T(8,128)S(1)}, bf16[16,160,128]{2,1,0:T(8,128)(2,1)}) custom-call(bf16[16,144,128]{2,1,0:T(8,128)(2,1)S(1)} %all_to_all.20.message, bf16[288,128]{1,0:T(8,128)(2,1)S(1)} %get-tuple-element.42.marks, bf16[3,3,32,32]{3,2,1,0:T(8,128)(2,1)S(1)} %bitcast.19, bf16[3,3,32,32]{3,2,1,0:T(8,128)(2,1)S(1)} %bitcast.20, ...), custom_call_target="tpu_custom_call" | custom-call | flops 2147483648 | bytes 1048576 | tf_op jit(solution)/shard_map/pallas_call | solution.py:549
  53.7 3.7 %all-to-all-start.1 = ((bf16[16,160,128]{2,1,0:T(8,128)(2,1)}), bf16[16,160,128]{2,1,0:T(8,128)(2,1)S(1)}, u32[]{:S(2)}, u32[]{:S(2)}) async-start(bf16[16,160,128]{2,1,0:T(8,128)(2,1)} %get-tuple-element.44), calls=%async_computation.1 | async-start | bytes 1310720 | tf_op jit(solution)/shard_map/all_to_all | solution.py:644
  57.5 3.7 %collective-permute-start.1 = (f32[16,32]{1,0:T(8,128)S(1)}, f32[16,32]{1,0:T(8,128)S(1)}, u32[]{:S(2)}, u32[]{:S(2)}) collective-permute-start(f32[16,32]{1,0:T(8,128)S(1)} %slice.18), channel_id=1, source_target_pairs={{0,1},{1,2},{2,3},{3,4},{4,5},{5,6},{6,7},{7,8},{8,9},{9,10},{10,1... | collective-permute-start | bytes 6152 | tf_op jit(solution)/shard_map/ppermute | solution.py:647
  61.2 1.1 shard_map.147
  62.5 14.6 %all-to-all-done.1.back = bf16[16,160,128]{2,1,0:T(8,128)(2,1)S(1)} async-done(((bf16[16,160,128]{2,1,0:T(8,128)(2,1)}), bf16[16,160,128]{2,1,0:T(8,128)(2,1)S(1)}, u32[]{:S(2)}, u32[]{:S(2)}) %all-to-all-start.1) | async-done | bytes 655392 | tf_op jit(solution)/shard_map/all_to_all | solution.py:644
  77.1 4.8 %shard_map.148 = (f32[88,128]{1,0:T(8,128)S(1)}, f32[88,128]{1,0:T(8,128)S(1)}, bf16[1,288,1024]{2,1,0:T(8,128)(2,1)}) custom-call(bf16[16,160,128]{2,1,0:T(8,128)(2,1)S(1)} %all-to-all-done.1.back, bf16[1,288,1024]{2,1,0:T(8,128)(2,1)S(1)} %get-tuple-element.49.hidden_two, bf16[1536,256]{1,0:T(8,128)(2,1)S(1)} %get-tuple-element.50.band_bt, ...), custom_call_target="tpu_custom_call" | custom-call | flops 2147483648 | bytes 1048576 | tf_op jit(solution)/shard_map/pallas_call | solution.py:549
  82.6 0.9 collective-permute-done.2
  83.5 0.7 broadcast_in_dim.23
  84.2 5.1 %all-to-all-start.2 = ((bf16[8,88,128]{2,1,0:T(8,128)(2,1)}), bf16[8,88,128]{2,1,0:T(8,128)(2,1)S(1)}, u32[]{:S(2)}, u32[]{:S(2)}) async-start(bf16[8,88,128]{2,1,0:T(8,128)(2,1)} %broadcast_in_dim.23), calls=%async_computation.2 | async-start | bytes 360448 | tf_op jit(solution)/shard_map/all_to_all | solution.py:573
  89.3 2.2 %shard_map.149.found = bf16[272,1024]{1,0:T(8,128)(2,1)S(1)} custom-call(bf16[1,288,1024]{2,1,0:T(8,128)(2,1)} %get-tuple-element.55.delta_a_in, bf16[3,3,32,32]{3,2,1,0:T(8,128)(2,1)S(1)} %bitcast.24), custom_call_target="tpu_custom_call" | custom-call | flops 1073741824 | bytes 1048576 | tf_op jit(solution)/shard_map/pallas_call | solution.py:549
  91.5 3.6 %all-to-all-done.2 = bf16[8,88,128]{2,1,0:T(8,128)(2,1)S(1)} async-done(((bf16[8,88,128]{2,1,0:T(8,128)(2,1)}), bf16[8,88,128]{2,1,0:T(8,128)(2,1)S(1)}, u32[]{:S(2)}, u32[]{:S(2)}) %all-to-all-start.2) | async-done | bytes 180256 | tf_op jit(solution)/shard_map/all_to_all | solution.py:573
  95.2 0.8 broadcast_in_dim.24
  95.9 4.7 %all-to-all-start.3 = ((bf16[16,88,128]{2,1,0:T(8,128)(2,1)}), bf16[16,88,128]{2,1,0:T(8,128)(2,1)S(1)}, u32[]{:S(2)}, u32[]{:S(2)}) async-start(bf16[16,88,128]{2,1,0:T(8,128)(2,1)} %broadcast_in_dim.24), calls=%async_computation.3 | async-start | bytes 720896 | tf_op jit(solution)/shard_map/all_to_all | solution.py:577
  100.6 3.8 %collective-permute-start.3 = (bf16[16,1024]{1,0:T(8,128)(2,1)S(1)}, bf16[16,1024]{1,0:T(8,128)(2,1)S(1)}, u32[]{:S(2)}, u32[]{:S(2)}) collective-permute-start(bf16[16,1024]{1,0:T(8,128)(2,1)S(1)} %slice.21), channel_id=1, source_target_pairs={{0,1},{1,2},{2,3},{3,4},{4,5},{5,6},{6,7},{7,8},{8,9},{9,10},{10,1... | collective-permute-start | bytes 98312 | tf_op jit(solution)/shard_map/ppermute | solution.py:675
  104.4 1.0 collective-permute-done.3.moved
  105.5 1.6 %shard_map.150 = bf16[32,32,256]{2,1,0:T(8,128)(2,1)} custom-call(bf16[272,1024]{1,0:T(8,128)(2,1)S(1)} %shard_map.149.found, bf16[16,1024]{1,0:T(8,128)(2,1)S(1)} %collective-permute-done.3.moved), custom_call_target="tpu_custom_call" | custom-call | flops 268435456 | bytes 1048576 | tf_op jit(solution)/shard_map/pallas_call | solution.py:549
  107.1 4.3 %all-to-all-done.3 = bf16[16,88,128]{2,1,0:T(8,128)(2,1)S(1)} async-done(((bf16[16,88,128]{2,1,0:T(8,128)(2,1)}), bf16[16,88,128]{2,1,0:T(8,128)(2,1)S(1)}, u32[]{:S(2)}, u32[]{:S(2)}) %all-to-all-start.3) | async-done | bytes 360480 | tf_op jit(solution)/shard_map/all_to_all | solution.py:577
  111.4 3.7 %collective-permute-start.4 = (f32[72,128]{1,0:T(8,128)S(1)}, f32[72,128]{1,0:T(8,128)S(1)}, u32[]{:S(2)}, u32[]{:S(2)}) collective-permute-start(f32[72,128]{1,0:T(8,128)S(1)} %convert_reduce_fusion.mine), channel_id=1, source_target_pairs={{0,1},{1,0},{2,3},{3,2},{4,5},{5,4},{6,7},{7,6},{8,9},{9,8},{10,11... | collective-permute-start | bytes 110600 | tf_op jit(solution)/shard_map/ppermute | solution.py:580
  115.9 1.0 shard_map.151
  (24 shorter events, 1.9 us)
Async XLA Ops:
  2.0 7.4 %collective-permute-start = (bf16[32,1152]{1,0:T(8,128)(2,1)S(1)}, bf16[32,1152]{1,0:T(8,128)(2,1)S(1)}, u32[]{:S(2)}, u32[]{:S(2)}) collective-permute-start(bf16[32,1152]{1,0:T(8,128)(2,1)S(1)} %shard_map.144), channel_id=1, source_target_pairs={{1,0},{2,1},{3,2},{4,3},{5,4},{6,5},{7,6},{8,7},{9,8},{10,9},{11,1... | collective-permute-start | bytes 221192 | tf_op jit(solution)/shard_map/ppermute | solution.py:600
  13.1 29.9 %copy-start = (bf16[32,3,3,32]{3,0,2,1:T(8,128)(2,1)S(1)}, bf16[32,3,3,32]{3,0,2,1:T(8,128)(2,1)}, u32[]{:S(2)}) copy-start(bf16[32,3,3,32]{3,0,2,1:T(8,128)(2,1)} %param.12) | copy-start | bytes 55300
  13.1 29.9 %copy-start.1 = (bf16[32,3,3,32]{3,0,2,1:T(8,128)(2,1)S(1)}, bf16[32,3,3,32]{3,0,2,1:T(8,128)(2,1)}, u32[]{:S(2)}) copy-start(bf16[32,3,3,32]{3,0,2,1:T(8,128)(2,1)} %param.13) | copy-start | bytes 55300
  53.7 7.5 %copy-start.2 = (bf16[32,3,3,32]{3,0,2,1:T(8,128)(2,1)S(1)}, bf16[32,3,3,32]{3,0,2,1:T(8,128)(2,1)}, u32[]{:S(2)}) copy-start(bf16[32,3,3,32]{3,0,2,1:T(8,128)(2,1)} %param.11) | copy-start | bytes 55300
  53.7 23.4 %all-to-all-start.1 = ((bf16[16,160,128]{2,1,0:T(8,128)(2,1)}), bf16[16,160,128]{2,1,0:T(8,128)(2,1)S(1)}, u32[]{:S(2)}, u32[]{:S(2)}) async-start(bf16[16,160,128]{2,1,0:T(8,128)(2,1)} %get-tuple-element.44), calls=%async_computation.1 | async-start | bytes 1310720 | tf_op jit(solution)/shard_map/all_to_all | solution.py:644
  57.5 4.9 %collective-permute-start.1 = (f32[16,32]{1,0:T(8,128)S(1)}, f32[16,32]{1,0:T(8,128)S(1)}, u32[]{:S(2)}, u32[]{:S(2)}) collective-permute-start(f32[16,32]{1,0:T(8,128)S(1)} %slice.18), channel_id=1, source_target_pairs={{0,1},{1,2},{2,3},{3,4},{4,5},{5,6},{6,7},{7,8},{8,9},{9,10},{10,1... | collective-permute-start | bytes 6152 | tf_op jit(solution)/shard_map/ppermute | solution.py:647
  82.0 1.5 %collective-permute-start.2 = (f32[88,128]{1,0:T(8,128)S(1)}, f32[88,128]{1,0:T(8,128)S(1)}, u32[]{:S(2)}, u32[]{:S(2)}) collective-permute-start(f32[88,128]{1,0:T(8,128)S(1)} %get-tuple-element.54), channel_id=1, source_target_pairs={{0,1},{1,0},{2,3},{3,2},{4,5},{5,4},{6,7},{7,6},{8,9},{9,8},{10,11... | collective-permute-start | bytes 135176 | tf_op jit(solution)/shard_map/ppermute | solution.py:570
  84.2 5.1 %copy-start.3 = (bf16[32,3,3,32]{3,0,2,1:T(8,128)(2,1)S(1)}, bf16[32,3,3,32]{3,0,2,1:T(8,128)(2,1)}, u32[]{:S(2)}) copy-start(bf16[32,3,3,32]{3,0,2,1:T(8,128)(2,1)} %param.10) | copy-start | bytes 55300
  84.2 10.9 %all-to-all-start.2 = ((bf16[8,88,128]{2,1,0:T(8,128)(2,1)}), bf16[8,88,128]{2,1,0:T(8,128)(2,1)S(1)}, u32[]{:S(2)}, u32[]{:S(2)}) async-start(bf16[8,88,128]{2,1,0:T(8,128)(2,1)} %broadcast_in_dim.23), calls=%async_computation.2 | async-start | bytes 360448 | tf_op jit(solution)/shard_map/all_to_all | solution.py:573
  95.9 15.4 %all-to-all-start.3 = ((bf16[16,88,128]{2,1,0:T(8,128)(2,1)}), bf16[16,88,128]{2,1,0:T(8,128)(2,1)S(1)}, u32[]{:S(2)}, u32[]{:S(2)}) async-start(bf16[16,88,128]{2,1,0:T(8,128)(2,1)} %broadcast_in_dim.24), calls=%async_computation.3 | async-start | bytes 720896 | tf_op jit(solution)/shard_map/all_to_all | solution.py:577
  100.6 4.8 %collective-permute-start.3 = (bf16[16,1024]{1,0:T(8,128)(2,1)S(1)}, bf16[16,1024]{1,0:T(8,128)(2,1)S(1)}, u32[]{:S(2)}, u32[]{:S(2)}) collective-permute-start(bf16[16,1024]{1,0:T(8,128)(2,1)S(1)} %slice.21), channel_id=1, source_target_pairs={{0,1},{1,2},{2,3},{3,4},{4,5},{5,6},{6,7},{7,8},{8,9},{9,10},{10,1... | collective-permute-start | bytes 98312 | tf_op jit(solution)/shard_map/ppermute | solution.py:675
  111.4 4.5 %collective-permute-start.4 = (f32[72,128]{1,0:T(8,128)S(1)}, f32[72,128]{1,0:T(8,128)S(1)}, u32[]{:S(2)}, u32[]{:S(2)}) collective-permute-start(f32[72,128]{1,0:T(8,128)S(1)} %convert_reduce_fusion.mine), channel_id=1, source_target_pairs={{0,1},{1,0},{2,3},{3,2},{4,5},{5,4},{6,7},{7,6},{8,9},{9,8},{10,11... | collective-permute-start | bytes 110600 | tf_op jit(solution)/shard_map/ppermute | solution.py:580

commit v5 on v4

--- a/solution.py
+++ b/solution.py
@@ -206,8 +206,8 @@
 
 def arrange_kernel(
     stem_in, labels_in, conv_a_in, conv_b_in, head_one_in, head_two_in,
-    stem_out, marks_out, band_a, band_b, spread_out,
-    flat, stem, labels, conv_a, conv_b, heads, spread, sems,
+    stem_out, marks_out, band_a, band_b, spread,
+    flat, stem, labels, conv_a, conv_b, heads, sems,
 ):
     cols = stem.shape[2]
     copies = Copies(sems)
@@ -225,7 +225,6 @@
         four = jnp.concatenate([heads[k].astype(F32)] * 4, axis=1)
         along = jnp.concatenate([four] * 8, axis=1)
         spread[32 * k : 32 * k + 32, :] = jnp.where(same, along, 0.0).astype(BF16)
-    leaving = copies.start(spread, spread_out)
     marks_out[...] = marks_first(labels[...])
     fill_band(conv_a, band_a, 1, False)
     fill_band(conv_b, band_b, 2, False)
@@ -236,7 +235,6 @@
         sides = [columns_first(stem, flat, side, group) for side in range(cols // 128)]
         value = jnp.concatenate(sides, axis=0).astype(BF16)
         stem_out[:, 128 * group : 128 * group + 128] = value
-    leaving.wait()
 
 
 def own_voxel():
@@ -247,34 +245,30 @@
 def forward_xy_kernel(
     stem, marks, after, band_a, band_b,
     stem_frame, hidden_one, hidden_two, marks_out, message,
-    stem_s, one_s, two, sems,
+    stem_s, one_s,
 ):
     _, inside = edge_gates()
-    copies = Copies(sems)
     clear_margins(stem_s)
     clear_margins(one_s)
     for window in range(4):
         lanes = slice(256 * window, 256 * window + 256)
         value = jnp.concatenate([stem[:, lanes], after[:, lanes]], axis=0)
+        stem_frame[0, :, lanes] = value
         store_shifted(stem_s, 0, 256 * window, value.astype(F32), 1)
-    copies.start(centre(stem_s), stem_frame)
     marks_out[...] = jnp.concatenate([marks[...], after[:, 1024:1152]], axis=0)
     for window in range(4):
         value = gated(softplus(conv_window(stem_s, 0, window, band_a)), inside)
+        hidden_one[0, :, 256 * window : 256 * window + 256] = value.astype(BF16)
         store_shifted(one_s, 0, 256 * window, value, 2)
-    copies.start(centre(one_s), hidden_one)
     for window in range(4):
         value = gated(softplus(conv_window(one_s, 0, window, band_b)), inside).astype(BF16)
-        lanes = pl.ds(256 * window, 256)
-        two[0, :, lanes] = value
-        copies.start(two.at[:, :, lanes], hidden_two.at[:, :, lanes])
+        hidden_two[0, :, 256 * window : 256 * window + 256] = value
         half = value.shape[0] // 2
         for peer in range(4):
             lanes = slice(64 * peer, 64 * peer + 64)
             message[4 * window + peer] = jnp.concatenate(
                 [value[:half, lanes], value[half:, lanes]], axis=1
             )
-    wait_all(copies.started)
 
 
 def load_features(message, two_s):
@@ -299,13 +293,11 @@
 
 
 def section_xz_kernel(
-    message, marks, conv_c, conv_d, spread_in,
+    message, marks, conv_c, conv_d, spread,
     probability, back,
-    two_s, ref_one_s, delta_two_s, delta_one_s, ref_two, packed, bands, spread, grads, sems,
+    two_s, ref_one_s, delta_two_s, delta_one_s, ref_two, bands, grads,
 ):
     left, inside = edge_gates()
-    copies = Copies(sems)
-    spread_here = copies.start(spread_in, spread)
     band_c, band_d, band_dt, band_ct = [bands.at[k] for k in range(4)]
     rows = marks.shape[0]
     half = rows // 2
@@ -324,7 +316,6 @@
     fill_band(conv_d, band_dt, 2, True)
 
     labels = marks[:, 0:32].astype(F32)
-    spread_here.wait()
     spread_one, spread_two = spread[0:32, :], spread[32:64, :]
     first, second = None, None
     for plane in range(2):
@@ -372,17 +363,13 @@
             values.append(value.astype(BF16))
         for z in range(8):
             lanes = slice(32 * z, 32 * z + 32)
-            packed[8 * window + z, :half] = jnp.concatenate(
+            back[8 * window + z, :half] = jnp.concatenate(
                 [
                     values[0][:half, lanes], values[1][:half, lanes],
                     values[0][half:, lanes], values[1][half:, lanes],
                 ],
                 axis=1,
             )
-        for part in range(2):
-            peers = pl.ds(8 * window + 4 * part, 4)
-            rows_sent = pl.ds(0, half)
-            copies.start(packed.at[peers, rows_sent], back.at[peers, rows_sent])
 
     same = own_voxel()
     same = jnp.concatenate([same, same], axis=0)
@@ -412,28 +399,16 @@
     blank = jnp.zeros((6, 128), F32)
     for peer in range(16):
         chunk = jnp.concatenate([grads[10 * peer : 10 * peer + 10, :], blank], axis=0)
-        packed[peer, half : half + 16, :] = chunk.astype(BF16)
-    rows_sent = pl.ds(half, 16)
-    copies.start(packed.at[:, rows_sent], back.at[:, rows_sent])
-    wait_all(copies.started[1:])
-
-
-def ready_kernel(conv_b, hidden_two_in, hidden_two, band_bt, sems):
-    copies = Copies(sems)
-    copies.start(hidden_two_in, hidden_two)
-    fill_band(conv_b, band_bt, 2, True)
-    wait_all(copies.started)
+        back[peer, half : half + 16, :] = chunk.astype(BF16)
 
 
 def backward_xy_kernel(
-    back, hidden_two, band_bt, hidden_one_in, stem_in,
-    mine_out, theirs_out, delta_a_out,
-    one_s, stem_s, delta_b_s, delta_b, delta_a, grads, hidden_one, stem, sems,
+    back, hidden_two, hidden_one, stem, conv_b,
+    mine_out, theirs_out, delta_a,
+    one_s, stem_s, delta_b_s, delta_b, grads, band_bt,
 ):
     first, inside = edge_gates()
-    copies = Copies(sems)
-    one_here = copies.start_lanes(hidden_one_in, hidden_one, 2)
-    stem_here = copies.start_lanes(stem_in, stem, 2)
+    fill_band(conv_b, band_bt, 2, True)
     for shifted in (one_s, stem_s, delta_b_s):
         clear_margins(shifted)
     half = back.shape[1] - 16
@@ -451,7 +426,6 @@
         value = gated(value * slope(hidden_two[0, :, lanes]), inside)
         delta_b[0, :, lanes] = value.astype(BF16)
         store_shifted(delta_b_s, 0, 128 * group, value, 2)
-    wait_all(one_here)
     for window in range(4):
         at = 256 * window
         value = conv_window(delta_b_s, 0, window, band_bt)
@@ -459,8 +433,6 @@
         value = gated(value * slope(stored), inside)
         delta_a[0, :, at : at + 256] = value.astype(BF16)
         store_shifted(one_s, 0, at, stored.astype(F32), 2)
-    leaving = copies.start(delta_a, delta_a_out)
-    wait_all(stem_here)
     for window in range(4):
         lanes = slice(256 * window, 256 * window + 256)
         store_shifted(stem_s, 0, 256 * window, stem[0, :, lanes].astype(F32), 1)
@@ -477,31 +449,36 @@
     theirs_out[0:72, :] = grads[pl.ds(pl.multiple_of(72 * (1 - core), 8), 72), :]
     mine_out[72:88, :] = chunk
     theirs_out[72:88, :] = chunk
-    leaving.wait()
-
-
-def stem_grad_kernel(delta_a_in, conv_a, stem_grad, delta_a_s, delta_a, band_at, sems):
-    copies = Copies(sems)
-    copies.start(delta_a_in, delta_a)
+
+
+def stem_grad_kernel(delta_a, probability, conv_a, stem_grad, leaving, delta_a_s, band_at):
     rows = delta_a.shape[1]
+    tail = slice(rows - 2 * LEFT, rows - LEFT)
     clear_margins(delta_a_s)
     fill_band(conv_a, band_at, 1, True)
-    wait_all(copies.started)
     for window in range(4):
         lanes = slice(256 * window, 256 * window + 256)
         store_shifted(delta_a_s, 0, 256 * window, delta_a[0, :, lanes].astype(F32), 1)
     for window in range(4):
-        at = 256 * window
-        value = conv_window(delta_a_s, 0, window, band_at)
-        stem_grad[:, at : at + 256] = value[: rows - LEFT].astype(BF16)
-
-
-def place_kernel(found, moved, stem_grad, flat):
+        lanes = slice(256 * window, 256 * window + 256)
+        value = conv_window(delta_a_s, 0, window, band_at).astype(BF16)
+        stem_grad[:, lanes] = value[: rows - 2 * LEFT]
+        leaving[:, lanes] = value[tail]
+    rest = probability[tail, :]
+    parts = []
+    for _ in range(3):
+        parts.append(rest.astype(BF16))
+        rest = rest - parts[-1].astype(F32)
+    parts.append(jnp.zeros((LEFT, 32), BF16))
+    leaving[:, 1024:1152] = jnp.concatenate(parts, axis=1)
+
+
+def place_kernel(found, probability, moved, stem_grad, share, flat):
     cols = stem_grad.shape[2]
     first, _ = edge_gates()
     for group in range(8):
         lanes = slice(128 * group, 128 * group + 128)
-        mine = found[:cols, lanes].astype(F32)
+        mine = found[:, lanes].astype(F32)
         head = mine[:LEFT] * first + moved[:, lanes].astype(F32) * (1.0 - first)
         value = jnp.concatenate([head, mine[LEFT:]], axis=0)
         for side in range(cols // 128):
@@ -512,29 +489,45 @@
     for side in range(cols // 128):
         part = flat[1024 * side : 1024 * side + 1024, :].reshape(32, 32, 128)
         stem_grad[:, :, 128 * side : 128 * side + 128] = part.astype(BF16)
-
-
-def finish_kernel(factor, mine, theirs, chunks, grad_a, grad_b, grad_c, grad_d, head_one, head_two, flat):
+    parts = moved[:, 1024:1152].astype(F32)
+    head = parts[:, 0:32] + parts[:, 32:64] + parts[:, 64:96]
+    head = probability[:LEFT, :] * first + head * (1.0 - first)
+    value = jnp.concatenate([head, probability[LEFT:cols, :]], axis=0).T
+    share[:, 0, :] = value[0:16]
+    share[:, 1, :] = value[16:32]
+
+
+def finish_cd_kernel(factor, chunks, grad_c, grad_d, head_one, head_two, flat):
+    for peer in range(16):
+        flat[10 * peer : 10 * peer + 10, :] = chunks[peer, 0:10, :].astype(F32) * factor
+
+    def piece(index):
+        row, lane = 32 * (index // 4), 32 * (index % 4)
+        return flat[row : row + 32, lane : lane + 32]
+
+    for tap in range(9):
+        grad_c[tap // 3, tap % 3] = piece(tap)
+        grad_d[tap // 3, tap % 3] = piece(9 + tap)
+    head_one[...] = piece(18)[0:1]
+    head_two[...] = piece(19)[0:1]
+
+
+def finish_ab_kernel(factor, mine, theirs, grad_a, grad_b, flat):
     core = lax.rem(lax.axis_index("gx"), 2)
     flat[pl.ds(pl.multiple_of(72 * core, 8), 72), :] = mine[...] * factor
     flat[pl.ds(pl.multiple_of(72 * (1 - core), 8), 72), :] = theirs[...] * factor
-    for peer in range(16):
-        flat[160 + 10 * peer : 170 + 10 * peer, :] = chunks[peer, 0:10, :].astype(F32) * factor
-
-    def piece(pair, index):
-        row, lane = 160 * pair + 32 * (index // 4), 32 * (index % 4)
-        if pair == 0 and index >= 16:
+
+    def piece(index):
+        row, lane = 32 * (index // 4), 32 * (index % 4)
+        if index >= 16:
             lane = 64 * (index % 4)
             halves = [flat[row : row + 16, lane + at : lane + at + 32] for at in (0, 32)]
             return jnp.concatenate(halves, axis=0)
         return flat[row : row + 32, lane : lane + 32]
 
-    for pair, (near, far) in enumerate(((grad_a, grad_b), (grad_c, grad_d))):
-        for tap in range(9):
-            near[tap // 3, tap % 3] = piece(pair, tap)
-            far[tap // 3, tap % 3] = piece(pair, 9 + tap)
-    head_one[...] = piece(1, 18)[0:1]
-    head_two[...] = piece(1, 19)[0:1]
+    for tap in range(9):
+        grad_a[tap // 3, tap % 3] = piece(tap)
+        grad_b[tap // 3, tap % 3] = piece(9 + tap)
 
 
 def call(kernel, outs, ins, scratch=(), flops=0, megabytes=16):
@@ -611,11 +604,11 @@
             (shape((cols, 128), BF16), VMEM),
             (band, VMEM),
             (band, VMEM),
-            (spreads, HBM),
+            (spreads, VMEM),
         ],
         [HBM] * 6,
         [pltpu.VMEM((1024 * cols // 128, 128), F32), vmem(stem_features), vmem(labels)]
-        + [vmem(taps_a), vmem(taps_b), pltpu.VMEM((2, 1, C), BF16), vmem(spreads), sems(10)],
+        + [vmem(taps_a), vmem(taps_b), pltpu.VMEM((2, 1, C), BF16), sems(9)],
         flops=1 << 29, megabytes=6,
     )(stem_features, labels, taps_a, taps_b, head_one[None], head_two[None])
 
@@ -626,69 +619,64 @@
     messages = shape((16, half, 128), BF16)
     stem, hidden_one, hidden_two, marks, message = call(
         forward_xy_kernel,
-        [(whole, HBM)] * 3 + [(shape((rows, 128), BF16), VMEM), (messages, VMEM)],
+        [(whole, VMEM)] * 3 + [(shape((rows, 128), BF16), VMEM), (messages, VMEM)],
         [VMEM] * 5,
-        [wide, wide, vmem(whole), sems(6)], flops=1 << 30, megabytes=8,
+        [wide, wide], flops=1 << 30, megabytes=8,
     )(stem, marks, after, band_a, band_b)
     message = lax.all_to_all(message, "slab", 0, 0, tiled=True)
 
     larger = shape((16, half + 16, 128), BF16)
     probability, back = call(
         section_xz_kernel,
-        [(shape((rows - LEFT, 32), F32), VMEM), (larger, HBM)],
-        [VMEM] * 4 + [HBM],
-        [tall, tall, tall, tall, vmem(planes), vmem(larger), pltpu.VMEM((4, 1536, 256), BF16)]
-        + [vmem(spreads), pltpu.VMEM((160, 128), F32), sems(6)],
+        [(shape((rows - LEFT, 32), F32), VMEM), (larger, VMEM)],
+        [VMEM] * 5,
+        [tall, tall, tall, tall, vmem(planes), pltpu.VMEM((4, 1536, 256), BF16)]
+        + [pltpu.VMEM((160, 128), F32)],
         flops=1 << 31, megabytes=28,
     )(message, marks, taps_c, taps_d, spread)
     back = lax.all_to_all(back, "slab", 0, 0, tiled=True)
 
-    def in_place(found):
-        moved = lax.ppermute(found[cols:], "gx", up)
-        moved = jnp.where(lax.axis_index("gx") > 0, moved, found[:LEFT])
-        return jnp.concatenate([moved, found[LEFT:cols]], axis=0)
-
-    probability = in_place(probability).reshape(cols, 2, 16)
-    probability = jnp.transpose(probability, (2, 1, 0))
-    back, probability = lax.optimization_barrier((back, probability))
-    hidden_two, band_bt = call(
-        ready_kernel, [(whole, VMEM), (band, VMEM)], [VMEM, HBM], [sems(1)],
-        flops=1 << 31, megabytes=3,
-    )(taps_b, hidden_two)
-
     half_sums = shape((88, 128), F32)
     mine, theirs, delta_a = call(
         backward_xy_kernel,
-        [(half_sums, VMEM), (half_sums, VMEM), (whole, HBM)],
-        [VMEM] * 3 + [HBM] * 2,
-        [wide, wide, wide, vmem(whole), vmem(whole), pltpu.VMEM((160, 128), F32)]
-        + [vmem(whole), vmem(whole), sems(5)],
+        [(half_sums, VMEM), (half_sums, VMEM), (whole, VMEM)],
+        [VMEM] * 5,
+        [wide, wide, wide, vmem(whole), pltpu.VMEM((160, 128), F32), vmem(band)],
         flops=1 << 31, megabytes=16,
-    )(back, hidden_two, band_bt, hidden_one, stem)
-    (stem_grad,) = call(
+    )(back, hidden_two, hidden_one, stem, taps_b)
+    edge = shape((LEFT, 1152), BF16)
+    beside = call(
         stem_grad_kernel,
-        [(shape((rows - LEFT, 1024), BF16), VMEM)],
-        [HBM, VMEM], [wide, vmem(whole), vmem(band), sems(1)], flops=1 << 30, megabytes=6,
-    )(delta_a, taps_a)
-
-    def outermost_last(found):
-        moved = lax.ppermute(found[cols:], "gx", up)
-        (placed,) = call(
-            place_kernel, [(shape((C, height, cols), BF16), VMEM)], [VMEM, VMEM],
-            [pltpu.VMEM((1024 * cols // 128, 128), F32)], flops=1 << 28, megabytes=4,
-        )(found, moved)
-        return placed
-
-    sums, stem_grad = sum_everywhere(mine, theirs, stem_grad, outermost_last, "slab", "gx")
+        [(shape((cols, 1024), BF16), VMEM), (edge, VMEM)],
+        [VMEM] * 3, [wide, vmem(band)], flops=1 << 30, megabytes=6,
+    )(delta_a, probability, taps_a)
+
+    def place(beside):
+        found, leaving = beside
+        moved = lax.ppermute(leaving, "gx", up)
+        return call(
+            place_kernel,
+            [(shape((C, height, cols), BF16), VMEM), (shape((16, 2, cols), F32), VMEM)],
+            [VMEM] * 3, [pltpu.VMEM((1024 * cols // 128, 128), F32)], flops=1 << 28, megabytes=4,
+        )(found, probability, moved)
+
+    (mine, theirs, chunks), (stem_grad, probability) = sum_everywhere(
+        mine, theirs, beside, place, "slab", "gx"
+    )
 
     taps = shape((3, 3, C, C), F32)
-    finals = call(
-        functools.partial(finish_kernel, 1.0 / (depth * height * cols)),
-        [(taps, VMEM)] * 4 + [(shape((1, C), F32), VMEM)] * 2,
-        [VMEM] * 3, [pltpu.VMEM((320, 128), F32)], flops=1 << 20, megabytes=2,
-    )(*sums)
-    kernels = [jnp.transpose(grad, (2, 0, 1, 3)) for grad in finals[:4]]
-    return (probability, stem_grad[:, None], *kernels, finals[4][0], finals[5][0])
+    head = shape((1, C), F32)
+    factor = 1.0 / (depth * height * cols)
+    grad_c, grad_d, grad_one, grad_two = call(
+        functools.partial(finish_cd_kernel, factor), [(taps, VMEM)] * 2 + [(head, VMEM)] * 2,
+        [VMEM], [pltpu.VMEM((160, 128), F32)], flops=1 << 24, megabytes=2,
+    )(chunks)
+    grad_a, grad_b = call(
+        functools.partial(finish_ab_kernel, factor), [(taps, VMEM)] * 2,
+        [VMEM] * 2, [pltpu.VMEM((144, 128), F32)], flops=1 << 20, megabytes=2,
+    )(mine, theirs)
+    kernels = [jnp.transpose(grad, (2, 0, 1, 3)) for grad in (grad_a, grad_b, grad_c, grad_d)]
+    return (probability, stem_grad[:, None], *kernels, grad_one[0], grad_two[0])
 
 
 def solution(mesh):

time: 118 us -> 114 us (0.966)
  blocking collectives: 29.9 us -> 51.9 us
  waiting for transfers between devices: 24.6 us -> 10.7 us
  starting transfers between devices: 30.4 us -> 24.1 us
  Pallas kernels: 28.7 us -> 24.6 us
    all_to_all x0 -> x1, blocking collectives: none -> 22 us  [per_device(): back = lax.all_to_all(back, 'slab', 0, 0, tiled=True)]
    all_to_all x1 -> x0, waiting for transfers between devices: 14.6 us -> none  [per_device(): back = lax.all_to_all(back, 'slab', 0, 0, tiled=True)]
    pallas_call x9, Pallas kernels: 28.7 us -> 24.6 us  [run(): return bound(*operands)]
    all_to_all x1 -> x0, starting transfers between devices: 3.74 us -> none  [per_device(): back = lax.all_to_all(back, 'slab', 0, 0, tiled=True)]
    ppermute x2 -> x1, starting transfers between devices: 7.46 us -> 3.8 us  [place(): moved = lax.ppermute(leaving, 'gx', up)]
    ppermute x1, starting transfers between devices: 0.66 us -> 2.73 us  [sum_everywhere(): mine = mine + lax.ppermute(theirs, gx, swap)]
  transfers between devices with their start and end apart: 8 -> 6, of which waited for: 6 -> 4; matrix products, arithmetic and copies ran while one was open for 1% -> 0% of each run, Pallas kernels for 6% -> 5%
where the time goes in v5:
time: 114 us
  blocking collectives  51.9 us (46%)
  Pallas kernels  24.6 us (22%)
  starting transfers between devices  24.1 us (21%)
  waiting for transfers between devices  10.7 us (9%)
  local copies, waits for them, and re-layouts  1.5 us (1%)
    all_to_all x1, blocking collectives, per_device(): message = lax.all_to_all(message, 'slab', 0, 0, tiled=True)  29.9 us
    pallas_call x9, Pallas kernels, run(): return bound(*operands)  24.6 us
    all_to_all x1, blocking collectives, per_device(): back = lax.all_to_all(back, 'slab', 0, 0, tiled=True)  22 us
    all_to_all x1, starting transfers between devices, sum_everywhere(): lax.all_to_all(spread, gx, 0, 0, tiled=True, axis_index_groups=same_core)  5.17 us
    ppermute x1, starting transfers between devices, per_device(): after = lax.ppermute(initial, 'gx', down)  5.15 us
    all_to_all x1, waiting for transfers between devices, sum_everywhere(): lax.all_to_all(spread, gx, 0, 0, tiled=True, axis_index_groups=same_core)  4.57 us
    all_to_all x1, waiting for transfers between devices, sum_everywhere(): found = lax.all_to_all(spread, slab, 0, 0, tiled=True)  4.17 us
    ppermute x1, starting transfers between devices, place(): moved = lax.ppermute(leaving, 'gx', up)  3.8 us
  transfers between devices with their start and end apart: 6, of which 4 were waited for; matrix products, arithmetic and copies ran while one was open for 0% of the time, Pallas kernels for 5%

profile of v5, /device:TPU:1, one launch (start us, length us, event | category | flops | bytes accessed | tf_op | source)
XLA Modules:
  0.0 113.5 jit_solution(121558704972543474)
XLA Ops:
  0.6 1.4 %shard_map.144 = bf16[32,1152]{1,0:T(8,128)(2,1)S(1)} custom-call(bf16[32,32,256]{2,1,0:T(8,128)(2,1)} %bitcast.22, s32[16,2,256]{2,1,0:T(2,128)} %labels_in.3), custom_call_target="tpu_custom_call" | custom-call | flops 268435456 | bytes 1048576 | tf_op jit(solution)/shard_map/pallas_call | solution.py:542
  2.0 5.1 %collective-permute-start = (bf16[32,1152]{1,0:T(8,128)(2,1)S(1)}, bf16[32,1152]{1,0:T(8,128)(2,1)S(1)}, u32[]{:S(2)}, u32[]{:S(2)}) collective-permute-start(bf16[32,1152]{1,0:T(8,128)(2,1)S(1)} %shard_map.144), channel_id=1, source_target_pairs={{1,0},{2,1},{3,2},{4,3},{5,4},{6,5},{7,6},{8,7},{9,8},{10,9},{11,1... | collective-permute-start | bytes 221192 | tf_op jit(solution)/shard_map/ppermute | solution.py:593
  7.2 2.3 %shard_map.143 = (bf16[256,1024]{1,0:T(8,128)(2,1)S(1)}, bf16[256,128]{1,0:T(8,128)(2,1)S(1)}, bf16[1536,256]{1,0:T(8,128)(2,1)S(1)}, bf16[1536,256]{1,0:T(8,128)(2,1)S(1)}, bf16[64,1024]{1,0:T(8,128)(2,1)S(1)}) custom-call(bf16[32,32,256]{2,1,0:T(8,128)(2,1)} %bitcast.23, s32[16,2,256]{2,1,0:T(2,128)} %labels_in.3, bf16[3,3,32,32]{3,2,1,0:T(8,128)(2,1)} %bitcast.20, ...), custom_call_target="tpu_custom_call" | custom-call | flops 536870912 | bytes 1048576 | tf_op jit(solution)/shard_map/pallas_call | solution.py:542
  9.4 2.9 %shard_map.145 = (bf16[1,288,1024]{2,1,0:T(8,128)(2,1)S(1)}, bf16[1,288,1024]{2,1,0:T(8,128)(2,1)S(1)}, bf16[1,288,1024]{2,1,0:T(8,128)(2,1)S(1)}, bf16[288,128]{1,0:T(8,128)(2,1)S(1)}, bf16[16,144,128]{2,1,0:T(8,128)(2,1)S(1)}) custom-call(bf16[256,1024]{1,0:T(8,128)(2,1)S(1)} %get-tuple-element.39.stem, bf16[256,128]{1,0:T(8,128)(2,1)S(1)} %get-tuple-element.40.marks, ...), custom_call_target="tpu_custom_call" | custom-call | flops 1073741824 | bytes 1048576 | tf_op jit(solution)/shard_map/pallas_call | solution.py:542
  12.4 29.9 %all_to_all.20.message = bf16[16,144,128]{2,1,0:T(8,128)(2,1)S(1)} all-to-all(bf16[16,144,128]{2,1,0:T(8,128)(2,1)S(1)} %get-tuple-element.43), channel_id=1, replica_groups=mesh['slab'=16,'gx'=16] {'slab'}, dimensions={0} | all-to-all | bytes 1179648 | tf_op jit(solution)/shard_map/all_to_all | solution.py:626
  42.3 9.1 %shard_map.146 = (f32[272,32]{1,0:T(8,128)S(1)}, bf16[16,160,128]{2,1,0:T(8,128)(2,1)S(1)}) custom-call(bf16[16,144,128]{2,1,0:T(8,128)(2,1)S(1)} %all_to_all.20.message, bf16[288,128]{1,0:T(8,128)(2,1)S(1)} %get-tuple-element.44.marks, bf16[3,3,32,32]{3,2,1,0:T(8,128)(2,1)S(1)} %bitcast.16, bf16[3,3,32,32]{3,2,1,0:T(8,128)(2,1)S(1)} %bitcast.17, ...), custom_call_target="tpu_custom_call" | custom-call | flops 2147483648 | bytes 1048576 | tf_op jit(solution)/shard_map/pallas_call | solution.py:542
  51.4 22.0 %all_to_all.21.back = bf16[16,160,128]{2,1,0:T(8,128)(2,1)S(1)} all-to-all(bf16[16,160,128]{2,1,0:T(8,128)(2,1)S(1)} %get-tuple-element.46), channel_id=1, replica_groups=mesh['slab'=16,'gx'=16] {'slab'}, dimensions={0} | all-to-all | bytes 1310720 | tf_op jit(solution)/shard_map/all_to_all | solution.py:637
  73.4 4.3 %shard_map.147 = (f32[88,128]{1,0:T(8,128)S(1)}, f32[88,128]{1,0:T(8,128)S(1)}, bf16[1,288,1024]{2,1,0:T(8,128)(2,1)S(1)}) custom-call(bf16[16,160,128]{2,1,0:T(8,128)(2,1)S(1)} %all_to_all.21.back, bf16[1,288,1024]{2,1,0:T(8,128)(2,1)S(1)} %get-tuple-element.47.hidden_two, bf16[1,288,1024]{2,1,0:T(8,128)(2,1)S(1)} %get-tuple-element.48.hidden_one, ...), custom_call_target="tpu_custom_call" | custom-call | flops 2147483648 | bytes 1048576 | tf_op jit(solution)/shard_map/pallas_call | solution.py:542
  77.7 2.7 %collective-permute-start.1 = (f32[88,128]{1,0:T(8,128)S(1)}, f32[88,128]{1,0:T(8,128)S(1)}, u32[]{:S(2)}, u32[]{:S(2)}) collective-permute-start(f32[88,128]{1,0:T(8,128)S(1)} %get-tuple-element.51), channel_id=1, source_target_pairs={{0,1},{1,0},{2,3},{3,2},{4,5},{5,4},{6,7},{7,6},{8,9},{9,8},{10,11... | collective-permute-start | bytes 135176 | tf_op jit(solution)/shard_map/ppermute | solution.py:563
  80.4 0.9 collective-permute-done.1
  81.3 0.7 broadcast_in_dim.23
  82.0 5.2 %all-to-all-start.2 = ((bf16[8,88,128]{2,1,0:T(8,128)(2,1)}), bf16[8,88,128]{2,1,0:T(8,128)(2,1)S(1)}, u32[]{:S(2)}, u32[]{:S(2)}) async-start(bf16[8,88,128]{2,1,0:T(8,128)(2,1)} %broadcast_in_dim.23), calls=%async_computation.2 | async-start | bytes 360448 | tf_op jit(solution)/shard_map/all_to_all | solution.py:566
  87.2 1.3 %shard_map.148 = (bf16[256,1024]{1,0:T(8,128)(2,1)S(1)}, bf16[16,1152]{1,0:T(8,128)(2,1)S(1)}) custom-call(bf16[1,288,1024]{2,1,0:T(8,128)(2,1)S(1)} %get-tuple-element.52.delta_a, f32[272,32]{1,0:T(8,128)S(1)} %get-tuple-element.53.probability, bf16[3,3,32,32]{3,2,1,0:T(8,128)(2,1)S(1)} %bitcast.21), custom_call_target="tpu_custom_call" | custom-call | flops 1073741824 | bytes 1048576 | tf_op jit(solution)/shard_map/pallas_call | solution.py:542
  88.5 4.6 %all-to-all-done.2 = bf16[8,88,128]{2,1,0:T(8,128)(2,1)S(1)} async-done(((bf16[8,88,128]{2,1,0:T(8,128)(2,1)}), bf16[8,88,128]{2,1,0:T(8,128)(2,1)S(1)}, u32[]{:S(2)}, u32[]{:S(2)}) %all-to-all-start.2) | async-done | bytes 180256 | tf_op jit(solution)/shard_map/all_to_all | solution.py:566
  93.1 0.8 broadcast_in_dim.24
  93.8 3.6 %all-to-all-start.3 = ((bf16[16,88,128]{2,1,0:T(8,128)(2,1)}), bf16[16,88,128]{2,1,0:T(8,128)(2,1)S(1)}, u32[]{:S(2)}, u32[]{:S(2)}) async-start(bf16[16,88,128]{2,1,0:T(8,128)(2,1)} %broadcast_in_dim.24), calls=%async_computation.3 | async-start | bytes 720896 | tf_op jit(solution)/shard_map/all_to_all | solution.py:570
  97.4 3.8 %collective-permute-start.2 = (bf16[16,1152]{1,0:T(8,128)(2,1)S(1)}, bf16[16,1152]{1,0:T(8,128)(2,1)S(1)}, u32[]{:S(2)}, u32[]{:S(2)}) collective-permute-start(bf16[16,1152]{1,0:T(8,128)(2,1)S(1)} %get-tuple-element.58), channel_id=1, source_target_pairs={{0,1},{1,2},{2,3},{3,4},{4,5},{5,6},{6,7},{7,8},{8,9},{9,10},{10,1... | collective-permute-start | bytes 110600 | tf_op jit(solution)/shard_map/ppermute | solution.py:656
  101.2 1.0 collective-permute-done.2.moved
  102.3 1.7 %shard_map.149 = (bf16[32,32,256]{2,1,0:T(8,128)(2,1)}, f32[16,2,256]{2,1,0:T(2,128)}) custom-call(bf16[256,1024]{1,0:T(8,128)(2,1)S(1)} %get-tuple-element.57.found, f32[272,32]{1,0:T(8,128)S(1)} %get-tuple-element.53.probability, bf16[16,1152]{1,0:T(8,128)(2,1)S(1)} %collective-permute-done.2.moved), custom_call_target="tpu_custom_call" | custom-call | flops 268435456 | bytes 1048576 | tf_op jit(solution)/shard_map/pallas_call | solution.py:542
  104.0 4.2 %all-to-all-done.3 = bf16[16,88,128]{2,1,0:T(8,128)(2,1)S(1)} async-done(((bf16[16,88,128]{2,1,0:T(8,128)(2,1)}), bf16[16,88,128]{2,1,0:T(8,128)(2,1)S(1)}, u32[]{:S(2)}, u32[]{:S(2)}) %all-to-all-start.3) | async-done | bytes 360480 | tf_op jit(solution)/shard_map/all_to_all | solution.py:570
  108.2 3.7 %collective-permute-start.3 = (f32[72,128]{1,0:T(8,128)S(1)}, f32[72,128]{1,0:T(8,128)S(1)}, u32[]{:S(2)}, u32[]{:S(2)}) collective-permute-start(f32[72,128]{1,0:T(8,128)S(1)} %convert_reduce_fusion.mine), channel_id=1, source_target_pairs={{0,1},{1,0},{2,3},{3,2},{4,5},{5,4},{6,7},{7,6},{8,9},{9,8},{10,11... | collective-permute-start | bytes 110600 | tf_op jit(solution)/shard_map/ppermute | solution.py:573
  111.8 0.8 shard_map.151
  112.7 0.0 collective-permute-done.3.theirs
  112.7 0.8 shard_map.150
  (13 shorter events, 0.1 us)
Async XLA Ops:
  2.0 7.4 %collective-permute-start = (bf16[32,1152]{1,0:T(8,128)(2,1)S(1)}, bf16[32,1152]{1,0:T(8,128)(2,1)S(1)}, u32[]{:S(2)}, u32[]{:S(2)}) collective-permute-start(bf16[32,1152]{1,0:T(8,128)(2,1)S(1)} %shard_map.144), channel_id=1, source_target_pairs={{1,0},{2,1},{3,2},{4,3},{5,4},{6,5},{7,6},{8,7},{9,8},{10,9},{11,1... | collective-permute-start | bytes 221192 | tf_op jit(solution)/shard_map/ppermute | solution.py:593
  12.4 29.9 %copy-start = (bf16[32,3,3,32]{3,0,2,1:T(8,128)(2,1)S(1)}, bf16[32,3,3,32]{3,0,2,1:T(8,128)(2,1)}, u32[]{:S(2)}) copy-start(bf16[32,3,3,32]{3,0,2,1:T(8,128)(2,1)} %param.12) | copy-start | bytes 55300
  12.4 29.9 %copy-start.1 = (bf16[32,3,3,32]{3,0,2,1:T(8,128)(2,1)S(1)}, bf16[32,3,3,32]{3,0,2,1:T(8,128)(2,1)}, u32[]{:S(2)}) copy-start(bf16[32,3,3,32]{3,0,2,1:T(8,128)(2,1)} %param.13) | copy-start | bytes 55300
  51.4 22.1 %copy-start.2 = (bf16[32,3,3,32]{3,0,2,1:T(8,128)(2,1)S(1)}, bf16[32,3,3,32]{3,0,2,1:T(8,128)(2,1)}, u32[]{:S(2)}) copy-start(bf16[32,3,3,32]{3,0,2,1:T(8,128)(2,1)} %param.11) | copy-start | bytes 55300
  77.7 3.6 %collective-permute-start.1 = (f32[88,128]{1,0:T(8,128)S(1)}, f32[88,128]{1,0:T(8,128)S(1)}, u32[]{:S(2)}, u32[]{:S(2)}) collective-permute-start(f32[88,128]{1,0:T(8,128)S(1)} %get-tuple-element.51), channel_id=1, source_target_pairs={{0,1},{1,0},{2,3},{3,2},{4,5},{5,4},{6,7},{7,6},{8,9},{9,8},{10,11... | collective-permute-start | bytes 135176 | tf_op jit(solution)/shard_map/ppermute | solution.py:563
  82.0 5.2 %copy-start.3 = (bf16[32,3,3,32]{3,0,2,1:T(8,128)(2,1)S(1)}, bf16[32,3,3,32]{3,0,2,1:T(8,128)(2,1)}, u32[]{:S(2)}) copy-start(bf16[32,3,3,32]{3,0,2,1:T(8,128)(2,1)} %param.10) | copy-start | bytes 55300
  82.0 11.0 %all-to-all-start.2 = ((bf16[8,88,128]{2,1,0:T(8,128)(2,1)}), bf16[8,88,128]{2,1,0:T(8,128)(2,1)S(1)}, u32[]{:S(2)}, u32[]{:S(2)}) async-start(bf16[8,88,128]{2,1,0:T(8,128)(2,1)} %broadcast_in_dim.23), calls=%async_computation.2 | async-start | bytes 360448 | tf_op jit(solution)/shard_map/all_to_all | solution.py:566
  93.8 14.3 %all-to-all-start.3 = ((bf16[16,88,128]{2,1,0:T(8,128)(2,1)}), bf16[16,88,128]{2,1,0:T(8,128)(2,1)S(1)}, u32[]{:S(2)}, u32[]{:S(2)}) async-start(bf16[16,88,128]{2,1,0:T(8,128)(2,1)} %broadcast_in_dim.24), calls=%async_computation.3 | async-start | bytes 720896 | tf_op jit(solution)/shard_map/all_to_all | solution.py:570
  97.4 4.8 %collective-permute-start.2 = (bf16[16,1152]{1,0:T(8,128)(2,1)S(1)}, bf16[16,1152]{1,0:T(8,128)(2,1)S(1)}, u32[]{:S(2)}, u32[]{:S(2)}) collective-permute-start(bf16[16,1152]{1,0:T(8,128)(2,1)S(1)} %get-tuple-element.58), channel_id=1, source_target_pairs={{0,1},{1,2},{2,3},{3,4},{4,5},{5,6},{6,7},{7,8},{8,9},{9,10},{10,1... | collective-permute-start | bytes 110600 | tf_op jit(solution)/shard_map/ppermute | solution.py:656
  108.2 4.5 %collective-permute-start.3 = (f32[72,128]{1,0:T(8,128)S(1)}, f32[72,128]{1,0:T(8,128)S(1)}, u32[]{:S(2)}, u32[]{:S(2)}) collective-permute-start(f32[72,128]{1,0:T(8,128)S(1)} %convert_reduce_fusion.mine), channel_id=1, source_target_pairs={{0,1},{1,0},{2,3},{3,2},{4,5},{5,4},{6,7},{7,6},{8,9},{9,8},{10,11... | collective-permute-start | bytes 110600 | tf_op jit(solution)/shard_map/ppermute | solution.py:573

commit v6 on v5

--- a/solution.py
+++ b/solution.py
@@ -8,7 +8,8 @@
 from jax.sharding import PartitionSpec as P
 
 HALO = 32
-LEFT = 16
+LEFT = 12
+MORE = 16
 C = 32
 F32 = jnp.float32
 BF16 = jnp.bfloat16
@@ -31,6 +32,15 @@
 def edge_gates():
     me, peers = lax.axis_index("gx"), lax.axis_size("gx")
     return jnp.where(me > 0, 0.0, 1.0), jnp.where(me < peers - 1, 1.0, 0.0)
+
+
+def counted(value, first):
+    row = lax.broadcasted_iota(jnp.int32, (MORE, 1), 0)
+    cols = value.shape[0] - MORE
+    head = value[:MORE].astype(F32) * jnp.where(row < LEFT, first, 1.0)
+    tail = value[cols:].astype(F32) * jnp.where(row < LEFT, 1.0, 0.0)
+    head, tail = head.astype(value.dtype), tail.astype(value.dtype)
+    return jnp.concatenate([head, value[MORE:cols], tail], axis=0)
 
 
 def gated(value, inside):
@@ -69,43 +79,43 @@
 
 
 def weight_grad(delta, shifted, step, grads, first_piece, first):
-    own = slice(LEFT, delta.shape[1] - LEFT)
+    part = slice(0, delta.shape[1] - MORE)
     places = windows_of(shifted)
-    head = jnp.concatenate(
-        [delta[plane, :LEFT, 256 * window : 256 * window + 256] for plane, window in places], axis=0
+    left = jnp.concatenate(
+        [
+            counted(delta[plane, part, 256 * window : 256 * window + 256], first)
+            for plane, window in places
+        ],
+        axis=0,
     )
-    head = (head.astype(F32) * first).astype(BF16)
-    for tap in range(3):
-        total = lax.dot_general(
-            head,
-            jnp.concatenate(
-                [
-                    shifted[plane, tap, :LEFT, 256 * window : 256 * window + 512]
-                    for plane, window in places
-                ],
-                axis=0,
-            ),
-            CONTRACT_ROWS,
-            preferred_element_type=F32,
+
+    def step_of(tap):
+        right = jnp.concatenate(
+            [
+                shifted[plane, tap, part, 256 * window : 256 * window + 512]
+                for plane, window in places
+            ],
+            axis=0,
         )
-        for plane, window in places:
-            total = total + lax.dot_general(
-                delta[plane, own, 256 * window : 256 * window + 256],
-                shifted[plane, tap, own, 256 * window : 256 * window + 512],
-                CONTRACT_ROWS,
-                preferred_element_type=F32,
-            )
+        total = lax.dot_general(left, right, CONTRACT_ROWS, preferred_element_type=F32)
         folded = None
         for r in range(4):
             near = total[32 * r : 32 * r + 32, 0:384]
             far = total[32 * r + 128 : 32 * r + 160, 128:512]
-            part = near + far
+            both = near + far
             if r:
-                part = pltpu.roll(part, 384 - 32 * r, 1)
-            folded = part if folded is None else folded + part
+                both = pltpu.roll(both, 384 - 32 * r, 1)
+            folded = both if folded is None else folded + both
         for row_tap in range(3):
             at = 32 * (4 + step * (row_tap - 1))
             put_piece(grads, first_piece + 3 * row_tap + tap, folded[:, at : at + 32])
+
+    return [functools.partial(step_of, tap) for tap in range(3)]
+
+
+def run(steps):
+    for step in steps:
+        step()
 
 
 def put_piece(grads, index, value):
@@ -138,8 +148,9 @@
 
 
 def fill_band(weight, band, step, backward):
-    for col_tap in range(3):
-        fill_tap(weight, band, step, backward, col_tap)
+    return [
+        functools.partial(fill_tap, weight, band, step, backward, col_tap) for col_tap in range(3)
+    ]
 
 
 class Copies:
@@ -226,8 +237,8 @@
         along = jnp.concatenate([four] * 8, axis=1)
         spread[32 * k : 32 * k + 32, :] = jnp.where(same, along, 0.0).astype(BF16)
     marks_out[...] = marks_first(labels[...])
-    fill_band(conv_a, band_a, 1, False)
-    fill_band(conv_b, band_b, 2, False)
+    run(fill_band(conv_a, band_a, 1, False))
+    run(fill_band(conv_b, band_b, 2, False))
     wait_all(copies.started[5:9])
     for side in range(cols // 128):
         fill_flat(stem, flat, side)
@@ -244,8 +255,7 @@
 
 def forward_xy_kernel(
     stem, marks, after, band_a, band_b,
-    stem_frame, hidden_one, hidden_two, marks_out, message,
-    stem_s, one_s,
+    stem_s, one_s, hidden_two, marks_out, message,
 ):
     _, inside = edge_gates()
     clear_margins(stem_s)
@@ -253,12 +263,10 @@
     for window in range(4):
         lanes = slice(256 * window, 256 * window + 256)
         value = jnp.concatenate([stem[:, lanes], after[:, lanes]], axis=0)
-        stem_frame[0, :, lanes] = value
         store_shifted(stem_s, 0, 256 * window, value.astype(F32), 1)
     marks_out[...] = jnp.concatenate([marks[...], after[:, 1024:1152]], axis=0)
     for window in range(4):
         value = gated(softplus(conv_window(stem_s, 0, window, band_a)), inside)
-        hidden_one[0, :, 256 * window : 256 * window + 256] = value.astype(BF16)
         store_shifted(one_s, 0, 256 * window, value, 2)
     for window in range(4):
         value = gated(softplus(conv_window(one_s, 0, window, band_b)), inside).astype(BF16)
@@ -300,20 +308,25 @@
     left, inside = edge_gates()
     band_c, band_d, band_dt, band_ct = [bands.at[k] for k in range(4)]
     rows = marks.shape[0]
-    half = rows // 2
+    half = (rows - MORE) // 2
+    upper = slice(half, 2 * half)
     for shifted in (two_s, ref_one_s, delta_two_s, delta_one_s):
         clear_margins(shifted)
     places = windows_of(two_s)
-    fill_band(conv_c, band_c, 1, False)
+    run(fill_band(conv_c, band_c, 1, False))
     load_features(message, two_s)
+    steps = fill_band(conv_d, band_d, 2, False)
     for plane, window in places:
         value = gated(softplus(conv_window(two_s, plane, window, band_c)), inside)
         store_shifted(ref_one_s, plane, 256 * window, value, 2)
-    fill_band(conv_d, band_d, 2, False)
+        run(steps[:1])
+        steps = steps[1:]
+    steps = fill_band(conv_d, band_dt, 2, True)
     for plane, window in places:
         value = softplus(conv_window(ref_one_s, plane, window, band_d))
         ref_two[plane, :, 256 * window : 256 * window + 256] = value.astype(BF16)
-    fill_band(conv_d, band_dt, 2, True)
+        run(steps[:1])
+        steps = steps[1:]
 
     labels = marks[:, 0:32].astype(F32)
     spread_one, spread_two = spread[0:32, :], spread[32:64, :]
@@ -332,7 +345,7 @@
     first = first.astype(BF16).astype(F32)
     second = second + first
     share = 1.0 / (1.0 + jnp.exp(-second))
-    probability[...] = share[: rows - LEFT]
+    probability[...] = share[: rows - MORE]
     error_two = gated(share - labels, inside)
     error_one = 1.0 / (1.0 + jnp.exp(-first)) - labels + error_two
     error_two = split(error_two)
@@ -346,13 +359,18 @@
         value = jnp.dot(error_two, spread_two[:, lanes], preferred_element_type=F32)
         value = value * slope(ref_two[plane, :, at : at + 256])
         store_shifted(delta_two_s, plane, at, value, 2)
-    fill_band(conv_c, band_ct, 1, True)
+    grads[...] = jnp.zeros(grads.shape, F32)
+    fills = fill_band(conv_c, band_ct, 1, True)
+    sums = weight_grad(centre(delta_two_s), ref_one_s, 2, grads, 9, left)
     for plane, window in places:
         at = 256 * window
         value = conv_window(delta_two_s, plane, window, band_dt)
         stored = ref_one_s[plane, 1, :, 128 + at : 384 + at]
         value = gated(value * slope(stored), inside)
         store_shifted(delta_one_s, plane, at, value, 1)
+        run(fills[:1] + sums[:1])
+        fills, sums = fills[1:], sums[1:]
+    sums = weight_grad(centre(delta_one_s), two_s, 1, grads, 0, left)
     for window in range(2):
         values = []
         for plane in range(2):
@@ -360,24 +378,25 @@
             lanes = slice(512 * plane + at, 512 * plane + at + 256)
             value = conv_window(delta_one_s, plane, window, band_ct)
             value = value + jnp.dot(error_one, spread_one[:, lanes], preferred_element_type=F32)
-            values.append(value.astype(BF16))
+            values.append([value[:half].astype(BF16), value[upper].astype(BF16)])
         for z in range(8):
             lanes = slice(32 * z, 32 * z + 32)
             back[8 * window + z, :half] = jnp.concatenate(
                 [
-                    values[0][:half, lanes], values[1][:half, lanes],
-                    values[0][half:, lanes], values[1][half:, lanes],
+                    values[0][0][:, lanes], values[1][0][:, lanes],
+                    values[0][1][:, lanes], values[1][1][:, lanes],
                 ],
                 axis=1,
             )
+        run(sums[:1])
+        sums = sums[1:]
 
     same = own_voxel()
     same = jnp.concatenate([same, same], axis=0)
-    kept_rows = slice(0, rows - LEFT)
+    kept_rows = slice(0, rows - MORE)
 
     def head_grad(errors, planes):
-        error = errors[kept_rows].astype(F32)
-        error = jnp.concatenate([error[:LEFT] * left, error[LEFT:]], axis=0).astype(BF16)
+        error = counted(errors[kept_rows], left)
         total = None
         for plane, feature in enumerate(planes):
             full = lax.dot_general(error, feature, CONTRACT_ROWS, preferred_element_type=F32)
@@ -389,13 +408,11 @@
         total = total + pltpu.roll(total, 32, 1)
         return total[:, 0:32]
 
-    grads[...] = jnp.zeros(grads.shape, F32)
+    run(sums)
     features = [two_s[plane, 1, kept_rows, 128:640] for plane in range(2)]
     put_piece(grads, 18, head_grad(error_one, features))
     features = [ref_two[plane, kept_rows, :] for plane in range(2)]
     put_piece(grads, 19, head_grad(error_two, features))
-    weight_grad(centre(delta_two_s), ref_one_s, 2, grads, 9, left)
-    weight_grad(centre(delta_one_s), two_s, 1, grads, 0, left)
     blank = jnp.zeros((6, 128), F32)
     for peer in range(16):
         chunk = jnp.concatenate([grads[10 * peer : 10 * peer + 10, :], blank], axis=0)
@@ -403,14 +420,13 @@
 
 
 def backward_xy_kernel(
-    back, hidden_two, hidden_one, stem, conv_b,
+    back, hidden_two, one_s, stem_s, conv_b,
     mine_out, theirs_out, delta_a,
-    one_s, stem_s, delta_b_s, delta_b, grads, band_bt,
+    delta_b_s, delta_b, grads, band_bt,
 ):
     first, inside = edge_gates()
-    fill_band(conv_b, band_bt, 2, True)
-    for shifted in (one_s, stem_s, delta_b_s):
-        clear_margins(shifted)
+    run(fill_band(conv_b, band_bt, 2, True))
+    clear_margins(delta_b_s)
     half = back.shape[1] - 16
     for group in range(8):
         parts = []
@@ -419,26 +435,22 @@
             parts.append(
                 jnp.concatenate(
                     [back[2 * group + q, :half, at : at + 64] for q in range(2)], axis=1
-                )
+                ).astype(F32)
             )
         lanes = slice(128 * group, 128 * group + 128)
-        value = jnp.concatenate(parts, axis=0).astype(F32)
+        value = jnp.concatenate(parts + [jnp.zeros((MORE, 128), F32)], axis=0)
         value = gated(value * slope(hidden_two[0, :, lanes]), inside)
         delta_b[0, :, lanes] = value.astype(BF16)
         store_shifted(delta_b_s, 0, 128 * group, value, 2)
     for window in range(4):
         at = 256 * window
         value = conv_window(delta_b_s, 0, window, band_bt)
-        stored = hidden_one[0, :, at : at + 256]
+        stored = one_s[0, 1, :, 128 + at : 384 + at]
         value = gated(value * slope(stored), inside)
         delta_a[0, :, at : at + 256] = value.astype(BF16)
-        store_shifted(one_s, 0, at, stored.astype(F32), 2)
-    for window in range(4):
-        lanes = slice(256 * window, 256 * window + 256)
-        store_shifted(stem_s, 0, 256 * window, stem[0, :, lanes].astype(F32), 1)
     grads[...] = jnp.zeros(grads.shape, F32)
-    weight_grad(delta_b, one_s, 2, grads, 9, first)
-    weight_grad(delta_a, stem_s, 1, grads, 0, first)
+    run(weight_grad(delta_b, one_s, 2, grads, 9, first))
+    run(weight_grad(delta_a, stem_s, 1, grads, 0, first))
     chunk = back[0, half:, :].astype(F32)
     for peer in range(1, 16):
         chunk = chunk + back[peer, half:, :].astype(F32)
@@ -453,34 +465,37 @@
 
 def stem_grad_kernel(delta_a, probability, conv_a, stem_grad, leaving, delta_a_s, band_at):
     rows = delta_a.shape[1]
-    tail = slice(rows - 2 * LEFT, rows - LEFT)
+    cols = rows - 2 * MORE
+    tail = slice(cols, cols + MORE)
     clear_margins(delta_a_s)
-    fill_band(conv_a, band_at, 1, True)
+    run(fill_band(conv_a, band_at, 1, True))
     for window in range(4):
         lanes = slice(256 * window, 256 * window + 256)
         store_shifted(delta_a_s, 0, 256 * window, delta_a[0, :, lanes].astype(F32), 1)
     for window in range(4):
         lanes = slice(256 * window, 256 * window + 256)
         value = conv_window(delta_a_s, 0, window, band_at).astype(BF16)
-        stem_grad[:, lanes] = value[: rows - 2 * LEFT]
+        stem_grad[:, lanes] = value[:cols]
         leaving[:, lanes] = value[tail]
     rest = probability[tail, :]
     parts = []
     for _ in range(3):
         parts.append(rest.astype(BF16))
         rest = rest - parts[-1].astype(F32)
-    parts.append(jnp.zeros((LEFT, 32), BF16))
+    parts.append(jnp.zeros((MORE, 32), BF16))
     leaving[:, 1024:1152] = jnp.concatenate(parts, axis=1)
 
 
 def place_kernel(found, probability, moved, stem_grad, share, flat):
     cols = stem_grad.shape[2]
     first, _ = edge_gates()
+    row = lax.broadcasted_iota(jnp.int32, (MORE, 1), 0)
+    taken = jnp.where(row < LEFT, 1.0 - first, 0.0)
     for group in range(8):
         lanes = slice(128 * group, 128 * group + 128)
         mine = found[:, lanes].astype(F32)
-        head = mine[:LEFT] * first + moved[:, lanes].astype(F32) * (1.0 - first)
-        value = jnp.concatenate([head, mine[LEFT:]], axis=0)
+        head = mine[:MORE] * (1.0 - taken) + moved[:, lanes].astype(F32) * taken
+        value = jnp.concatenate([head, mine[MORE:]], axis=0)
         for side in range(cols // 128):
             turned = value[128 * side : 128 * side + 128].T
             for k in range(4):
@@ -491,8 +506,8 @@
         stem_grad[:, :, 128 * side : 128 * side + 128] = part.astype(BF16)
     parts = moved[:, 1024:1152].astype(F32)
     head = parts[:, 0:32] + parts[:, 32:64] + parts[:, 64:96]
-    head = probability[:LEFT, :] * first + head * (1.0 - first)
-    value = jnp.concatenate([head, probability[LEFT:cols, :]], axis=0).T
+    head = probability[:MORE, :] * (1.0 - taken) + head * taken
+    value = jnp.concatenate([head, probability[MORE:cols, :]], axis=0).T
     share[:, 0, :] = value[0:16]
     share[:, 1, :] = value[16:32]
 
@@ -560,11 +575,11 @@
 def sum_everywhere(mine, theirs, beside, later, slab, gx):
     peers, copies = lax.axis_size(gx), lax.axis_size(slab)
     swap = [(i, i ^ 1) for i in range(peers)]
-    mine = mine + lax.ppermute(theirs, gx, swap)
+    theirs, beside = lax.optimization_barrier((lax.ppermute(theirs, gx, swap), beside))
+    mine = mine + theirs
     spread = jnp.broadcast_to(mine.astype(BF16)[None], (peers // 2,) + mine.shape)
     same_core = [[i for i in range(peers) if i % 2 == core] for core in range(2)]
     mine = lax.all_to_all(spread, gx, 0, 0, tiled=True, axis_index_groups=same_core)
-    mine, beside = lax.optimization_barrier((mine, beside))
     mine = jnp.sum(mine.astype(F32), axis=0)
     spread = jnp.broadcast_to(mine.astype(BF16)[None], (copies,) + mine.shape)
     found = lax.all_to_all(spread, slab, 0, 0, tiled=True)
@@ -612,23 +627,24 @@
         flops=1 << 29, megabytes=6,
     )(stem_features, labels, taps_a, taps_b, head_one[None], head_two[None])
 
-    wide = pltpu.VMEM((1, 3, rows, 1280), BF16)
+    shifted = shape((1, 3, rows, 1280), BF16)
+    wide = vmem(shifted)
     tall = pltpu.VMEM((2, 3, rows, 768), BF16)
     whole = shape((1, rows, 1024), BF16)
     planes = shape((2, rows, 512), BF16)
     messages = shape((16, half, 128), BF16)
-    stem, hidden_one, hidden_two, marks, message = call(
+    stem_s, one_s, hidden_two, marks, message = call(
         forward_xy_kernel,
-        [(whole, VMEM)] * 3 + [(shape((rows, 128), BF16), VMEM), (messages, VMEM)],
-        [VMEM] * 5,
-        [wide, wide], flops=1 << 30, megabytes=8,
+        [(shifted, VMEM)] * 2
+        + [(whole, VMEM), (shape((rows, 128), BF16), VMEM), (messages, VMEM)],
+        [VMEM] * 5, flops=1 << 30, megabytes=8,
     )(stem, marks, after, band_a, band_b)
     message = lax.all_to_all(message, "slab", 0, 0, tiled=True)
 
-    larger = shape((16, half + 16, 128), BF16)
+    larger = shape((16, (cols + MORE) // 2 + MORE, 128), BF16)
     probability, back = call(
         section_xz_kernel,
-        [(shape((rows - LEFT, 32), F32), VMEM), (larger, VMEM)],
+        [(shape((rows - MORE, 32), F32), VMEM), (larger, VMEM)],
         [VMEM] * 5,
         [tall, tall, tall, tall, vmem(planes), pltpu.VMEM((4, 1536, 256), BF16)]
         + [pltpu.VMEM((160, 128), F32)],
@@ -641,10 +657,10 @@
         backward_xy_kernel,
         [(half_sums, VMEM), (half_sums, VMEM), (whole, VMEM)],
         [VMEM] * 5,
-        [wide, wide, wide, vmem(whole), pltpu.VMEM((160, 128), F32), vmem(band)],
+        [wide, vmem(whole), pltpu.VMEM((160, 128), F32), vmem(band)],
         flops=1 << 31, megabytes=16,
-    )(back, hidden_two, hidden_one, stem, taps_b)
-    edge = shape((LEFT, 1152), BF16)
+    )(back, hidden_two, one_s, stem_s, taps_b)
+    edge = shape((MORE, 1152), BF16)
     beside = call(
         stem_grad_kernel,
         [(shape((cols, 1024), BF16), VMEM), (edge, VMEM)],

time: 114 us -> 112 us (0.982)
  blocking collectives: 51.9 us -> 61.9 us
  starting transfers between devices: 24.1 us -> 18.8 us
  waiting for transfers between devices: 10.7 us -> 5.66 us
    all_to_all x0 -> x1, blocking collectives: none -> 10.3 us  [sum_everywhere(): lax.all_to_all(spread, gx, 0, 0, tiled=True, axis_index_groups=same_core)]
    all_to_all x1 -> x0, starting transfers between devices: 5.17 us -> none  [sum_everywhere(): lax.all_to_all(spread, gx, 0, 0, tiled=True, axis_index_groups=same_core)]
    all_to_all x1 -> x0, waiting for transfers between devices: 4.57 us -> none  [sum_everywhere(): lax.all_to_all(spread, gx, 0, 0, tiled=True, axis_index_groups=same_core)]
  transfers between devices with their start and end apart: 6 -> 5, of which waited for: 4 -> 2; matrix products, arithmetic and copies ran while one was open for 0% -> 0% of each run, Pallas kernels for 5% -> 5%
where the time goes in v6:
time: 112 us
  blocking collectives  61.9 us (55%)
  Pallas kernels  24 us (21%)
  starting transfers between devices  18.8 us (17%)
  waiting for transfers between devices  5.66 us (5%)
    all_to_all x1, blocking collectives, per_device(): message = lax.all_to_all(message, 'slab', 0, 0, tiled=True)  29.7 us
    pallas_call x9, Pallas kernels, run(): return bound(*operands)  24 us
    all_to_all x1, blocking collectives, per_device(): back = lax.all_to_all(back, 'slab', 0, 0, tiled=True)  21.8 us
    all_to_all x1, blocking collectives, sum_everywhere(): lax.all_to_all(spread, gx, 0, 0, tiled=True, axis_index_groups=same_core)  10.3 us
    ppermute x1, starting transfers between devices, per_device(): after = lax.ppermute(initial, 'gx', down)  5.15 us
    all_to_all x1, waiting for transfers between devices, sum_everywhere(): found = lax.all_to_all(spread, slab, 0, 0, tiled=True)  4.59 us
    ppermute x1, starting transfers between devices, sum_everywhere(): return ((mine, lax.ppermute(mine, gx, swap), found[:, 72:]), beside)  3.63 us
    all_to_all x1, starting transfers between devices, sum_everywhere(): found = lax.all_to_all(spread, slab, 0, 0, tiled=True)  3.55 us
  transfers between devices with their start and end apart: 5, of which 2 were waited for; matrix products, arithmetic and copies ran while one was open for 0% of the time, Pallas kernels for 5%

profile of v6, /device:TPU:1, one launch (start us, length us, event | category | flops | bytes accessed | tf_op | source)
XLA Modules:
  0.0 112.0 jit_solution(1751916183418932023)
XLA Ops:
  0.6 1.4 %shard_map.144 = bf16[32,1152]{1,0:T(8,128)(2,1)S(1)} custom-call(bf16[32,32,256]{2,1,0:T(8,128)(2,1)} %bitcast.22, s32[16,2,256]{2,1,0:T(2,128)} %labels_in.3), custom_call_target="tpu_custom_call" | custom-call | flops 268435456 | bytes 1048576 | tf_op jit(solution)/shard_map/pallas_call | solution.py:557
  2.0 5.1 %collective-permute-start = (bf16[32,1152]{1,0:T(8,128)(2,1)S(1)}, bf16[32,1152]{1,0:T(8,128)(2,1)S(1)}, u32[]{:S(2)}, u32[]{:S(2)}) collective-permute-start(bf16[32,1152]{1,0:T(8,128)(2,1)S(1)} %shard_map.144), channel_id=1, source_target_pairs={{1,0},{2,1},{3,2},{4,3},{5,4},{6,5},{7,6},{8,7},{9,8},{10,9},{11,1... | collective-permute-start | bytes 221192 | tf_op jit(solution)/shard_map/ppermute | solution.py:608
  7.2 2.3 %shard_map.143 = (bf16[256,1024]{1,0:T(8,128)(2,1)S(1)}, bf16[256,128]{1,0:T(8,128)(2,1)S(1)}, bf16[1536,256]{1,0:T(8,128)(2,1)S(1)}, bf16[1536,256]{1,0:T(8,128)(2,1)S(1)}, bf16[64,1024]{1,0:T(8,128)(2,1)S(1)}) custom-call(bf16[32,32,256]{2,1,0:T(8,128)(2,1)} %bitcast.23, s32[16,2,256]{2,1,0:T(2,128)} %labels_in.3, bf16[3,3,32,32]{3,2,1,0:T(8,128)(2,1)} %bitcast.20, ...), custom_call_target="tpu_custom_call" | custom-call | flops 536870912 | bytes 1048576 | tf_op jit(solution)/shard_map/pallas_call | solution.py:557
  9.4 0.0 collective-permute-done.after
  9.4 0.0 copy-start
  9.5 0.0 copy-start.1
  9.5 2.9 %shard_map.145 = (bf16[1,3,288,1280]{3,2,1,0:T(8,128)(2,1)S(1)}, bf16[1,3,288,1280]{3,2,1,0:T(8,128)(2,1)S(1)}, bf16[1,288,1024]{2,1,0:T(8,128)(2,1)S(1)}, bf16[...) custom-call(bf16[256,1024]{1,0:T(8,128)(2,1)S(1)} %get-tuple-element.39.stem, ...), custom_call_target="tpu_custom_call" | custom-call | flops 1073741824 | bytes 1048576 | tf_op jit(solution)/shard_map/pallas_call | solution.py:557
  12.4 29.7 %all_to_all.20.message = bf16[16,144,128]{2,1,0:T(8,128)(2,1)S(1)} all-to-all(bf16[16,144,128]{2,1,0:T(8,128)(2,1)S(1)} %get-tuple-element.43), channel_id=1, replica_groups=mesh['slab'=16,'gx'=16] {'slab'}, dimensions={0} | all-to-all | bytes 1179648 | tf_op jit(solution)/shard_map/all_to_all | solution.py:642
  42.2 8.9 %shard_map.146 = (f32[272,32]{1,0:T(8,128)S(1)}, bf16[16,152,128]{2,1,0:T(8,128)(2,1)S(1)}) custom-call(bf16[16,144,128]{2,1,0:T(8,128)(2,1)S(1)} %all_to_all.20.message, bf16[288,128]{1,0:T(8,128)(2,1)S(1)} %get-tuple-element.44.marks, bf16[3,3,32,32]{3,2,1,0:T(8,128)(2,1)S(1)} %bitcast.16, bf16[3,3,32,32]{3,2,1,0:T(8,128)(2,1)S(1)} %bitcast.17, ...), custom_call_target="tpu_custom_call" | custom-call | flops 2147483648 | bytes 1048576 | tf_op jit(solution)/shard_map/pallas_call | solution.py:557
  51.0 21.8 %all_to_all.21.back = bf16[16,152,128]{2,1,0:T(8,128)(2,1)S(1)} all-to-all(bf16[16,152,128]{2,1,0:T(8,128)(2,1)S(1)} %get-tuple-element.46), channel_id=1, replica_groups=mesh['slab'=16,'gx'=16] {'slab'}, dimensions={0} | all-to-all | bytes 1245184 | tf_op jit(solution)/shard_map/all_to_all | solution.py:653
  72.8 3.9 %shard_map.147 = (f32[88,128]{1,0:T(8,128)S(1)}, f32[88,128]{1,0:T(8,128)S(1)}, bf16[1,288,1024]{2,1,0:T(8,128)(2,1)S(1)}) custom-call(bf16[16,152,128]{2,1,0:T(8,128)(2,1)S(1)} %all_to_all.21.back, bf16[1,288,1024]{2,1,0:T(8,128)(2,1)S(1)} %get-tuple-element.47.hidden_two, bf16[1,3,288,1280]{3,2,1,0:T(8,128)(2,1)S(1)} %get-tuple-element.48.one_s, ...), custom_call_target="tpu_custom_call" | custom-call | flops 2147483648 | bytes 1048576 | tf_op jit(solution)/shard_map/pallas_call | solution.py:557
  76.8 3.0 %collective-permute-start.1 = (f32[88,128]{1,0:T(8,128)S(1)}, f32[88,128]{1,0:T(8,128)S(1)}, u32[]{:S(2)}, u32[]{:S(2)}) collective-permute-start(f32[88,128]{1,0:T(8,128)S(1)} %get-tuple-element.51), channel_id=1, source_target_pairs={{0,1},{1,0},{2,3},{3,2},{4,5},{5,4},{6,7},{7,6},{8,9},{9,8},{10,11... | collective-permute-start | bytes 135176 | tf_op jit(solution)/shard_map/ppermute | solution.py:578
  79.7 1.3 %shard_map.148 = (bf16[256,1024]{1,0:T(8,128)(2,1)S(1)}, bf16[16,1152]{1,0:T(8,128)(2,1)S(1)}) custom-call(bf16[1,288,1024]{2,1,0:T(8,128)(2,1)S(1)} %get-tuple-element.52.delta_a, f32[272,32]{1,0:T(8,128)S(1)} %get-tuple-element.53.probability, bf16[3,3,32,32]{3,2,1,0:T(8,128)(2,1)S(1)} %bitcast.21), custom_call_target="tpu_custom_call" | custom-call | flops 1073741824 | bytes 1048576 | tf_op jit(solution)/shard_map/pallas_call | solution.py:557
  81.1 10.3 %all_to_all.22 = bf16[8,88,128]{2,1,0:T(8,128)(2,1)S(1)} all-to-all(bf16[8,88,128]{2,1,0:T(8,128)(2,1)S(1)} %broadcast_in_dim.23), channel_id=1, replica_groups={{0,2,4,6,8,10,12,14},{1,3,5,7,9,11,13,15},{16,18,20,22,24,26,28,30},{17..., dimensions={0} | all-to-all | bytes 360448 | tf_op jit(solution)/shard_map/all_to_all | solution.py:582
  91.4 0.8 broadcast_in_dim.24
  92.2 3.5 %all-to-all-start.3 = ((bf16[16,88,128]{2,1,0:T(8,128)(2,1)}), bf16[16,88,128]{2,1,0:T(8,128)(2,1)S(1)}, u32[]{:S(2)}, u32[]{:S(2)}) async-start(bf16[16,88,128]{2,1,0:T(8,128)(2,1)} %broadcast_in_dim.24), calls=%async_computation.3 | async-start | bytes 720896 | tf_op jit(solution)/shard_map/all_to_all | solution.py:585
  95.8 3.5 %collective-permute-start.2 = (bf16[16,1152]{1,0:T(8,128)(2,1)S(1)}, bf16[16,1152]{1,0:T(8,128)(2,1)S(1)}, u32[]{:S(2)}, u32[]{:S(2)}) collective-permute-start(bf16[16,1152]{1,0:T(8,128)(2,1)S(1)} %get-tuple-element.58), channel_id=1, source_target_pairs={{0,1},{1,2},{2,3},{3,4},{4,5},{5,6},{6,7},{7,8},{8,9},{9,10},{10,1... | collective-permute-start | bytes 110600 | tf_op jit(solution)/shard_map/ppermute | solution.py:672
  99.3 1.0 collective-permute-done.2.moved
  100.4 1.7 %shard_map.149 = (bf16[32,32,256]{2,1,0:T(8,128)(2,1)}, f32[16,2,256]{2,1,0:T(2,128)}) custom-call(bf16[256,1024]{1,0:T(8,128)(2,1)S(1)} %get-tuple-element.57.found, f32[272,32]{1,0:T(8,128)S(1)} %get-tuple-element.53.probability, bf16[16,1152]{1,0:T(8,128)(2,1)S(1)} %collective-permute-done.2.moved), custom_call_target="tpu_custom_call" | custom-call | flops 268435456 | bytes 1048576 | tf_op jit(solution)/shard_map/pallas_call | solution.py:557
  102.1 4.6 %all-to-all-done.3 = bf16[16,88,128]{2,1,0:T(8,128)(2,1)S(1)} async-done(((bf16[16,88,128]{2,1,0:T(8,128)(2,1)}), bf16[16,88,128]{2,1,0:T(8,128)(2,1)S(1)}, u32[]{:S(2)}, u32[]{:S(2)}) %all-to-all-start.3) | async-done | bytes 360480 | tf_op jit(solution)/shard_map/all_to_all | solution.py:585
  106.7 3.6 %collective-permute-start.3 = (f32[72,128]{1,0:T(8,128)S(1)}, f32[72,128]{1,0:T(8,128)S(1)}, u32[]{:S(2)}, u32[]{:S(2)}) collective-permute-start(f32[72,128]{1,0:T(8,128)S(1)} %convert_reduce_fusion.mine), channel_id=1, source_target_pairs={{0,1},{1,0},{2,3},{3,2},{4,5},{5,4},{6,7},{7,6},{8,9},{9,8},{10,11... | collective-permute-start | bytes 110600 | tf_op jit(solution)/shard_map/ppermute | solution.py:588
  110.3 0.8 shard_map.151
  111.2 0.0 collective-permute-done.3.theirs
  111.2 0.8 shard_map.150
  (12 shorter events, 0.1 us)
Async XLA Ops:
  2.0 7.4 %collective-permute-start = (bf16[32,1152]{1,0:T(8,128)(2,1)S(1)}, bf16[32,1152]{1,0:T(8,128)(2,1)S(1)}, u32[]{:S(2)}, u32[]{:S(2)}) collective-permute-start(bf16[32,1152]{1,0:T(8,128)(2,1)S(1)} %shard_map.144), channel_id=1, source_target_pairs={{1,0},{2,1},{3,2},{4,3},{5,4},{6,5},{7,6},{8,7},{9,8},{10,9},{11,1... | collective-permute-start | bytes 221192 | tf_op jit(solution)/shard_map/ppermute | solution.py:608
  9.4 32.7 %copy-start = (bf16[32,3,3,32]{3,0,2,1:T(8,128)(2,1)S(1)}, bf16[32,3,3,32]{3,0,2,1:T(8,128)(2,1)}, u32[]{:S(2)}) copy-start(bf16[32,3,3,32]{3,0,2,1:T(8,128)(2,1)} %param.12) | copy-start | bytes 55300
  9.5 32.7 %copy-start.1 = (bf16[32,3,3,32]{3,0,2,1:T(8,128)(2,1)S(1)}, bf16[32,3,3,32]{3,0,2,1:T(8,128)(2,1)}, u32[]{:S(2)}) copy-start(bf16[32,3,3,32]{3,0,2,1:T(8,128)(2,1)} %param.13) | copy-start | bytes 55300
  42.2 30.7 %copy-start.2 = (bf16[32,3,3,32]{3,0,2,1:T(8,128)(2,1)S(1)}, bf16[32,3,3,32]{3,0,2,1:T(8,128)(2,1)}, u32[]{:S(2)}) copy-start(bf16[32,3,3,32]{3,0,2,1:T(8,128)(2,1)} %param.11) | copy-start | bytes 55300
  72.8 6.9 %copy-start.3 = (bf16[32,3,3,32]{3,0,2,1:T(8,128)(2,1)S(1)}, bf16[32,3,3,32]{3,0,2,1:T(8,128)(2,1)}, u32[]{:S(2)}) copy-start(bf16[32,3,3,32]{3,0,2,1:T(8,128)(2,1)} %param.10) | copy-start | bytes 55300
  76.8 4.2 %collective-permute-start.1 = (f32[88,128]{1,0:T(8,128)S(1)}, f32[88,128]{1,0:T(8,128)S(1)}, u32[]{:S(2)}, u32[]{:S(2)}) collective-permute-start(f32[88,128]{1,0:T(8,128)S(1)} %get-tuple-element.51), channel_id=1, source_target_pairs={{0,1},{1,0},{2,3},{3,2},{4,5},{5,4},{6,7},{7,6},{8,9},{9,8},{10,11... | collective-permute-start | bytes 135176 | tf_op jit(solution)/shard_map/ppermute | solution.py:578
  92.2 14.4 %all-to-all-start.3 = ((bf16[16,88,128]{2,1,0:T(8,128)(2,1)}), bf16[16,88,128]{2,1,0:T(8,128)(2,1)S(1)}, u32[]{:S(2)}, u32[]{:S(2)}) async-start(bf16[16,88,128]{2,1,0:T(8,128)(2,1)} %broadcast_in_dim.24), calls=%async_computation.3 | async-start | bytes 720896 | tf_op jit(solution)/shard_map/all_to_all | solution.py:585
  95.8 4.6 %collective-permute-start.2 = (bf16[16,1152]{1,0:T(8,128)(2,1)S(1)}, bf16[16,1152]{1,0:T(8,128)(2,1)S(1)}, u32[]{:S(2)}, u32[]{:S(2)}) collective-permute-start(bf16[16,1152]{1,0:T(8,128)(2,1)S(1)} %get-tuple-element.58), channel_id=1, source_target_pairs={{0,1},{1,2},{2,3},{3,4},{4,5},{5,6},{6,7},{7,8},{8,9},{9,10},{10,1... | collective-permute-start | bytes 110600 | tf_op jit(solution)/shard_map/ppermute | solution.py:672
  106.7 4.5 %collective-permute-start.3 = (f32[72,128]{1,0:T(8,128)S(1)}, f32[72,128]{1,0:T(8,128)S(1)}, u32[]{:S(2)}, u32[]{:S(2)}) collective-permute-start(f32[72,128]{1,0:T(8,128)S(1)} %convert_reduce_fusion.mine), channel_id=1, source_target_pairs={{0,1},{1,0},{2,3},{3,2},{4,5},{5,4},{6,7},{7,6},{8,9},{9,8},{10,11... | collective-permute-start | bytes 110600 | tf_op jit(solution)/shard_map/ppermute | solution.py:588

commit v7 on v6

--- a/solution.py
+++ b/solution.py
@@ -200,37 +200,36 @@
     return marks.T.astype(BF16)
 
 
-def edge_kernel(stem_in, labels_in, initial, flat, stem, labels, sems):
+def edge_kernel(
+    stem_in, labels_in, conv_a_in, conv_b_in, head_one_in, head_two_in,
+    initial, stem, labels, conv_a, conv_b, heads, flat, sems,
+):
     copies = Copies(sems)
-    near = pl.ds(0, 128)
-    for k in range(4):
-        rows = pl.ds(8 * k, 8)
-        copies.start(stem_in.at[rows, :, near], stem.at[rows])
-    copies.start(labels_in.at[:, :, near], labels)
-    wait_all(copies.started)
+    for side in range(stem.shape[2] // 128):
+        lanes = pl.ds(128 * side, 128)
+        for k in range(4):
+            rows = pl.ds(8 * k, 8)
+            copies.start(stem_in.at[rows, :, lanes], stem.at[rows, :, lanes])
+        if side == 0:
+            copies.start(labels_in, labels)
+    copies.start(conv_a_in, conv_a)
+    copies.start(conv_b_in, conv_b)
+    copies.start(head_one_in, heads.at[0])
+    copies.start(head_two_in, heads.at[1])
+    wait_all(copies.started[:5])
     fill_flat(stem, flat, 0)
     for group in range(8):
         value = columns_first(stem, flat, 0, group)
         initial[:, 128 * group : 128 * group + 128] = value[:HALO].astype(BF16)
-    initial[:, 1024:1152] = marks_first(labels[...])[:HALO]
+    initial[:, 1024:1152] = marks_first(labels[:, :, :128])[:HALO]
+    wait_all(copies.started[5:])
 
 
 def arrange_kernel(
-    stem_in, labels_in, conv_a_in, conv_b_in, head_one_in, head_two_in,
-    stem_out, marks_out, band_a, band_b, spread,
-    flat, stem, labels, conv_a, conv_b, heads, sems,
+    stem, labels, conv_a, conv_b, heads,
+    stem_out, marks_out, band_a, band_b, spread, flat,
 ):
     cols = stem.shape[2]
-    copies = Copies(sems)
-    copies.start(conv_a_in, conv_a)
-    copies.start(conv_b_in, conv_b)
-    copies.start(head_one_in, heads.at[0])
-    copies.start(head_two_in, heads.at[1])
-    copies.start(labels_in, labels)
-    for k in range(4):
-        rows = pl.ds(8 * k, 8)
-        copies.start(stem_in.at[rows], stem.at[rows])
-    wait_all(copies.started[:5])
     same = own_voxel()
     for k in range(2):
         four = jnp.concatenate([heads[k].astype(F32)] * 4, axis=1)
@@ -239,7 +238,6 @@
     marks_out[...] = marks_first(labels[...])
     run(fill_band(conv_a, band_a, 1, False))
     run(fill_band(conv_b, band_b, 2, False))
-    wait_all(copies.started[5:9])
     for side in range(cols // 128):
         fill_flat(stem, flat, side)
     for group in range(8):
@@ -514,7 +512,9 @@
 
 def finish_cd_kernel(factor, chunks, grad_c, grad_d, head_one, head_two, flat):
     for peer in range(16):
-        flat[10 * peer : 10 * peer + 10, :] = chunks[peer, 0:10, :].astype(F32) * factor
+        upper, z = peer // 8, peer % 8
+        chunk = chunks[z, 10 * upper : 10 * upper + 10, :].astype(F32)
+        flat[10 * peer : 10 * peer + 10, :] = chunk * factor
 
     def piece(index):
         row, lane = 32 * (index // 4), 32 * (index % 4)
@@ -573,17 +573,25 @@
 
 
 def sum_everywhere(mine, theirs, beside, later, slab, gx):
-    peers, copies = lax.axis_size(gx), lax.axis_size(slab)
+    peers, slabs = lax.axis_size(gx), lax.axis_size(slab)
+    depth, wide = slabs // 2, peers // 2
     swap = [(i, i ^ 1) for i in range(peers)]
     theirs, beside = lax.optimization_barrier((lax.ppermute(theirs, gx, swap), beside))
     mine = mine + theirs
-    spread = jnp.broadcast_to(mine.astype(BF16)[None], (peers // 2,) + mine.shape)
-    same_core = [[i for i in range(peers) if i % 2 == core] for core in range(2)]
-    mine = lax.all_to_all(spread, gx, 0, 0, tiled=True, axis_index_groups=same_core)
-    mine = jnp.sum(mine.astype(F32), axis=0)
-    spread = jnp.broadcast_to(mine.astype(BF16)[None], (copies,) + mine.shape)
-    found = lax.all_to_all(spread, slab, 0, 0, tiled=True)
+    across = [
+        [(upper * depth + z) * peers + 2 * chip + core for upper in range(2) for chip in range(wide)]
+        for z in range(depth)
+        for core in range(2)
+    ]
+    spread = jnp.broadcast_to(mine.astype(BF16)[None], (2 * wide,) + mine.shape)
+    found = lax.all_to_all(spread, (slab, gx), 0, 0, tiled=True, axis_index_groups=across)
     found, beside = lax.optimization_barrier((found, later(beside)))
+    halves = jnp.sum(found.astype(F32).reshape((2, wide) + mine.shape), axis=1)
+    chunks = halves[:, 72:82].reshape(20, 128)
+    mine = jnp.concatenate([halves[0, :72] + halves[1, :72], chunks, jnp.zeros((4, 128), F32)])
+    along = [[upper * depth + z for z in range(depth)] for upper in range(2)]
+    spread = jnp.broadcast_to(mine.astype(BF16)[None], (depth,) + mine.shape)
+    found = lax.all_to_all(spread, slab, 0, 0, tiled=True, axis_index_groups=along)
     mine = jnp.sum(found[:, :72].astype(F32), axis=0)
     return (mine, lax.ppermute(mine, gx, swap), found[:, 72:]), beside
 
@@ -599,17 +607,19 @@
     vmem = lambda kind: pltpu.VMEM(kind.shape, kind.dtype)
 
     stem_features = stem_features[:, 0]
-    near = pltpu.VMEM((C, height, 128), BF16)
-    near_labels = pltpu.VMEM((16, 2, 128), labels.dtype)
-    (initial,) = call(
-        edge_kernel, [(shape((HALO, 1152), BF16), VMEM)], [HBM, HBM],
-        [pltpu.VMEM((1024, 128), F32), near, near_labels, sems(5)], flops=1 << 28, megabytes=3,
-    )(stem_features, labels)
-    after = lax.ppermute(initial, "gx", down)
-
     taps_a, taps_b, taps_c, taps_d = [
         jnp.transpose(w, (1, 2, 0, 3)) for w in (conv_a, conv_b, conv_c, conv_d)
     ]
+    held = [stem_features, labels, taps_a, taps_b]
+    initial, *loaded = call(
+        edge_kernel,
+        [(shape((HALO, 1152), BF16), VMEM)]
+        + [(shape(array.shape, array.dtype), VMEM) for array in held]
+        + [(shape((2, 1, C), BF16), VMEM)],
+        [HBM] * 6, [pltpu.VMEM((1024, 128), F32), sems(13)], flops=1 << 28, megabytes=3,
+    )(*held, head_one[None], head_two[None])
+    after = lax.ppermute(initial, "gx", down)
+
     band = shape((1536, 256), BF16)
     spreads = shape((64, 1024), BF16)
     stem, marks, band_a, band_b, spread = call(
@@ -621,11 +631,10 @@
             (band, VMEM),
             (spreads, VMEM),
         ],
-        [HBM] * 6,
-        [pltpu.VMEM((1024 * cols // 128, 128), F32), vmem(stem_features), vmem(labels)]
-        + [vmem(taps_a), vmem(taps_b), pltpu.VMEM((2, 1, C), BF16), sems(9)],
+        [VMEM] * 5,
+        [pltpu.VMEM((1024 * cols // 128, 128), F32)],
         flops=1 << 29, megabytes=6,
-    )(stem_features, labels, taps_a, taps_b, head_one[None], head_two[None])
+    )(*loaded)
 
     shifted = shape((1, 3, rows, 1280), BF16)
     wide = vmem(shifted)

time: 112 us -> 112 us (level)
  waiting for transfers between devices: 5.66 us -> 3.69 us
  blocking collectives: 61.9 us -> 63.1 us
    all_to_all x1, waiting for transfers between devices: 4.59 us -> 0.86 us  [sum_everywhere(): lax.all_to_all(spread, (slab, gx), 0, 0, tiled=True, axis_index_groups=ac...]
    all_to_all x1, starting transfers between devices: 3.55 us -> 5.41 us  [sum_everywhere(): lax.all_to_all(spread, (slab, gx), 0, 0, tiled=True, axis_index_groups=ac...]
    ppermute x1, waiting for transfers between devices: 1.04 us -> 2.47 us  [place(): moved = lax.ppermute(leaving, 'gx', up)]
  transfers between devices with their start and end apart: 5 -> 5, of which waited for: 2 -> 3; matrix products, arithmetic and copies ran while one was open for 0% -> 0% of each run, Pallas kernels for 5% -> 4%
where the time goes in v7:
time: 112 us
  blocking collectives  63.1 us (56%)
  Pallas kernels  23 us (21%)
  starting transfers between devices  19.9 us (18%)
  waiting for transfers between devices  3.69 us (3%)
    all_to_all x1, blocking collectives, per_device(): message = lax.all_to_all(message, 'slab', 0, 0, tiled=True)  30.2 us
    pallas_call x9, Pallas kernels, run(): return bound(*operands)  23 us
    all_to_all x1, blocking collectives, per_device(): back = lax.all_to_all(back, 'slab', 0, 0, tiled=True)  21.9 us
    all_to_all x1, blocking collectives, sum_everywhere(): lax.all_to_all(spread, slab, 0, 0, tiled=True, axis_index_groups=along)  11.1 us
    all_to_all x1, starting transfers between devices, sum_everywhere(): lax.all_to_all(spread, (slab, gx), 0, 0, tiled=True, axis_index_groups=ac...  5.41 us
    ppermute x1, starting transfers between devices, per_device(): after = lax.ppermute(initial, 'gx', down)  5.15 us
    ppermute x1, starting transfers between devices, place(): moved = lax.ppermute(leaving, 'gx', up)  3.73 us
    ppermute x1, starting transfers between devices, sum_everywhere(): return ((mine, lax.ppermute(mine, gx, swap), found[:, 72:]), beside)  2.99 us
  transfers between devices with their start and end apart: 5, of which 3 were waited for; matrix products, arithmetic and copies ran while one was open for 0% of the time, Pallas kernels for 4%

profile of v7, /device:TPU:1, one launch (start us, length us, event | category | flops | bytes accessed | tf_op | source)
XLA Modules:
  0.0 111.5 jit_solution(2691327714235186267)
XLA Ops:
  0.6 1.5 %shard_map.143 = (bf16[32,1152]{1,0:T(8,128)(2,1)S(1)}, bf16[32,32,256]{2,1,0:T(8,128)(2,1)S(1)}, s32[16,2,256]{2,1,0:T(2,128)S(1)}, bf16[3,3,32,32]{3,2,1,0:T(8...) custom-call(bf16[32,32,256]{2,1,0:T(8,128)(2,1)} %bitcast.27, s32[16,2,256]{2,1,0:T(2,128)} %labels_in.1, ...), custom_call_target="tpu_custom_call" | custom-call | flops 268435456 | bytes 1048576 | tf_op jit(solution)/shard_map/pallas_call | solution.py:557
  2.1 5.1 %collective-permute-start = (bf16[32,1152]{1,0:T(8,128)(2,1)S(1)}, bf16[32,1152]{1,0:T(8,128)(2,1)S(1)}, u32[]{:S(2)}, u32[]{:S(2)}) collective-permute-start(bf16[32,1152]{1,0:T(8,128)(2,1)S(1)} %get-tuple-element.52), channel_id=1, source_target_pairs={{1,0},{2,1},{3,2},{4,3},{5,4},{6,5},{7,6},{8,7},{9,8},{10,9},{11,1... | collective-permute-start | bytes 221192 | tf_op jit(solution)/shard_map/ppermute | solution.py:621
  7.3 1.1 %shard_map.144 = (bf16[256,1024]{1,0:T(8,128)(2,1)S(1)}, bf16[256,128]{1,0:T(8,128)(2,1)S(1)}, bf16[1536,256]{1,0:T(8,128)(2,1)S(1)}, bf16[1536,256]{1,0:T(8,128)(2,1)S(1)}, bf16[64,1024]{1,0:T(8,128)(2,1)S(1)}) custom-call(bf16[32,32,256]{2,1,0:T(8,128)(2,1)S(1)} %get-tuple-element.45.stem, s32[16,2,256]{2,1,0:T(2,128)S(1)} %get-tuple-element.46.labels, ...), custom_call_target="tpu_custom_call" | custom-call | flops 536870912 | bytes 1048576 | tf_op jit(solution)/shard_map/pallas_call | solution.py:557
  8.4 0.3 collective-permute-done.after
  8.7 2.9 %shard_map.145 = (bf16[1,3,288,1280]{3,2,1,0:T(8,128)(2,1)S(1)}, bf16[1,3,288,1280]{3,2,1,0:T(8,128)(2,1)S(1)}, bf16[1,288,1024]{2,1,0:T(8,128)(2,1)S(1)}, bf16[...) custom-call(bf16[256,1024]{1,0:T(8,128)(2,1)S(1)} %get-tuple-element.50.stem, ...), custom_call_target="tpu_custom_call" | custom-call | flops 1073741824 | bytes 1048576 | tf_op jit(solution)/shard_map/pallas_call | solution.py:557
  11.7 30.2 %all_to_all.20.message = bf16[16,144,128]{2,1,0:T(8,128)(2,1)S(1)} all-to-all(bf16[16,144,128]{2,1,0:T(8,128)(2,1)S(1)} %get-tuple-element.55), channel_id=1, replica_groups=mesh['slab'=16,'gx'=16] {'slab'}, dimensions={0} | all-to-all | bytes 1179648 | tf_op jit(solution)/shard_map/all_to_all | solution.py:651
  41.9 8.9 %shard_map.146 = (f32[272,32]{1,0:T(8,128)S(1)}, bf16[16,152,128]{2,1,0:T(8,128)(2,1)S(1)}) custom-call(bf16[16,144,128]{2,1,0:T(8,128)(2,1)S(1)} %all_to_all.20.message, bf16[288,128]{1,0:T(8,128)(2,1)S(1)} %get-tuple-element.56.marks, bf16[3,3,32,32]{3,2,1,0:T(8,128)(2,1)S(1)} %bitcast.21, bf16[3,3,32,32]{3,2,1,0:T(8,128)(2,1)S(1)} %bitcast.22, ...), custom_call_target="tpu_custom_call" | custom-call | flops 2147483648 | bytes 1048576 | tf_op jit(solution)/shard_map/pallas_call | solution.py:557
  50.8 21.9 %all_to_all.21.back = bf16[16,152,128]{2,1,0:T(8,128)(2,1)S(1)} all-to-all(bf16[16,152,128]{2,1,0:T(8,128)(2,1)S(1)} %get-tuple-element.58), channel_id=1, replica_groups=mesh['slab'=16,'gx'=16] {'slab'}, dimensions={0} | all-to-all | bytes 1245184 | tf_op jit(solution)/shard_map/all_to_all | solution.py:662
  72.7 3.9 %shard_map.147 = (f32[88,128]{1,0:T(8,128)S(1)}, f32[88,128]{1,0:T(8,128)S(1)}, bf16[1,288,1024]{2,1,0:T(8,128)(2,1)S(1)}) custom-call(bf16[16,152,128]{2,1,0:T(8,128)(2,1)S(1)} %all_to_all.21.back, bf16[1,288,1024]{2,1,0:T(8,128)(2,1)S(1)} %get-tuple-element.59.hidden_two, bf16[1,3,288,1280]{3,2,1,0:T(8,128)(2,1)S(1)} %get-tuple-element.60.one_s, ...), custom_call_target="tpu_custom_call" | custom-call | flops 2147483648 | bytes 1048576 | tf_op jit(solution)/shard_map/pallas_call | solution.py:557
  76.6 2.6 %collective-permute-start.1 = (f32[88,128]{1,0:T(8,128)S(1)}, f32[88,128]{1,0:T(8,128)S(1)}, u32[]{:S(2)}, u32[]{:S(2)}) collective-permute-start(f32[88,128]{1,0:T(8,128)S(1)} %get-tuple-element.63), channel_id=1, source_target_pairs={{0,1},{1,0},{2,3},{3,2},{4,5},{5,4},{6,7},{7,6},{8,9},{9,8},{10,11... | collective-permute-start | bytes 135176 | tf_op jit(solution)/shard_map/ppermute | solution.py:579
  79.2 1.3 %shard_map.148 = (bf16[256,1024]{1,0:T(8,128)(2,1)S(1)}, bf16[16,1152]{1,0:T(8,128)(2,1)S(1)}) custom-call(bf16[1,288,1024]{2,1,0:T(8,128)(2,1)S(1)} %get-tuple-element.64.delta_a, f32[272,32]{1,0:T(8,128)S(1)} %get-tuple-element.65.probability, bf16[3,3,32,32]{3,2,1,0:T(8,128)(2,1)S(1)} %bitcast.26), custom_call_target="tpu_custom_call" | custom-call | flops 1073741824 | bytes 1048576 | tf_op jit(solution)/shard_map/pallas_call | solution.py:557
  80.5 0.8 broadcast_in_dim.26
  81.3 5.4 %all-to-all-start.2 = ((bf16[16,88,128]{2,1,0:T(8,128)(2,1)}), bf16[16,88,128]{2,1,0:T(8,128)(2,1)S(1)}, u32[]{:S(2)}, u32[]{:S(2)}) async-start(bf16[16,88,128]{2,1,0:T(8,128)(2,1)} %broadcast_in_dim.26), calls=%async_computation.2 | async-start | bytes 720896 | tf_op jit(solution)/shard_map/all_to_all | solution.py:587
  86.7 3.7 %collective-permute-start.2 = (bf16[16,1152]{1,0:T(8,128)(2,1)S(1)}, bf16[16,1152]{1,0:T(8,128)(2,1)S(1)}, u32[]{:S(2)}, u32[]{:S(2)}) collective-permute-start(bf16[16,1152]{1,0:T(8,128)(2,1)S(1)} %get-tuple-element.70), channel_id=1, source_target_pairs={{0,1},{1,2},{2,3},{3,4},{4,5},{5,6},{6,7},{7,8},{8,9},{9,10},{10,1... | collective-permute-start | bytes 110600 | tf_op jit(solution)/shard_map/ppermute | solution.py:681
  90.5 0.1 pad.2.clone
  90.5 2.5 %collective-permute-done.2.moved = bf16[16,1152]{1,0:T(8,128)(2,1)S(1)} collective-permute-done((bf16[16,1152]{1,0:T(8,128)(2,1)S(1)}, bf16[16,1152]{1,0:T(8,128)(2,1)S(1)}, u32[]{:S(2)}, u32[]{:S(2)}) %collective-permute-start.2) | collective-permute-done | bytes 36896 | tf_op jit(solution)/shard_map/ppermute | solution.py:681
  93.0 1.7 %shard_map.149 = (bf16[32,32,256]{2,1,0:T(8,128)(2,1)}, f32[16,2,256]{2,1,0:T(2,128)}) custom-call(bf16[256,1024]{1,0:T(8,128)(2,1)S(1)} %get-tuple-element.69.found, f32[272,32]{1,0:T(8,128)S(1)} %get-tuple-element.65.probability, bf16[16,1152]{1,0:T(8,128)(2,1)S(1)} %collective-permute-done.2.moved), custom_call_target="tpu_custom_call" | custom-call | flops 268435456 | bytes 1048576 | tf_op jit(solution)/shard_map/pallas_call | solution.py:557
  94.7 0.9 all-to-all-done.2
  95.6 0.1 maximum_maximum_fusion
  95.8 11.1 %all_to_all.22 = bf16[8,96,128]{2,1,0:T(8,128)(2,1)S(1)} all-to-all(bf16[8,96,128]{2,1,0:T(8,128)(2,1)S(1)} %broadcast_in_dim.29), channel_id=1, replica_groups={{0,16,32,48,64,80,96,112},{128,144,160,176,192,208,224,240},{1,17,33,49..., dimensions={0} | all-to-all | bytes 393216 | tf_op jit(solution)/shard_map/all_to_all | solution.py:594
  106.8 3.0 %collective-permute-start.3 = (f32[72,128]{1,0:T(8,128)S(1)}, f32[72,128]{1,0:T(8,128)S(1)}, u32[]{:S(2)}, u32[]{:S(2)}) collective-permute-start(f32[72,128]{1,0:T(8,128)S(1)} %convert_reduce_fusion.1.mine), channel_id=1, source_target_pairs={{0,1},{1,0},{2,3},{3,2},{4,5},{5,4},{6,7},{7,6},{8,9},{9,8},{10,11... | collective-permute-start | bytes 110600 | tf_op jit(solution)/shard_map/ppermute | solution.py:596
  109.8 0.8 shard_map.151
  110.7 0.0 collective-permute-done.3.theirs
  110.7 0.8 shard_map.150
  (18 shorter events, 0.2 us)
Async XLA Ops:
  2.1 6.6 %collective-permute-start = (bf16[32,1152]{1,0:T(8,128)(2,1)S(1)}, bf16[32,1152]{1,0:T(8,128)(2,1)S(1)}, u32[]{:S(2)}, u32[]{:S(2)}) collective-permute-start(bf16[32,1152]{1,0:T(8,128)(2,1)S(1)} %get-tuple-element.52), channel_id=1, source_target_pairs={{1,0},{2,1},{3,2},{4,3},{5,4},{6,5},{7,6},{8,7},{9,8},{10,9},{11,1... | collective-permute-start | bytes 221192 | tf_op jit(solution)/shard_map/ppermute | solution.py:621
  8.7 33.2 %copy-start = (bf16[32,3,3,32]{3,0,2,1:T(8,128)(2,1)S(1)}, bf16[32,3,3,32]{3,0,2,1:T(8,128)(2,1)}, u32[]{:S(2)}) copy-start(bf16[32,3,3,32]{3,0,2,1:T(8,128)(2,1)} %param.12) | copy-start | bytes 55300
  8.7 33.2 %copy-start.1 = (bf16[32,3,3,32]{3,0,2,1:T(8,128)(2,1)S(1)}, bf16[32,3,3,32]{3,0,2,1:T(8,128)(2,1)}, u32[]{:S(2)}) copy-start(bf16[32,3,3,32]{3,0,2,1:T(8,128)(2,1)} %param.13) | copy-start | bytes 55300
  41.9 30.8 %copy-start.2 = (bf16[32,3,3,32]{3,0,2,1:T(8,128)(2,1)S(1)}, bf16[32,3,3,32]{3,0,2,1:T(8,128)(2,1)}, u32[]{:S(2)}) copy-start(bf16[32,3,3,32]{3,0,2,1:T(8,128)(2,1)} %param.11) | copy-start | bytes 55300
  72.7 6.5 %copy-start.3 = (bf16[32,3,3,32]{3,0,2,1:T(8,128)(2,1)S(1)}, bf16[32,3,3,32]{3,0,2,1:T(8,128)(2,1)}, u32[]{:S(2)}) copy-start(bf16[32,3,3,32]{3,0,2,1:T(8,128)(2,1)} %param.10) | copy-start | bytes 55300
  76.6 3.9 %collective-permute-start.1 = (f32[88,128]{1,0:T(8,128)S(1)}, f32[88,128]{1,0:T(8,128)S(1)}, u32[]{:S(2)}, u32[]{:S(2)}) collective-permute-start(f32[88,128]{1,0:T(8,128)S(1)} %get-tuple-element.63), channel_id=1, source_target_pairs={{0,1},{1,0},{2,3},{3,2},{4,5},{5,4},{6,7},{7,6},{8,9},{9,8},{10,11... | collective-permute-start | bytes 135176 | tf_op jit(solution)/shard_map/ppermute | solution.py:579
  81.3 14.3 %all-to-all-start.2 = ((bf16[16,88,128]{2,1,0:T(8,128)(2,1)}), bf16[16,88,128]{2,1,0:T(8,128)(2,1)S(1)}, u32[]{:S(2)}, u32[]{:S(2)}) async-start(bf16[16,88,128]{2,1,0:T(8,128)(2,1)} %broadcast_in_dim.26), calls=%async_computation.2 | async-start | bytes 720896 | tf_op jit(solution)/shard_map/all_to_all | solution.py:587
  86.7 6.3 %collective-permute-start.2 = (bf16[16,1152]{1,0:T(8,128)(2,1)S(1)}, bf16[16,1152]{1,0:T(8,128)(2,1)S(1)}, u32[]{:S(2)}, u32[]{:S(2)}) collective-permute-start(bf16[16,1152]{1,0:T(8,128)(2,1)S(1)} %get-tuple-element.70), channel_id=1, source_target_pairs={{0,1},{1,2},{2,3},{3,4},{4,5},{5,6},{6,7},{7,8},{8,9},{9,10},{10,1... | collective-permute-start | bytes 110600 | tf_op jit(solution)/shard_map/ppermute | solution.py:681
  106.8 3.9 %collective-permute-start.3 = (f32[72,128]{1,0:T(8,128)S(1)}, f32[72,128]{1,0:T(8,128)S(1)}, u32[]{:S(2)}, u32[]{:S(2)}) collective-permute-start(f32[72,128]{1,0:T(8,128)S(1)} %convert_reduce_fusion.1.mine), channel_id=1, source_target_pairs={{0,1},{1,0},{2,3},{3,2},{4,5},{5,4},{6,7},{7,6},{8,9},{9,8},{10,11... | collective-permute-start | bytes 110600 | tf_op jit(solution)/shard_map/ppermute | solution.py:596

commit v8 on v7

--- a/solution.py
+++ b/solution.py
@@ -545,6 +545,13 @@
         grad_b[tap // 3, tap % 3] = piece(9 + tap)
 
 
+def finish_kernel(
+    factor, mine, theirs, chunks, grad_a, grad_b, grad_c, grad_d, head_one, head_two, flat, other
+):
+    finish_cd_kernel(factor, chunks, grad_c, grad_d, head_one, head_two, other)
+    finish_ab_kernel(factor, mine, theirs, grad_a, grad_b, flat)
+
+
 def call(kernel, outs, ins, scratch=(), flops=0, megabytes=16):
     places = [place for _, place in outs]
     shapes = [pltpu.HBM(out.shape, out.dtype) if place is HBM else out for out, place in outs]
@@ -692,14 +699,11 @@
     taps = shape((3, 3, C, C), F32)
     head = shape((1, C), F32)
     factor = 1.0 / (depth * height * cols)
-    grad_c, grad_d, grad_one, grad_two = call(
-        functools.partial(finish_cd_kernel, factor), [(taps, VMEM)] * 2 + [(head, VMEM)] * 2,
-        [VMEM], [pltpu.VMEM((160, 128), F32)], flops=1 << 24, megabytes=2,
-    )(chunks)
-    grad_a, grad_b = call(
-        functools.partial(finish_ab_kernel, factor), [(taps, VMEM)] * 2,
-        [VMEM] * 2, [pltpu.VMEM((144, 128), F32)], flops=1 << 20, megabytes=2,
-    )(mine, theirs)
+    grad_a, grad_b, grad_c, grad_d, grad_one, grad_two = call(
+        functools.partial(finish_kernel, factor), [(taps, VMEM)] * 4 + [(head, VMEM)] * 2,
+        [VMEM] * 3, [pltpu.VMEM((144, 128), F32), pltpu.VMEM((160, 128), F32)],
+        flops=1 << 20, megabytes=3,
+    )(mine, theirs, chunks)
     kernels = [jnp.transpose(grad, (2, 0, 1, 3)) for grad in (grad_a, grad_b, grad_c, grad_d)]
     return (probability, stem_grad[:, None], *kernels, grad_one[0], grad_two[0])
 

time: 112 us -> 112 us (level)
    pallas_call x9 -> x8, Pallas kernels: 23 us -> 22.3 us  [run(): return bound(*operands)]
  transfers between devices with their start and end apart: 5 -> 5, of which waited for: 3 -> 4; matrix products, arithmetic and copies ran while one was open for 0% -> 0% of each run, Pallas kernels for 4% -> 4%
where the time goes in v8:
time: 112 us
  blocking collectives  63.1 us (56%)
  Pallas kernels  22.3 us (20%)
  starting transfers between devices  19.9 us (18%)
  waiting for transfers between devices  4.53 us (4%)
    all_to_all x1, blocking collectives, per_device(): message = lax.all_to_all(message, 'slab', 0, 0, tiled=True)  30.2 us
    pallas_call x8, Pallas kernels, run(): return bound(*operands)  22.3 us
    all_to_all x1, blocking collectives, per_device(): back = lax.all_to_all(back, 'slab', 0, 0, tiled=True)  21.9 us
    all_to_all x1, blocking collectives, sum_everywhere(): lax.all_to_all(spread, slab, 0, 0, tiled=True, axis_index_groups=along)  11 us
    all_to_all x1, starting transfers between devices, sum_everywhere(): lax.all_to_all(spread, (slab, gx), 0, 0, tiled=True, axis_index_groups=ac...  5.41 us
    ppermute x1, starting transfers between devices, per_device(): after = lax.ppermute(initial, 'gx', down)  5.15 us
    ppermute x1, starting transfers between devices, place(): moved = lax.ppermute(leaving, 'gx', up)  3.73 us
    ppermute x1, starting transfers between devices, sum_everywhere(): return ((mine, lax.ppermute(mine, gx, swap), found[:, 72:]), beside)  2.99 us
  transfers between devices with their start and end apart: 5, of which 4 were waited for; matrix products, arithmetic and copies ran while one was open for 0% of the time, Pallas kernels for 4%

profile of v8, /device:TPU:1, one launch (start us, length us, event | category | flops | bytes accessed | tf_op | source)
XLA Modules:
  0.0 111.7 jit_solution(4237893326521952865)
XLA Ops:
  0.6 1.5 %shard_map.143 = (bf16[32,1152]{1,0:T(8,128)(2,1)S(1)}, bf16[32,32,256]{2,1,0:T(8,128)(2,1)S(1)}, s32[16,2,256]{2,1,0:T(2,128)S(1)}, bf16[3,3,32,32]{3,2,1,0:T(8...) custom-call(bf16[32,32,256]{2,1,0:T(8,128)(2,1)} %bitcast.27, s32[16,2,256]{2,1,0:T(2,128)} %labels_in.1, ...), custom_call_target="tpu_custom_call" | custom-call | flops 268435456 | bytes 1048576 | tf_op jit(solution)/shard_map/pallas_call | solution.py:564
  2.1 5.1 %collective-permute-start = (bf16[32,1152]{1,0:T(8,128)(2,1)S(1)}, bf16[32,1152]{1,0:T(8,128)(2,1)S(1)}, u32[]{:S(2)}, u32[]{:S(2)}) collective-permute-start(bf16[32,1152]{1,0:T(8,128)(2,1)S(1)} %get-tuple-element.52), channel_id=1, source_target_pairs={{1,0},{2,1},{3,2},{4,3},{5,4},{6,5},{7,6},{8,7},{9,8},{10,9},{11,1... | collective-permute-start | bytes 221192 | tf_op jit(solution)/shard_map/ppermute | solution.py:628
  7.3 1.1 %shard_map.144 = (bf16[256,1024]{1,0:T(8,128)(2,1)S(1)}, bf16[256,128]{1,0:T(8,128)(2,1)S(1)}, bf16[1536,256]{1,0:T(8,128)(2,1)S(1)}, bf16[1536,256]{1,0:T(8,128)(2,1)S(1)}, bf16[64,1024]{1,0:T(8,128)(2,1)S(1)}) custom-call(bf16[32,32,256]{2,1,0:T(8,128)(2,1)S(1)} %get-tuple-element.45.stem, s32[16,2,256]{2,1,0:T(2,128)S(1)} %get-tuple-element.46.labels, ...), custom_call_target="tpu_custom_call" | custom-call | flops 536870912 | bytes 1048576 | tf_op jit(solution)/shard_map/pallas_call | solution.py:564
  8.4 0.3 collective-permute-done.after
  8.7 2.9 %shard_map.145 = (bf16[1,3,288,1280]{3,2,1,0:T(8,128)(2,1)S(1)}, bf16[1,3,288,1280]{3,2,1,0:T(8,128)(2,1)S(1)}, bf16[1,288,1024]{2,1,0:T(8,128)(2,1)S(1)}, bf16[...) custom-call(bf16[256,1024]{1,0:T(8,128)(2,1)S(1)} %get-tuple-element.50.stem, ...), custom_call_target="tpu_custom_call" | custom-call | flops 1073741824 | bytes 1048576 | tf_op jit(solution)/shard_map/pallas_call | solution.py:564
  11.7 30.2 %all_to_all.20.message = bf16[16,144,128]{2,1,0:T(8,128)(2,1)S(1)} all-to-all(bf16[16,144,128]{2,1,0:T(8,128)(2,1)S(1)} %get-tuple-element.55), channel_id=1, replica_groups=mesh['slab'=16,'gx'=16] {'slab'}, dimensions={0} | all-to-all | bytes 1179648 | tf_op jit(solution)/shard_map/all_to_all | solution.py:658
  41.9 8.9 %shard_map.146 = (f32[272,32]{1,0:T(8,128)S(1)}, bf16[16,152,128]{2,1,0:T(8,128)(2,1)S(1)}) custom-call(bf16[16,144,128]{2,1,0:T(8,128)(2,1)S(1)} %all_to_all.20.message, bf16[288,128]{1,0:T(8,128)(2,1)S(1)} %get-tuple-element.56.marks, bf16[3,3,32,32]{3,2,1,0:T(8,128)(2,1)S(1)} %bitcast.21, bf16[3,3,32,32]{3,2,1,0:T(8,128)(2,1)S(1)} %bitcast.22, ...), custom_call_target="tpu_custom_call" | custom-call | flops 2147483648 | bytes 1048576 | tf_op jit(solution)/shard_map/pallas_call | solution.py:564
  50.8 21.9 %all_to_all.21.back = bf16[16,152,128]{2,1,0:T(8,128)(2,1)S(1)} all-to-all(bf16[16,152,128]{2,1,0:T(8,128)(2,1)S(1)} %get-tuple-element.58), channel_id=1, replica_groups=mesh['slab'=16,'gx'=16] {'slab'}, dimensions={0} | all-to-all | bytes 1245184 | tf_op jit(solution)/shard_map/all_to_all | solution.py:669
  72.7 3.9 %shard_map.147 = (f32[88,128]{1,0:T(8,128)S(1)}, f32[88,128]{1,0:T(8,128)S(1)}, bf16[1,288,1024]{2,1,0:T(8,128)(2,1)S(1)}) custom-call(bf16[16,152,128]{2,1,0:T(8,128)(2,1)S(1)} %all_to_all.21.back, bf16[1,288,1024]{2,1,0:T(8,128)(2,1)S(1)} %get-tuple-element.59.hidden_two, bf16[1,3,288,1280]{3,2,1,0:T(8,128)(2,1)S(1)} %get-tuple-element.60.one_s, ...), custom_call_target="tpu_custom_call" | custom-call | flops 2147483648 | bytes 1048576 | tf_op jit(solution)/shard_map/pallas_call | solution.py:564
  76.6 2.6 %collective-permute-start.1 = (f32[88,128]{1,0:T(8,128)S(1)}, f32[88,128]{1,0:T(8,128)S(1)}, u32[]{:S(2)}, u32[]{:S(2)}) collective-permute-start(f32[88,128]{1,0:T(8,128)S(1)} %get-tuple-element.63), channel_id=1, source_target_pairs={{0,1},{1,0},{2,3},{3,2},{4,5},{5,4},{6,7},{7,6},{8,9},{9,8},{10,11... | collective-permute-start | bytes 135176 | tf_op jit(solution)/shard_map/ppermute | solution.py:586
  79.2 1.3 %shard_map.148 = (bf16[256,1024]{1,0:T(8,128)(2,1)S(1)}, bf16[16,1152]{1,0:T(8,128)(2,1)S(1)}) custom-call(bf16[1,288,1024]{2,1,0:T(8,128)(2,1)S(1)} %get-tuple-element.64.delta_a, f32[272,32]{1,0:T(8,128)S(1)} %get-tuple-element.65.probability, bf16[3,3,32,32]{3,2,1,0:T(8,128)(2,1)S(1)} %bitcast.26), custom_call_target="tpu_custom_call" | custom-call | flops 1073741824 | bytes 1048576 | tf_op jit(solution)/shard_map/pallas_call | solution.py:564
  80.5 0.0 collective-permute-done.1
  80.5 0.8 broadcast_in_dim.26
  81.3 5.4 %all-to-all-start.2 = ((bf16[16,88,128]{2,1,0:T(8,128)(2,1)}), bf16[16,88,128]{2,1,0:T(8,128)(2,1)S(1)}, u32[]{:S(2)}, u32[]{:S(2)}) async-start(bf16[16,88,128]{2,1,0:T(8,128)(2,1)} %broadcast_in_dim.26), calls=%async_computation.2 | async-start | bytes 720896 | tf_op jit(solution)/shard_map/all_to_all | solution.py:594
  86.7 3.7 %collective-permute-start.2 = (bf16[16,1152]{1,0:T(8,128)(2,1)S(1)}, bf16[16,1152]{1,0:T(8,128)(2,1)S(1)}, u32[]{:S(2)}, u32[]{:S(2)}) collective-permute-start(bf16[16,1152]{1,0:T(8,128)(2,1)S(1)} %get-tuple-element.70), channel_id=1, source_target_pairs={{0,1},{1,2},{2,3},{3,4},{4,5},{5,6},{6,7},{7,8},{8,9},{9,10},{10,1... | collective-permute-start | bytes 110600 | tf_op jit(solution)/shard_map/ppermute | solution.py:688
  90.5 0.1 pad.2.clone
  90.5 2.5 %collective-permute-done.2.moved = bf16[16,1152]{1,0:T(8,128)(2,1)S(1)} collective-permute-done((bf16[16,1152]{1,0:T(8,128)(2,1)S(1)}, bf16[16,1152]{1,0:T(8,128)(2,1)S(1)}, u32[]{:S(2)}, u32[]{:S(2)}) %collective-permute-start.2) | collective-permute-done | bytes 36896 | tf_op jit(solution)/shard_map/ppermute | solution.py:688
  93.0 1.7 %shard_map.149 = (bf16[32,32,256]{2,1,0:T(8,128)(2,1)}, f32[16,2,256]{2,1,0:T(2,128)}) custom-call(bf16[256,1024]{1,0:T(8,128)(2,1)S(1)} %get-tuple-element.69.found, f32[272,32]{1,0:T(8,128)S(1)} %get-tuple-element.65.probability, bf16[16,1152]{1,0:T(8,128)(2,1)S(1)} %collective-permute-done.2.moved), custom_call_target="tpu_custom_call" | custom-call | flops 268435456 | bytes 1048576 | tf_op jit(solution)/shard_map/pallas_call | solution.py:564
  94.7 0.9 all-to-all-done.2
  95.7 0.1 maximum_maximum_fusion
  95.8 11.0 %all_to_all.22 = bf16[8,96,128]{2,1,0:T(8,128)(2,1)S(1)} all-to-all(bf16[8,96,128]{2,1,0:T(8,128)(2,1)S(1)} %broadcast_in_dim.29), channel_id=1, replica_groups={{0,16,32,48,64,80,96,112},{128,144,160,176,192,208,224,240},{1,17,33,49..., dimensions={0} | all-to-all | bytes 393216 | tf_op jit(solution)/shard_map/all_to_all | solution.py:601
  106.8 3.0 %collective-permute-start.3 = (f32[72,128]{1,0:T(8,128)S(1)}, f32[72,128]{1,0:T(8,128)S(1)}, u32[]{:S(2)}, u32[]{:S(2)}) collective-permute-start(f32[72,128]{1,0:T(8,128)S(1)} %convert_reduce_fusion.1.mine), channel_id=1, source_target_pairs={{0,1},{1,0},{2,3},{3,2},{4,5},{5,4},{6,7},{7,6},{8,9},{9,8},{10,11... | collective-permute-start | bytes 110600 | tf_op jit(solution)/shard_map/ppermute | solution.py:603
  109.8 0.9 collective-permute-done.3.theirs
  110.7 1.0 shard_map.150
  (17 shorter events, 0.2 us)
Async XLA Ops:
  2.1 6.6 %collective-permute-start = (bf16[32,1152]{1,0:T(8,128)(2,1)S(1)}, bf16[32,1152]{1,0:T(8,128)(2,1)S(1)}, u32[]{:S(2)}, u32[]{:S(2)}) collective-permute-start(bf16[32,1152]{1,0:T(8,128)(2,1)S(1)} %get-tuple-element.52), channel_id=1, source_target_pairs={{1,0},{2,1},{3,2},{4,3},{5,4},{6,5},{7,6},{8,7},{9,8},{10,9},{11,1... | collective-permute-start | bytes 221192 | tf_op jit(solution)/shard_map/ppermute | solution.py:628
  8.7 33.2 %copy-start = (bf16[32,3,3,32]{3,0,2,1:T(8,128)(2,1)S(1)}, bf16[32,3,3,32]{3,0,2,1:T(8,128)(2,1)}, u32[]{:S(2)}) copy-start(bf16[32,3,3,32]{3,0,2,1:T(8,128)(2,1)} %param.12) | copy-start | bytes 55300
  8.7 33.2 %copy-start.1 = (bf16[32,3,3,32]{3,0,2,1:T(8,128)(2,1)S(1)}, bf16[32,3,3,32]{3,0,2,1:T(8,128)(2,1)}, u32[]{:S(2)}) copy-start(bf16[32,3,3,32]{3,0,2,1:T(8,128)(2,1)} %param.13) | copy-start | bytes 55300
  41.9 30.8 %copy-start.2 = (bf16[32,3,3,32]{3,0,2,1:T(8,128)(2,1)S(1)}, bf16[32,3,3,32]{3,0,2,1:T(8,128)(2,1)}, u32[]{:S(2)}) copy-start(bf16[32,3,3,32]{3,0,2,1:T(8,128)(2,1)} %param.11) | copy-start | bytes 55300
  72.7 6.5 %copy-start.3 = (bf16[32,3,3,32]{3,0,2,1:T(8,128)(2,1)S(1)}, bf16[32,3,3,32]{3,0,2,1:T(8,128)(2,1)}, u32[]{:S(2)}) copy-start(bf16[32,3,3,32]{3,0,2,1:T(8,128)(2,1)} %param.10) | copy-start | bytes 55300
  76.6 3.9 %collective-permute-start.1 = (f32[88,128]{1,0:T(8,128)S(1)}, f32[88,128]{1,0:T(8,128)S(1)}, u32[]{:S(2)}, u32[]{:S(2)}) collective-permute-start(f32[88,128]{1,0:T(8,128)S(1)} %get-tuple-element.63), channel_id=1, source_target_pairs={{0,1},{1,0},{2,3},{3,2},{4,5},{5,4},{6,7},{7,6},{8,9},{9,8},{10,11... | collective-permute-start | bytes 135176 | tf_op jit(solution)/shard_map/ppermute | solution.py:586
  81.3 14.3 %all-to-all-start.2 = ((bf16[16,88,128]{2,1,0:T(8,128)(2,1)}), bf16[16,88,128]{2,1,0:T(8,128)(2,1)S(1)}, u32[]{:S(2)}, u32[]{:S(2)}) async-start(bf16[16,88,128]{2,1,0:T(8,128)(2,1)} %broadcast_in_dim.26), calls=%async_computation.2 | async-start | bytes 720896 | tf_op jit(solution)/shard_map/all_to_all | solution.py:594
  86.7 6.3 %collective-permute-start.2 = (bf16[16,1152]{1,0:T(8,128)(2,1)S(1)}, bf16[16,1152]{1,0:T(8,128)(2,1)S(1)}, u32[]{:S(2)}, u32[]{:S(2)}) collective-permute-start(bf16[16,1152]{1,0:T(8,128)(2,1)S(1)} %get-tuple-element.70), channel_id=1, source_target_pairs={{0,1},{1,2},{2,3},{3,4},{4,5},{5,6},{6,7},{7,8},{8,9},{9,10},{10,1... | collective-permute-start | bytes 110600 | tf_op jit(solution)/shard_map/ppermute | solution.py:688
  106.8 3.9 %collective-permute-start.3 = (f32[72,128]{1,0:T(8,128)S(1)}, f32[72,128]{1,0:T(8,128)S(1)}, u32[]{:S(2)}, u32[]{:S(2)}) collective-permute-start(f32[72,128]{1,0:T(8,128)S(1)} %convert_reduce_fusion.1.mine), channel_id=1, source_target_pairs={{0,1},{1,0},{2,3},{3,2},{4,5},{5,4},{6,7},{7,6},{8,9},{9,8},{10,11... | collective-permute-start | bytes 110600 | tf_op jit(solution)/shard_map/ppermute | solution.py:603
